TPU v7x, 32 devices: a whole 2x2x4 slice. The times are simulated.
32 devices in a mesh: wide: 8 (over z, x), narrow: 4 (over y, core).
Axes of the slice: x: 2, y: 2, z: 4, core: 2. Of those that a mesh axis runs over, the one named last changes fastest.
Arguments:
- tokens: bfloat16 [8, 512, 1152], P('wide', 'narrow'), may hold values from -3 to 3
- cond: bfloat16 [8, 4, 1152], P('wide'), may hold values from -3 to 3
- seg_ids: int32 [8, 512], P('wide'), may hold values from 0 to 3, as said below
- cond_index: int32 [8, 4], P('wide'), may hold values from 0 to 3
- cotangent: bfloat16 [8, 512, 1152], P('wide', 'narrow'), may hold values from -3 to 3
- ada_weight: bfloat16 [2, 1152, 6912], P(None, 'wide'), may hold values from -0.1875 to 0.1875
- ada_bias: bfloat16 [2, 6912], P(None, 'wide'), may hold values from -0.5 to 0.5
- qkv_weight: bfloat16 [2, 1152, 3456], P(None, 'wide'), may hold values from -0.1875 to 0.1875
- qkv_bias: bfloat16 [2, 3456], P(None, 'wide'), may hold values from -0.5 to 0.5
- out_weight: bfloat16 [2, 1152, 1152], P(None, 'wide'), may hold values from -0.375 to 0.375
- out_bias: bfloat16 [2, 1152], P(None, 'wide'), may hold values from -0.5 to 0.5
- up_weight: bfloat16 [2, 1152, 4608], P(None, 'wide'), may hold values from -0.1875 to 0.1875
- up_bias: bfloat16 [2, 4608], P(None, 'wide'), may hold values from -0.5 to 0.5
- down_weight: bfloat16 [2, 4608, 1152], P(None, 'wide'), may hold values from -0.09375 to 0.09375
- down_bias: bfloat16 [2, 1152], P(None, 'wide'), may hold values from -0.5 to 0.5
Outputs:
- mixed: bfloat16 [8, 512, 1152], P('wide', 'narrow')
- token_grad: float32 [8, 512, 1152], P('wide', 'narrow')
- cond_grad: float32 [8, 4, 1152], P('wide')
- ada_weight_grad: float32 [2, 1152, 6912], P(None, 'wide')
- ada_bias_grad: float32 [2, 6912], P(None, 'wide')
- qkv_weight_grad: float32 [2, 1152, 3456], P(None, 'wide')
- qkv_bias_grad: float32 [2, 3456], P(None, 'wide')
- out_weight_grad: float32 [2, 1152, 1152], P(None, 'wide')
- out_bias_grad: float32 [2, 1152], P(None, 'wide')
- up_weight_grad: float32 [2, 1152, 4608], P(None, 'wide')
- up_bias_grad: float32 [2, 4608], P(None, 'wide')
- down_weight_grad: float32 [2, 4608, 1152], P(None, 'wide')
- down_bias_grad: float32 [2, 1152], P(None, 'wide')
Inputs may be any that keep to these rules, and one draw needn't show every extreme that they name: `seg_ids`: within a row the ids never fall and each of 0 to 3 occurs; segment 1 of every row begins among the row's first 128 tokens and ends among its last 128.
All inputs are finite; a program needn't handle non-finite values.
Results may differ from a plain program's by a relative error of at most 0.02.
Values may be sent and summed in bfloat16 or wider, within the bound.
A program may use at most 384 MiB of HBM per device.

v0:
```python
from functools import partial
import math

import jax
import jax.numpy as jnp
from jax import lax
from jax.sharding import PartitionSpec as P

HEADS = 16
HEAD = 72
LAYERS = 2
SEGS = 4


EXACT = lax.Precision.HIGHEST


def layer_norm(values):
    row_mean = jnp.mean(values, -1, keepdims=True)
    centred = values - row_mean
    return centred * lax.rsqrt(jnp.mean(centred * centred, -1, keepdims=True) + 1e-06)


def modulate(values, scale, shift):
    return layer_norm(values) * (1.0 + scale) + shift


def silu_value(values):
    return values * jax.nn.sigmoid(values)


def fetch(stacks, layer_idx):
    return (
        lax.all_gather(stacks[0][layer_idx], "wide", axis=0, tiled=True),
        lax.all_gather(stacks[1][layer_idx], "wide", axis=0, tiled=True),
        lax.all_gather(stacks[2][layer_idx], "wide", axis=0, tiled=True),
        lax.all_gather(stacks[3][layer_idx], "wide", axis=0, tiled=True),
        lax.all_gather(stacks[4][layer_idx], "wide", axis=0, tiled=True),
        lax.all_gather(stacks[5][layer_idx], "wide", axis=0, tiled=True),
        lax.all_gather(stacks[6][layer_idx], "wide", axis=0, tiled=True),
        lax.all_gather(stacks[7][layer_idx], "wide", axis=0, tiled=True),
        lax.all_gather(stacks[8][layer_idx], "wide", axis=0, tiled=True),
        lax.all_gather(stacks[9][layer_idx], "wide", axis=0, tiled=True),
    )


def fetch_again(stacks, layer_idx):
    return (
        lax.all_gather(stacks[0][layer_idx], "wide", axis=0, tiled=True),
        lax.all_gather(stacks[1][layer_idx], "wide", axis=0, tiled=True),
        lax.all_gather(stacks[2][layer_idx], "wide", axis=0, tiled=True),
        lax.all_gather(stacks[3][layer_idx], "wide", axis=0, tiled=True),
        lax.all_gather(stacks[4][layer_idx], "wide", axis=0, tiled=True),
        lax.all_gather(stacks[5][layer_idx], "wide", axis=0, tiled=True),
        lax.all_gather(stacks[6][layer_idx], "wide", axis=0, tiled=True),
        lax.all_gather(stacks[7][layer_idx], "wide", axis=0, tiled=True),
        lax.all_gather(stacks[8][layer_idx], "wide", axis=0, tiled=True),
        lax.all_gather(stacks[9][layer_idx], "wide", axis=0, tiled=True),
    )


def reduce_grads(grads):
    shares = (
        lax.psum_scatter(
            grads[0].astype(jnp.bfloat16), "wide", scatter_dimension=0, tiled=True
        ).astype(jnp.float32),
        lax.psum_scatter(
            grads[1].astype(jnp.bfloat16), "wide", scatter_dimension=0, tiled=True
        ).astype(jnp.float32),
        lax.psum_scatter(
            grads[2].astype(jnp.bfloat16), "wide", scatter_dimension=0, tiled=True
        ).astype(jnp.float32),
        lax.psum_scatter(
            grads[3].astype(jnp.bfloat16), "wide", scatter_dimension=0, tiled=True
        ).astype(jnp.float32),
        lax.psum_scatter(
            grads[4].astype(jnp.bfloat16), "wide", scatter_dimension=0, tiled=True
        ).astype(jnp.float32),
        lax.psum_scatter(
            grads[5].astype(jnp.bfloat16), "wide", scatter_dimension=0, tiled=True
        ).astype(jnp.float32),
        lax.psum_scatter(
            grads[6].astype(jnp.bfloat16), "wide", scatter_dimension=0, tiled=True
        ).astype(jnp.float32),
        lax.psum_scatter(
            grads[7].astype(jnp.bfloat16), "wide", scatter_dimension=0, tiled=True
        ).astype(jnp.float32),
        lax.psum_scatter(
            grads[8].astype(jnp.bfloat16), "wide", scatter_dimension=0, tiled=True
        ).astype(jnp.float32),
        lax.psum_scatter(
            grads[9].astype(jnp.bfloat16), "wide", scatter_dimension=0, tiled=True
        ).astype(jnp.float32),
    )
    quarters = (
        lax.psum_scatter(
            shares[0].astype(jnp.bfloat16), "narrow", scatter_dimension=0, tiled=True
        ).astype(jnp.float32),
        lax.psum_scatter(
            shares[1].astype(jnp.bfloat16), "narrow", scatter_dimension=0, tiled=True
        ).astype(jnp.float32),
        lax.psum_scatter(
            shares[2].astype(jnp.bfloat16), "narrow", scatter_dimension=0, tiled=True
        ).astype(jnp.float32),
        lax.psum_scatter(
            shares[3].astype(jnp.bfloat16), "narrow", scatter_dimension=0, tiled=True
        ).astype(jnp.float32),
        lax.psum_scatter(
            shares[4].astype(jnp.bfloat16), "narrow", scatter_dimension=0, tiled=True
        ).astype(jnp.float32),
        lax.psum_scatter(
            shares[5].astype(jnp.bfloat16), "narrow", scatter_dimension=0, tiled=True
        ).astype(jnp.float32),
        lax.psum_scatter(
            shares[6].astype(jnp.bfloat16), "narrow", scatter_dimension=0, tiled=True
        ).astype(jnp.float32),
        lax.psum_scatter(
            shares[7].astype(jnp.bfloat16), "narrow", scatter_dimension=0, tiled=True
        ).astype(jnp.float32),
        lax.psum_scatter(
            shares[8].astype(jnp.bfloat16), "narrow", scatter_dimension=0, tiled=True
        ).astype(jnp.float32),
        lax.psum_scatter(
            shares[9].astype(jnp.bfloat16), "narrow", scatter_dimension=0, tiled=True
        ).astype(jnp.float32),
    )
    return (
        lax.all_gather(quarters[0].astype(jnp.bfloat16), "narrow", axis=0, tiled=True).astype(
            jnp.float32
        ),
        lax.all_gather(quarters[1].astype(jnp.bfloat16), "narrow", axis=0, tiled=True).astype(
            jnp.float32
        ),
        lax.all_gather(quarters[2].astype(jnp.bfloat16), "narrow", axis=0, tiled=True).astype(
            jnp.float32
        ),
        lax.all_gather(quarters[3].astype(jnp.bfloat16), "narrow", axis=0, tiled=True).astype(
            jnp.float32
        ),
        lax.all_gather(quarters[4].astype(jnp.bfloat16), "narrow", axis=0, tiled=True).astype(
            jnp.float32
        ),
        lax.all_gather(quarters[5].astype(jnp.bfloat16), "narrow", axis=0, tiled=True).astype(
            jnp.float32
        ),
        lax.all_gather(quarters[6].astype(jnp.bfloat16), "narrow", axis=0, tiled=True).astype(
            jnp.float32
        ),
        lax.all_gather(quarters[7].astype(jnp.bfloat16), "narrow", axis=0, tiled=True).astype(
            jnp.float32
        ),
        lax.all_gather(quarters[8].astype(jnp.bfloat16), "narrow", axis=0, tiled=True).astype(
            jnp.float32
        ),
        lax.all_gather(quarters[9].astype(jnp.bfloat16), "narrow", axis=0, tiled=True).astype(
            jnp.float32
        ),
    )


def layer_forward(state, lead_rows, token_hot, seg_query, seg_ids, weights):
    (
        ada_weight,
        ada_bias,
        qkv_weight,
        qkv_bias,
        out_weight,
        out_bias,
        up_weight,
        up_bias,
        down_weight,
        down_bias,
    ) = weights
    row_count, local_len, model_width = state.shape
    modulation = jnp.dot(lead_rows, ada_weight, preferred_element_type=jnp.float32) + ada_bias
    modulation = modulation.reshape(row_count, -1, 6 * model_width)
    per_token = jnp.einsum("rls,rse->rle", token_hot, modulation, precision=EXACT)
    shift_attn, scale_attn, gate_attn, shift_mlp, scale_mlp, gate_mlp = jnp.split(
        per_token, 6, axis=-1
    )
    hidden_full, pull_attn = jax.vjp(modulate, state, scale_attn, shift_attn)
    hidden_attn = hidden_full.astype(jnp.bfloat16)
    qkv_rows = (
        jnp.dot(hidden_attn, qkv_weight, preferred_element_type=jnp.float32) + qkv_bias
    ).astype(jnp.bfloat16)
    queries = qkv_rows[..., :model_width].reshape(row_count, local_len, HEADS, HEAD)
    key_value = lax.all_gather(qkv_rows[..., model_width:], "narrow", axis=1, tiled=True)
    full_len = key_value.shape[1]
    keys = key_value[..., :model_width].reshape(row_count, full_len, HEADS, HEAD)
    values = key_value[..., model_width:].reshape(row_count, full_len, HEADS, HEAD)
    scores = jnp.einsum("rqhe,rkhe->rhqk", queries, keys, preferred_element_type=jnp.float32) * (
        1.0 / math.sqrt(HEAD)
    )
    same_seg = seg_query[:, :, None] == seg_ids[:, None, :]
    attn_probs = jax.nn.softmax(jnp.where(same_seg[:, None], scores, -1e30), axis=-1)
    probs_low = attn_probs.astype(jnp.bfloat16)
    attn_mixed = jnp.einsum(
        "rhqk,rkhe->rqhe", probs_low, values, preferred_element_type=jnp.float32
    )
    attn_mixed = attn_mixed.reshape(row_count, local_len, model_width).astype(jnp.bfloat16)
    branch = jnp.dot(attn_mixed, out_weight, preferred_element_type=jnp.float32) + out_bias
    middle = state + gate_attn * branch
    hidden_wide, pull_mlp = jax.vjp(modulate, middle, scale_mlp, shift_mlp)
    hidden_mlp = hidden_wide.astype(jnp.bfloat16)
    up_proj = jnp.dot(hidden_mlp, up_weight, preferred_element_type=jnp.float32) + up_bias
    activated_full, pull_gelu = jax.vjp(partial(jax.nn.gelu, approximate=True), up_proj)
    activated = activated_full.astype(jnp.bfloat16)
    down_proj = jnp.dot(activated, down_weight, preferred_element_type=jnp.float32) + down_bias
    result = middle + gate_mlp * down_proj
    kept = (
        hidden_attn,
        pull_attn,
        queries,
        keys,
        values,
        attn_probs,
        probs_low,
        attn_mixed,
        branch,
        gate_attn,
        pull_mlp,
        hidden_mlp,
        pull_gelu,
        activated,
        down_proj,
        gate_mlp,
    )
    return (result, kept)


def layer_backward(grad_out, kept, weights, token_hot, lead_rows):
    (
        ada_weight,
        ada_bias,
        qkv_weight,
        qkv_bias,
        out_weight,
        out_bias,
        up_weight,
        up_bias,
        down_weight,
        down_bias,
    ) = weights
    (
        hidden_attn,
        pull_attn,
        queries,
        keys,
        values,
        attn_probs,
        probs_low,
        attn_mixed,
        branch,
        gate_attn,
        pull_mlp,
        hidden_mlp,
        pull_gelu,
        activated,
        down_proj,
        gate_mlp,
    ) = kept
    row_count, local_len, model_width = grad_out.shape
    full_len = keys.shape[1]
    scale_inv = 1.0 / math.sqrt(HEAD)
    grad_down = (gate_mlp * grad_out).astype(jnp.bfloat16)
    grad_gate_mlp = down_proj * grad_out
    grad_down_weight = jnp.einsum(
        "rlf,rld->fd", activated, grad_down, preferred_element_type=jnp.float32
    )
    grad_down_bias = jnp.sum(grad_down.astype(jnp.float32), axis=(0, 1))
    grad_act = jnp.einsum("rld,fd->rlf", grad_down, down_weight, preferred_element_type=jnp.float32)
    grad_up = pull_gelu(grad_act)[0].astype(jnp.bfloat16)
    grad_up_weight = jnp.einsum(
        "rld,rlf->df", hidden_mlp, grad_up, preferred_element_type=jnp.float32
    )
    grad_up_bias = jnp.sum(grad_up.astype(jnp.float32), axis=(0, 1))
    grad_hidden_mlp = jnp.einsum(
        "rlf,df->rld", grad_up, up_weight, preferred_element_type=jnp.float32
    )
    grad_middle, grad_scale_mlp, grad_shift_mlp = pull_mlp(grad_hidden_mlp)
    grad_middle = grad_middle + grad_out
    grad_branch = (gate_attn * grad_middle).astype(jnp.bfloat16)
    grad_gate_attn = branch * grad_middle
    grad_out_weight = jnp.einsum(
        "rld,rle->de", attn_mixed, grad_branch, preferred_element_type=jnp.float32
    )
    grad_out_bias = jnp.sum(grad_branch.astype(jnp.float32), axis=(0, 1))
    grad_attn = jnp.einsum(
        "rle,de->rld", grad_branch, out_weight, preferred_element_type=jnp.float32
    ).astype(jnp.bfloat16)
    grad_heads = grad_attn.reshape(queries.shape)
    grad_probs = jnp.einsum(
        "rqhe,rkhe->rhqk", grad_heads, values, preferred_element_type=jnp.float32
    )
    grad_scores = attn_probs * (grad_probs - jnp.sum(attn_probs * grad_probs, -1, keepdims=True))
    grad_scores = grad_scores.astype(jnp.bfloat16)
    grad_queries = (
        jnp.einsum("rhqk,rkhe->rqhe", grad_scores, keys, preferred_element_type=jnp.float32)
        * scale_inv
    )
    grad_keys = (
        jnp.einsum("rhqk,rqhe->rkhe", grad_scores, queries, preferred_element_type=jnp.float32)
        * scale_inv
    )
    grad_values = jnp.einsum(
        "rhqk,rqhe->rkhe", probs_low, grad_heads, preferred_element_type=jnp.float32
    )
    pair_grad = jnp.concatenate(
        [
            grad_keys.reshape(row_count, full_len, model_width),
            grad_values.reshape(row_count, full_len, model_width),
        ],
        axis=-1,
    )
    pair_own = lax.psum_scatter(
        pair_grad.astype(jnp.bfloat16), "narrow", scatter_dimension=1, tiled=True
    ).astype(jnp.float32)
    grad_qkv = jnp.concatenate(
        [grad_queries.reshape(row_count, local_len, model_width), pair_own], axis=-1
    ).astype(jnp.bfloat16)
    grad_qkv_weight = jnp.einsum(
        "rld,rle->de", hidden_attn, grad_qkv, preferred_element_type=jnp.float32
    )
    grad_qkv_bias = jnp.sum(grad_qkv.astype(jnp.float32), axis=(0, 1))
    grad_hidden_attn = jnp.einsum(
        "rle,de->rld", grad_qkv, qkv_weight, preferred_element_type=jnp.float32
    )
    grad_state, grad_scale_attn, grad_shift_attn = pull_attn(grad_hidden_attn)
    grad_state = grad_state + grad_middle
    grad_token_mod = jnp.concatenate(
        [
            grad_shift_attn,
            grad_scale_attn,
            grad_gate_attn,
            grad_shift_mlp,
            grad_scale_mlp,
            grad_gate_mlp,
        ],
        axis=-1,
    )
    grad_mod_part = jnp.einsum("rls,rle->rse", token_hot, grad_token_mod, precision=EXACT)
    grad_mod = lax.psum(grad_mod_part.astype(jnp.bfloat16), "narrow")
    grad_mod = grad_mod.reshape(-1, 6 * model_width)
    leader = (lax.axis_index("narrow") == 0).astype(jnp.float32)
    grad_ada_weight = (
        jnp.einsum("nd,ne->de", lead_rows, grad_mod, preferred_element_type=jnp.float32) * leader
    )
    grad_ada_bias = jnp.sum(grad_mod.astype(jnp.float32), axis=0) * leader
    grad_lead = jnp.einsum("ne,de->nd", grad_mod, ada_weight, preferred_element_type=jnp.float32)
    grads = (
        grad_ada_weight,
        grad_ada_bias,
        grad_qkv_weight,
        grad_qkv_bias,
        grad_out_weight,
        grad_out_bias,
        grad_up_weight,
        grad_up_bias,
        grad_down_weight,
        grad_down_bias,
    )
    return (grad_state, grad_lead, grads)


def per_device(
    tokens,
    cond,
    seg_ids,
    cond_index,
    cotangent,
    ada_weight,
    ada_bias,
    qkv_weight,
    qkv_bias,
    out_weight,
    out_bias,
    up_weight,
    up_bias,
    down_weight,
    down_bias,
):
    stacks = (
        ada_weight,
        ada_bias,
        qkv_weight,
        qkv_bias,
        out_weight,
        out_bias,
        up_weight,
        up_bias,
        down_weight,
        down_bias,
    )
    local_len = tokens.shape[1]
    seg_query = lax.dynamic_slice_in_dim(
        seg_ids, lax.axis_index("narrow") * local_len, local_len, 1
    )
    seg_range = jnp.arange(SEGS, dtype=jnp.int32)[None, None, :]
    token_hot = (seg_query[:, :, None] == seg_range).astype(jnp.float32)
    cond_hot = (cond_index[:, :, None] == seg_range).astype(jnp.float32)
    chosen = jnp.einsum("rsk,rkd->rsd", cond_hot, cond.astype(jnp.float32), precision=EXACT)
    lead_value, pull_lead = jax.vjp(silu_value, chosen)
    lead_rows = lead_value.astype(jnp.bfloat16).reshape(-1, lead_value.shape[-1])
    state = tokens.astype(jnp.float32)
    saved_inputs = []
    fetched = []
    for layer_idx in range(LAYERS):
        weights = fetch(stacks, layer_idx)
        fetched.append(weights)
        saved_inputs.append(state)
        state, unused_kept = layer_forward(state, lead_rows, token_hot, seg_query, seg_ids, weights)
    result = state.astype(jnp.bfloat16)
    grad_state = cotangent.astype(jnp.float32)
    grad_lead = jnp.zeros(lead_rows.shape, jnp.float32)
    reduced = [None] * LAYERS
    for layer_idx in reversed(range(LAYERS)):
        weights = fetch_again(stacks, layer_idx)
        unused_out, kept = layer_forward(
            saved_inputs[layer_idx], lead_rows, token_hot, seg_query, seg_ids, weights
        )
        grad_state, lead_part, grads = layer_backward(
            grad_state, kept, weights, token_hot, lead_rows
        )
        grad_lead = grad_lead + lead_part
        reduced[layer_idx] = reduce_grads(grads)
    grad_chosen = pull_lead(grad_lead.reshape(lead_value.shape))[0]
    cond_grad = jnp.einsum("rsk,rsd->rkd", cond_hot, grad_chosen, precision=EXACT)
    stacked = tuple(
        (
            jnp.stack([reduced[layer_pos][member_pos] for layer_pos in range(LAYERS)])
            for member_pos in range(10)
        )
    )
    return (result, grad_state, cond_grad) + stacked


def solution(mesh):
    placed = (
        P("wide", "narrow", None),
        P("wide", None, None),
        P("wide", None),
        P("wide", None),
        P("wide", "narrow", None),
        P(None, "wide", None),
        P(None, "wide"),
        P(None, "wide", None),
        P(None, "wide"),
        P(None, "wide", None),
        P(None, "wide"),
        P(None, "wide", None),
        P(None, "wide"),
        P(None, "wide", None),
        P(None, "wide"),
    )
    return jax.shard_map(
        per_device,
        mesh=mesh,
        in_specs=placed,
        out_specs=(
            P("wide", "narrow", None),
            P("wide", "narrow", None),
            P("wide", None, None),
            P(None, "wide", None),
            P(None, "wide"),
            P(None, "wide", None),
            P(None, "wide"),
            P(None, "wide", None),
            P(None, "wide"),
            P(None, "wide", None),
            P(None, "wide"),
            P(None, "wide", None),
            P(None, "wide"),
        ),
        check_vma=False,
    )
```

profile of v0, /device:TPU:17, one launch (start us, length us, event | category | flops | bytes accessed | tf_op | source)
XLA Modules:
  0.0 3825.3 jit_solution(3418225391759596608)
XLA Ops:
  28.2 61.5 %all-reduce.68.cloned.1.call-done = (bf16[6912]{0:T(1024)(128)(2,1)}, bf16[3456]{0:T(1024)(128)(2,1)}, bf16[1152]{0:T(1024)(128)(2,1)}, bf16[1152]{0:T(1024)(128...) async-done(((bf16[6912]{0:T(1024)(128)(2,1)}, ...) | async-done | bytes 69136
  91.7 218.4 %all-gather.55.cloned.1.call-done = bf16[1,1152,6912]{2,1,0:T(8,128)(2,1)} async-done(((bf16[1,144,6912]{2,1,0:T(8,128)(2,1)}), bf16[1,1152,6912]{2,1,0:T(8,128)(2,1)}) %all-gather.55.cloned.1.call-update) | async-done | bytes 15925264 | tf_op jit(solution)/shard_map/all_gather | solution.py:34
  310.1 7.7 fusion.42
  320.4 110.2 %all-gather.57.cloned.1.call-done = bf16[1,1152,3456]{2,1,0:T(8,128)(2,1)} async-done(((bf16[1,144,3456]{2,1,0:T(8,128)(2,1)}), bf16[1,1152,3456]{2,1,0:T(8,128)(2,1)}) %all-gather.57.cloned.1.call-update) | async-done | bytes 7962640 | tf_op jit(solution)/shard_map/all_gather | solution.py:36
  457.1 191.6 %all-gather.65.cloned.1.call-done = bf16[1,1152,6912]{2,1,0:T(8,128)(2,1)} async-done(((bf16[1,144,6912]{2,1,0:T(8,128)(2,1)}), bf16[1,1152,6912]{2,1,0:T(8,128)(2,1)}) %all-gather.65.cloned.1.call-update) | async-done | bytes 15925264 | tf_op jit(solution)/shard_map/all_gather | solution.py:34
  648.7 7.7 fusion.45
  659.8 14.9 all-gather.47.cloned.1.call-done
  692.5 37.6 all-gather.59.cloned.1.call-done
  735.8 148.1 %all-gather.61.cloned.1.call-done = bf16[1,1152,4608]{2,1,0:T(8,128)(2,1)} async-done(((bf16[1,144,4608]{2,1,0:T(8,128)(2,1)}), bf16[1,1152,4608]{2,1,0:T(8,128)(2,1)}) %all-gather.61.cloned.1.call-update) | async-done | bytes 10616848 | tf_op jit(solution)/shard_map/all_gather | solution.py:40
  883.9 7.1 fusion.48
  891.0 146.3 %all-gather.63.cloned.1.call-done = bf16[1,4608,1152]{2,1,0:T(8,128)(2,1)} async-done(((bf16[1,576,1152]{2,1,0:T(8,128)(2,1)}), bf16[1,4608,1152]{2,1,0:T(8,128)(2,1)}) %all-gather.63.cloned.1.call-update) | async-done | bytes 10616848 | tf_op jit(solution)/shard_map/all_gather | solution.py:42
  1037.3 7.7 fusion.238
  1048.2 109.2 %all-gather.67.cloned.1.call-done = bf16[1,1152,3456]{2,1,0:T(8,128)(2,1)} async-done(((bf16[1,144,3456]{2,1,0:T(8,128)(2,1)}), bf16[1,1152,3456]{2,1,0:T(8,128)(2,1)}) %all-gather.67.cloned.1.call-update) | async-done | bytes 7962640 | tf_op jit(solution)/shard_map/all_gather | solution.py:36
  1175.3 12.6 all-gather.49.cloned.1.call-done
  1206.1 37.3 all-gather.69.cloned.1.call-done
  1250.1 146.4 %all-gather.71.cloned.1.call-done = bf16[1,1152,4608]{2,1,0:T(8,128)(2,1)} async-done(((bf16[1,144,4608]{2,1,0:T(8,128)(2,1)}), bf16[1,1152,4608]{2,1,0:T(8,128)(2,1)}) %all-gather.71.cloned.1.call-update) | async-done | bytes 10616848 | tf_op jit(solution)/shard_map/all_gather | solution.py:40
  1396.5 7.2 fusion.51
  1403.7 146.2 %all-gather.73.cloned.1.call-done = bf16[1,4608,1152]{2,1,0:T(8,128)(2,1)} async-done(((bf16[1,576,1152]{2,1,0:T(8,128)(2,1)}), bf16[1,4608,1152]{2,1,0:T(8,128)(2,1)}) %all-gather.73.cloned.1.call-update) | async-done | bytes 10616848 | tf_op jit(solution)/shard_map/all_gather | solution.py:42
  1549.9 10.4 fusion.251
  1566.3 7.3 fusion.236
  1587.9 11.2 copy.60
  1606.8 29.1 reduce-scatter.59.cloned.1.call-done
  1652.4 9.8 fusion.252
  1682.7 11.2 copy.62
  1698.4 9.4 convolution_convert_fusion
  1707.9 8.8 convolution_convert_fusion.1
  1748.5 165.3 %reduce-scatter.55.cloned.1.call-done = bf16[576,1152]{1,0:T(8,128)(2,1)} async-done(((bf16[4608,1152]{1,0:T(8,128)(2,1)}), bf16[576,1152]{1,0:T(8,128)(2,1)}) %reduce-scatter.55.cloned.1.call-update) | async-done | bytes 1327120 | tf_op jit(solution)/shard_map/reduce_scatter | solution.py:88
  1913.9 182.9 %reduce-scatter.51.cloned.1.call-done = bf16[576,1152]{1,0:T(8,128)(2,1)} async-done(((bf16[4608,1152]{1,0:T(8,128)(2,1)}), bf16[576,1152]{1,0:T(8,128)(2,1)}) %reduce-scatter.51.cloned.1.call-update) | async-done | bytes 1327120 | tf_op jit(solution)/shard_map/reduce_scatter | solution.py:88
  2129.5 8.8 multiply_convert_fusion.1
  2139.1 7.9 multiply_convert_fusion
  2150.4 9.5 reduce-scatter.57.cloned.1.call-done
  2159.9 29.0 reduce-scatter.53.cloned.1.call-done
  2189.0 73.0 %reduce-scatter.45.cloned.1.call-done = bf16[144,1152]{1,0:T(8,128)(2,1)} async-done(((bf16[1152,1152]{1,0:T(8,128)(2,1)}), bf16[144,1152]{1,0:T(8,128)(2,1)}) %reduce-scatter.45.cloned.1.call-update) | async-done | bytes 331792 | tf_op jit(solution)/shard_map/reduce_scatter | solution.py:76
  2262.0 73.9 %reduce-scatter.43.cloned.1.call-done = bf16[144,1152]{1,0:T(8,128)(2,1)} async-done(((bf16[1152,1152]{1,0:T(8,128)(2,1)}), bf16[144,1152]{1,0:T(8,128)(2,1)}) %reduce-scatter.43.cloned.1.call-update) | async-done | bytes 331792 | tf_op jit(solution)/shard_map/reduce_scatter | solution.py:76
  2335.9 147.6 %reduce-scatter.41.cloned.1.call-done = bf16[144,3456]{1,0:T(8,128)(2,1)} async-done(((bf16[1152,3456]{1,0:T(8,128)(2,1)}), bf16[144,3456]{1,0:T(8,128)(2,1)}) %reduce-scatter.41.cloned.1.call-update) | async-done | bytes 995344 | tf_op jit(solution)/shard_map/reduce_scatter | solution.py:70
  2483.5 182.8 %reduce-scatter.49.cloned.1.call-done = bf16[144,4608]{1,0:T(8,128)(2,1)} async-done(((bf16[1152,4608]{1,0:T(8,128)(2,1)}), bf16[144,4608]{1,0:T(8,128)(2,1)}) %reduce-scatter.49.cloned.1.call-update) | async-done | bytes 1327120 | tf_op jit(solution)/shard_map/reduce_scatter | solution.py:82
  2666.3 145.3 %reduce-scatter.39.cloned.1.call-done = bf16[144,3456]{1,0:T(8,128)(2,1)} async-done(((bf16[1152,3456]{1,0:T(8,128)(2,1)}), bf16[144,3456]{1,0:T(8,128)(2,1)}) %reduce-scatter.39.cloned.1.call-update) | async-done | bytes 995344 | tf_op jit(solution)/shard_map/reduce_scatter | solution.py:70
  2811.7 182.6 %reduce-scatter.47.cloned.1.call-done = bf16[144,4608]{1,0:T(8,128)(2,1)} async-done(((bf16[1152,4608]{1,0:T(8,128)(2,1)}), bf16[144,4608]{1,0:T(8,128)(2,1)}) %reduce-scatter.47.cloned.1.call-update) | async-done | bytes 1327120 | tf_op jit(solution)/shard_map/reduce_scatter | solution.py:82
  2994.2 272.0 %reduce-scatter.35.cloned.1.call-done = bf16[144,6912]{1,0:T(8,128)(2,1)} async-done(((bf16[1152,6912]{1,0:T(8,128)(2,1)}), bf16[144,6912]{1,0:T(8,128)(2,1)}) %reduce-scatter.35.cloned.1.call-update) | async-done | bytes 1990672 | tf_op jit(solution)/shard_map/reduce_scatter | solution.py:64
  3266.2 272.2 %reduce-scatter.37.cloned.1.call-done = bf16[144,6912]{1,0:T(8,128)(2,1)} async-done(((bf16[1152,6912]{1,0:T(8,128)(2,1)}), bf16[144,6912]{1,0:T(8,128)(2,1)}) %reduce-scatter.37.cloned.1.call-update) | async-done | bytes 1990672 | tf_op jit(solution)/shard_map/reduce_scatter | solution.py:64
  3538.4 101.1 %fusion.227 = (bf16[40,6912]{1,0:T(8,128)(2,1)S(1)}, bf16[40,6912]{1,0:T(8,128)(2,1)S(1)}, bf16[48,3456]{1,0:T(8,128)(2,1)S(1)}, bf16[48,3456]{1,0:T(8,128)(2,1)...) fusion(bf16[144,6912]{1,0:T(8,128)(2,1)} %reduce-scatter.37.clo, ...), kind=kCustom, calls=%all-reduce-scatter.8 | all-reduce-scatter fusion | flops 5455874 | bytes 12018176
  3672.3 9.8 fusion.10
  3686.0 9.7 fusion.144
  3704.2 9.5 all-reduce.59
  3716.5 11.1 all-reduce.58
  3749.6 7.1 all-gather.24
  3772.1 14.5 all-gather.22
  3788.0 12.3 all-gather.23
  (566 shorter events, 355.3 us)
Async XLA Ops:
  7.2 82.5 %all-reduce.68.cloned.1.call-start = ((), (), s32[]{:S(2)}) async-start(), calls=%async_computation.47 | async-start | bytes 163840
  18.3 291.8 %all-gather.55.cloned.1.call-start = ((), (), s32[]{:S(2)}) async-start(), calls=%async_computation.30 | async-start | bytes 17915904 | tf_op jit(solution)/shard_map/all_gather | solution.py:34
  22.8 407.9 %all-gather.57.cloned.1.call-start = ((), (), s32[]{:S(2)}) async-start(), calls=%async_computation.31 | async-start | bytes 8957952 | tf_op jit(solution)/shard_map/all_gather | solution.py:36
  25.7 623.0 %all-gather.65.cloned.1.call-start = ((), (), s32[]{:S(2)}) async-start(), calls=%async_computation.35 | async-start | bytes 17915904 | tf_op jit(solution)/shard_map/all_gather | solution.py:34
  26.3 648.4 %all-gather.47.cloned.1.call-start = ((), (), s32[]{:S(2)}) async-start(), calls=%async_computation.14 | async-start | bytes 2949120 | tf_op jit(solution)/shard_map/all_gather | solution.py:187
  437.1 293.1 %all-gather.59.cloned.1.call-start = ((), (), s32[]{:S(2)}) async-start(), calls=%async_computation.32 | async-start | bytes 2985984 | tf_op jit(solution)/shard_map/all_gather | solution.py:38
  439.2 444.7 %all-gather.61.cloned.1.call-start = ((), (), s32[]{:S(2)}) async-start(), calls=%async_computation.33 | async-start | bytes 11943936 | tf_op jit(solution)/shard_map/all_gather | solution.py:40
  442.9 594.4 %all-gather.63.cloned.1.call-start = ((), (), s32[]{:S(2)}) async-start(), calls=%async_computation.34 | async-start | bytes 11943936 | tf_op jit(solution)/shard_map/all_gather | solution.py:42
  446.6 710.7 %all-gather.67.cloned.1.call-start = ((), (), s32[]{:S(2)}) async-start(), calls=%async_computation.36 | async-start | bytes 8957952 | tf_op jit(solution)/shard_map/all_gather | solution.py:36
  447.4 740.5 %all-gather.49.cloned.1.call-start = ((), (), s32[]{:S(2)}) async-start(), calls=%async_computation.15 | async-start | bytes 2949120 | tf_op jit(solution)/shard_map/all_gather | solution.py:187
  735.8 301.5 %copy-start.87 = (f32[1152]{0:T(1024)S(1)}, f32[1152]{0:T(1024)}, u32[]{:S(2)}) copy-start(f32[1152]{0:T(1024)} %convert_element_type.475) | copy-start | bytes 13828
  1163.7 79.8 %all-gather.69.cloned.1.call-start = ((), (), s32[]{:S(2)}) async-start(), calls=%async_computation.37 | async-start | bytes 2985984 | tf_op jit(solution)/shard_map/all_gather | solution.py:38
  1164.5 232.0 %all-gather.71.cloned.1.call-start = ((), (), s32[]{:S(2)}) async-start(), calls=%async_computation.38 | async-start | bytes 11943936 | tf_op jit(solution)/shard_map/all_gather | solution.py:40
  1165.1 384.9 %all-gather.73.cloned.1.call-start = ((), (), s32[]{:S(2)}) async-start(), calls=%async_computation.39 | async-start | bytes 11943936 | tf_op jit(solution)/shard_map/all_gather | solution.py:42
  1165.8 470.1 %reduce-scatter.59.cloned.1.call-start = ((), (), s32[]{:S(2)}) async-start(), calls=%async_computation.44 | async-start | bytes 2949120
  1247.1 319.1 %copy-start.82 = (f32[128]{0:T(128)}, f32[128]{0:T(128)S(1)}, u32[]{:S(2)}) copy-start(f32[128]{0:T(128)S(1)} %broadcast_multiply_fusion) | copy-start | bytes 1540
  1247.9 318.3 %copy-start.97 = (f32[128]{0:T(128)}, f32[128]{0:T(128)S(1)}, u32[]{:S(2)}) copy-start(f32[128]{0:T(128)S(1)} %fusion.217) | copy-start | bytes 1540
  1603.2 128.0 %reduce-scatter.61.cloned.1.call-start = ((), (), s32[]{:S(2)}) async-start(), calls=%async_computation.45 | async-start | bytes 2949120
  1698.0 215.8 %reduce-scatter.55.cloned.1.call-start = ((), (), s32[]{:S(2)}) async-start(), calls=%async_computation.27 | async-start | bytes 11943936 | tf_op jit(solution)/shard_map/reduce_scatter | solution.py:88
  1707.8 388.9 %reduce-scatter.51.cloned.1.call-start = ((), (), s32[]{:S(2)}) async-start(), calls=%async_computation.24 | async-start | bytes 11943936 | tf_op jit(solution)/shard_map/reduce_scatter | solution.py:88
  1716.8 412.7 %all-reduce.70.cloned.1.call-start = ((), (), s32[]{:S(2)}) async-start(), calls=%async_computation.48 | async-start | bytes 221184 | tf_op jit(solution)/shard_map/psum | solution.py:342
  1746.6 350.3 %copy-start.50 = (bf16[1,128,1152]{2,1,0:T(8,128)(2,1)S(1)}, bf16[1,128,1152]{2,1,0:T(8,128)(2,1)}, u32[]{:S(2)}) copy-start(bf16[1,128,1152]{2,1,0:T(8,128)(2,1)} %copy-done.49) | copy-start | bytes 884740
  1746.6 350.3 %copy-start.54 = (bf16[16,72,128]{2,1,0:T(8,128)(2,1)S(1)}, bf16[16,72,128]{2,1,0:T(8,128)(2,1)}, u32[]{:S(2)}) copy-start(bf16[16,72,128]{2,1,0:T(8,128)(2,1)} %convolution_convert_fusion.12) | copy-start | bytes 884740
  1748.5 411.4 %reduce-scatter.57.cloned.1.call-start = ((), (), s32[]{:S(2)}) async-start(), calls=%async_computation.28 | async-start | bytes 1658880 | tf_op jit(solution)/shard_map/reduce_scatter | solution.py:120
  1913.8 275.1 %reduce-scatter.53.cloned.1.call-start = ((), (), s32[]{:S(2)}) async-start(), calls=%async_computation.25 | async-start | bytes 1658880 | tf_op jit(solution)/shard_map/reduce_scatter | solution.py:120
  2096.8 165.2 %reduce-scatter.45.cloned.1.call-start = ((), (), s32[]{:S(2)}) async-start(), calls=%async_computation.21 | async-start | bytes 2985984 | tf_op jit(solution)/shard_map/reduce_scatter | solution.py:76
  2099.3 236.6 %reduce-scatter.43.cloned.1.call-start = ((), (), s32[]{:S(2)}) async-start(), calls=%async_computation.20 | async-start | bytes 2985984 | tf_op jit(solution)/shard_map/reduce_scatter | solution.py:76
  2101.7 381.8 %reduce-scatter.41.cloned.1.call-start = ((), (), s32[]{:S(2)}) async-start(), calls=%async_computation.19 | async-start | bytes 8957952 | tf_op jit(solution)/shard_map/reduce_scatter | solution.py:70
  2107.3 559.0 %reduce-scatter.49.cloned.1.call-start = ((), (), s32[]{:S(2)}) async-start(), calls=%async_computation.23 | async-start | bytes 11943936 | tf_op jit(solution)/shard_map/reduce_scatter | solution.py:82
  2114.2 697.4 %reduce-scatter.39.cloned.1.call-start = ((), (), s32[]{:S(2)}) async-start(), calls=%async_computation.18 | async-start | bytes 8957952 | tf_op jit(solution)/shard_map/reduce_scatter | solution.py:70
  2121.0 873.3 %reduce-scatter.47.cloned.1.call-start = ((), (), s32[]{:S(2)}) async-start(), calls=%async_computation.22 | async-start | bytes 11943936 | tf_op jit(solution)/shard_map/reduce_scatter | solution.py:82
  2127.9 1138.3 %reduce-scatter.35.cloned.1.call-start = ((), (), s32[]{:S(2)}) async-start(), calls=%async_computation.16 | async-start | bytes 17915904 | tf_op jit(solution)/shard_map/reduce_scatter | solution.py:64
  2138.3 1400.1 %reduce-scatter.37.cloned.1.call-start = ((), (), s32[]{:S(2)}) async-start(), calls=%async_computation.17 | async-start | bytes 17915904 | tf_op jit(solution)/shard_map/reduce_scatter | solution.py:64
  2147.1 1549.6 %all-reduce.66.cloned.1.call-start = ((), (), s32[]{:S(2)}) async-start(), calls=%async_computation.46 | async-start | bytes 163840
  2150.3 1586.6 %all-gather.53.cloned.1.call-start = ((), (), s32[]{:S(2)}) async-start(), calls=%async_computation.29 | async-start | bytes 1658880 | tf_op jit(solution)/shard_map/all_gather | solution.py:152
  2159.9 1577.1 %all-gather.51.cloned.1.call-start = ((), (), s32[]{:S(2)}) async-start(), calls=%async_computation.26 | async-start | bytes 1658880 | tf_op jit(solution)/shard_map/all_gather | solution.py:152
  2188.9 1613.8 %all-gather.79.cloned.1.call-start = ((), (), s32[]{:S(2)}) async-start(), calls=%async_computation.42 | async-start | bytes 1843200 | tf_op jit(solution)/shard_map/all_gather | solution.py:146
  3639.6 6.5 collective-permute-start.6
  3648.4 155.9 %all-gather.81.cloned.1.call-start = ((), (), s32[]{:S(2)}) async-start(), calls=%async_computation.43 | async-start | bytes 1843200 | tf_op jit(solution)/shard_map/all_gather | solution.py:146
  3648.5 9.7 collective-permute-start.7
  3659.6 148.9 %all-gather.75.cloned.1.call-start = ((), (), s32[]{:S(2)}) async-start(), calls=%async_computation.40 | async-start | bytes 2764800 | tf_op jit(solution)/shard_map/all_gather | solution.py:128
  3667.7 14.4 collective-permute-start
  3686.0 124.4 %all-gather.77.cloned.1.call-start = ((), (), s32[]{:S(2)}) async-start(), calls=%async_computation.41 | async-start | bytes 2764800 | tf_op jit(solution)/shard_map/all_gather | solution.py:128
  3730.7 18.1 collective-permute-start.4
  3735.0 14.2 collective-permute-start.5
  3742.2 27.0 collective-permute-start.2
  3744.9 41.9 %collective-permute-start.3 = (bf16[36,3456]{1,0:T(8,128)(2,1)}, bf16[36,3456]{1,0:T(8,128)(2,1)S(1)}, u32[]{:S(2)}, u32[]{:S(2)}) collective-permute-start(bf16[36,3456]{1,0:T(8,128)(2,1)} %slice.151), channel_id=1, source_target_pairs={{0,1},{1,2},{2,3},{4,5},{5,6},{6,7},{8,9},{9,10},{10,11},{12,13},{... | collective-permute-start | bytes 746504
  3746.9 16.4 collective-permute-start.1
  (110 other events, 1481.2 us)
Sparse Core Ops, SparseCore 0:
  18.5 71.1 all-reduce.67
  92.4 217.6 all-gather.54
  312.9 117.7 all-gather.56
  433.3 215.3 all-gather.64
  650.7 23.9 all-gather.46
  676.7 53.4 all-gather.58
  732.9 150.9 all-gather.60
  886.7 150.6 all-gather.62
  1039.5 117.7 all-gather.66
  1163.9 23.9 all-gather.48
  1190.0 53.4 all-gather.68
  1245.5 150.9 all-gather.70
  1399.2 150.6 all-gather.72
  1603.3 32.5 reduce-scatter.58
  1698.1 33.0 reduce-scatter.60
  1734.7 179.0 reduce-scatter.54
  1917.7 179.0 reduce-scatter.50
  2099.0 30.4 all-reduce.69
  2132.2 27.6 reduce-scatter.56
  2162.2 26.6 reduce-scatter.52
  2193.6 68.3 reduce-scatter.44
  2266.2 69.6 reduce-scatter.42
  2340.5 142.9 reduce-scatter.40
  2487.4 178.9 reduce-scatter.48
  2670.0 141.6 reduce-scatter.38
  2815.1 179.0 reduce-scatter.46
  2998.4 267.7 reduce-scatter.34
  3270.6 267.7 reduce-scatter.36
  3544.9 69.8 all-reduce.65
  3616.2 24.1 all-gather.52
  3642.1 18.2 all-gather.50
  3662.1 20.6 all-gather.78
  3684.8 21.4 all-gather.80
  3708.0 23.5 all-gather.74
  3768.2 27.3 all-gather.76
where the time goes:
time: 3840 us; the launch traced here: 3830 us
  waiting for transfers between devices  3160 us (82%)
  matrix products  237 us (6%)
  blocking collectives  162 us (4%)
  local copies, waits for them, and re-layouts  153 us (4%)
  other arithmetic  60.1 us (2%)
    reduce_scatter x2, waiting for transfers between devices, reduce_grads(): lax.psum_scatter(grads[0].astype(jnp.bfloat16), 'wide', scatter_dimension...  544 us
    all_gather x2, waiting for transfers between devices, fetch(): lax.all_gather(stacks[0][layer_idx], 'wide', axis=0, tiled=True)  410 us
    reduce_scatter x2, waiting for transfers between devices, reduce_grads(): lax.psum_scatter(grads[6].astype(jnp.bfloat16), 'wide', scatter_dimension...  365 us
    reduce_scatter x2, waiting for transfers between devices, reduce_grads(): lax.psum_scatter(grads[8].astype(jnp.bfloat16), 'wide', scatter_dimension...  348 us
    all_gather x2, waiting for transfers between devices, fetch(): lax.all_gather(stacks[6][layer_idx], 'wide', axis=0, tiled=True)  295 us
    reduce_scatter x2, waiting for transfers between devices, reduce_grads(): lax.psum_scatter(grads[2].astype(jnp.bfloat16), 'wide', scatter_dimension...  293 us
    all_gather x2, waiting for transfers between devices, fetch(): lax.all_gather(stacks[8][layer_idx], 'wide', axis=0, tiled=True)  293 us
    all_gather x2, waiting for transfers between devices, fetch(): lax.all_gather(stacks[2][layer_idx], 'wide', axis=0, tiled=True)  219 us
  transfers between devices with their start and end apart: 43, of which 30 were waited for; matrix products, arithmetic and copies ran while one was open for 11% of the time, Pallas kernels for 0%

commit v1 on v0

v1 whole, which is shorter than its diff:
```python
from functools import partial
import math

import jax
import jax.numpy as jnp
from jax import lax
from jax.sharding import PartitionSpec as P

HEADS = 16
HEAD = 72
LAYERS = 2
SEGS = 4
EPS = 1e-06
EXACT = lax.Precision.HIGHEST
F32 = jnp.float32
BF16 = jnp.bfloat16


def dot(left, right, dims):
    return lax.dot_general(left, right, (dims, ((), ())), preferred_element_type=F32)


def norm(values):
    centred = values - jnp.mean(values, -1, keepdims=True)
    inv = lax.rsqrt(jnp.mean(centred * centred, -1, keepdims=True) + EPS)
    return centred * inv, inv


def norm_back(grad, unit, inv):
    return inv * (
        grad
        - jnp.mean(grad, -1, keepdims=True)
        - unit * jnp.mean(grad * unit, -1, keepdims=True)
    )


def gather_tokens(values):
    return lax.all_gather(values, "narrow", axis=0, tiled=True)


def scatter_tokens(values):
    return lax.psum_scatter(
        values.astype(BF16), "narrow", scatter_dimension=0, tiled=True
    ).astype(F32)


def gelu(values):
    return jax.nn.gelu(values, approximate=True)


def layer_forward(state, mods, same_seg, weights):
    qkv_w, qkv_b, out_w, out_b, up_w, up_b, down_w, down_b = weights
    shift_attn, scale_attn, gate_attn, shift_mlp, scale_mlp, gate_mlp = mods
    own_heads = out_w.shape[0] // HEAD
    unit_attn, inv_attn = norm(state)
    hidden_attn = gather_tokens((unit_attn * (1.0 + scale_attn) + shift_attn).astype(BF16))
    full_len = hidden_attn.shape[0]
    qkv = (dot(hidden_attn, qkv_w, ((1,), (0,))) + qkv_b).astype(BF16)
    queries, keys, values = [
        part.reshape(full_len, own_heads, HEAD) for part in jnp.split(qkv, 3, axis=-1)
    ]
    scores = jnp.einsum("qhe,khe->hqk", queries, keys, preferred_element_type=F32) * (
        1.0 / math.sqrt(HEAD)
    )
    probs = jax.nn.softmax(jnp.where(same_seg[None], scores, -1e30), axis=-1)
    mixed = jnp.einsum("hqk,khe->qhe", probs.astype(BF16), values, preferred_element_type=F32)
    mixed = mixed.reshape(full_len, own_heads * HEAD).astype(BF16)
    branch = scatter_tokens(dot(mixed, out_w, ((1,), (0,)))) + out_b
    middle = state + gate_attn * branch
    unit_mlp, inv_mlp = norm(middle)
    hidden_mlp = gather_tokens((unit_mlp * (1.0 + scale_mlp) + shift_mlp).astype(BF16))
    up_proj = dot(hidden_mlp, up_w, ((1,), (0,))) + up_b
    activated = gelu(up_proj).astype(BF16)
    down_proj = scatter_tokens(dot(activated, down_w, ((1,), (0,)))) + down_b
    result = middle + gate_mlp * down_proj
    kept = (
        unit_attn, inv_attn, hidden_attn, queries, keys, values, probs, mixed, branch,
        unit_mlp, inv_mlp, hidden_mlp, up_proj, activated, down_proj,
    )
    return result, kept


def layer_backward(grad_out, kept, mods, weights):
    qkv_w, qkv_b, out_w, out_b, up_w, up_b, down_w, down_b = weights
    shift_attn, scale_attn, gate_attn, shift_mlp, scale_mlp, gate_mlp = mods
    (
        unit_attn, inv_attn, hidden_attn, queries, keys, values, probs, mixed, branch,
        unit_mlp, inv_mlp, hidden_mlp, up_proj, activated, down_proj,
    ) = kept
    scale_inv = 1.0 / math.sqrt(HEAD)
    full_len = hidden_attn.shape[0]
    own_down = (gate_mlp * grad_out).astype(BF16)
    grad_gate_mlp = down_proj * grad_out
    grad_down = gather_tokens(own_down)
    grad_act = dot(grad_down, down_w, ((1,), (1,)))
    grad_up = jax.vjp(gelu, up_proj)[1](grad_act)[0].astype(BF16)
    grad_hidden_mlp = scatter_tokens(dot(grad_up, up_w, ((1,), (1,))))
    grad_down_w = dot(activated, grad_down, ((0,), (0,)))
    grad_up_w = dot(hidden_mlp, grad_up, ((0,), (0,)))
    grad_middle = grad_out + norm_back(grad_hidden_mlp * (1.0 + scale_mlp), unit_mlp, inv_mlp)
    own_branch = (gate_attn * grad_middle).astype(BF16)
    grad_gate_attn = branch * grad_middle
    grad_branch = gather_tokens(own_branch)
    grad_attn = dot(grad_branch, out_w, ((1,), (1,))).astype(BF16).reshape(queries.shape)
    grad_probs = jnp.einsum("qhe,khe->hqk", grad_attn, values, preferred_element_type=F32)
    grad_scores = probs * (grad_probs - jnp.sum(probs * grad_probs, -1, keepdims=True))
    grad_scores = grad_scores.astype(BF16)
    grad_q = jnp.einsum("hqk,khe->qhe", grad_scores, keys, preferred_element_type=F32) * scale_inv
    grad_k = jnp.einsum("hqk,qhe->khe", grad_scores, queries, preferred_element_type=F32) * scale_inv
    grad_v = jnp.einsum("hqk,qhe->khe", probs.astype(BF16), grad_attn, preferred_element_type=F32)
    grad_qkv = jnp.concatenate(
        [part.astype(BF16).reshape(full_len, -1) for part in (grad_q, grad_k, grad_v)], axis=-1
    )
    grad_hidden_attn = scatter_tokens(dot(grad_qkv, qkv_w, ((1,), (1,))))
    grad_out_w = dot(mixed, grad_branch, ((0,), (0,)))
    grad_qkv_w = dot(hidden_attn, grad_qkv, ((0,), (0,)))
    grad_state = grad_middle + norm_back(grad_hidden_attn * (1.0 + scale_attn), unit_attn, inv_attn)
    token_mod = jnp.concatenate(
        [
            grad_hidden_attn, grad_hidden_attn * unit_attn, grad_gate_attn,
            grad_hidden_mlp, grad_hidden_mlp * unit_mlp, grad_gate_mlp,
        ],
        axis=-1,
    )
    bias_grads = (
        jnp.sum(grad_qkv.astype(F32), 0),
        jnp.sum(own_branch.astype(F32), 0),
        jnp.sum(grad_up.astype(F32), 0),
        jnp.sum(own_down.astype(F32), 0),
    )
    return grad_state, token_mod, (grad_qkv_w, grad_out_w, grad_up_w, grad_down_w), bias_grads


def per_device(
    wide, narrow,
    tokens, cond, seg_ids, cond_index, cotangent,
    ada_weight, ada_bias, qkv_weight, qkv_bias, out_weight, out_bias,
    up_weight, up_bias, down_weight, down_bias,
):
    w = lax.axis_index("wide")
    n = lax.axis_index("narrow")
    local_len, width = tokens.shape[1:]
    depth = width // wide
    cols = width // narrow
    hidden_own = up_weight.shape[-1] // wide // narrow
    mod_cols = ada_weight.shape[-1] // narrow

    def own(values, axis):
        return lax.dynamic_index_in_dim(values, n, axis, keepdims=False)

    bias_parts = (ada_bias, qkv_bias, out_bias, up_bias, down_bias)
    sizes = [part.shape[1] for part in bias_parts]
    packed = lax.all_gather(jnp.concatenate(bias_parts, axis=1), "wide", axis=1, tiled=False)
    biases = []
    at = 0
    for size in sizes:
        biases.append(packed[:, :, at : at + size].reshape(LAYERS, -1).astype(F32))
        at += size
    ada_b, qkv_b, out_b, up_b, down_b = biases
    qkv_b = own(qkv_b.reshape(LAYERS, 3, narrow, cols), 2).reshape(LAYERS, 3 * cols)
    up_b = own(up_b.reshape(LAYERS, wide, narrow, hidden_own), 2).reshape(LAYERS, -1)

    cond_hot = (cond_index[0, :, None] == jnp.arange(SEGS, dtype=jnp.int32)[None, :]).astype(F32)
    chosen = jnp.dot(cond_hot, cond[0].astype(F32), precision=EXACT)
    lead = (chosen * jax.nn.sigmoid(chosen)).astype(BF16)
    lead_all = lax.all_gather(lead, "wide", axis=0, tiled=True)
    lead_own = lax.dynamic_slice_in_dim(lead_all, w * depth, depth, 1)
    ada_quarter = lax.dynamic_slice_in_dim(ada_weight, n * mod_cols, mod_cols, 2)
    mod_part = jnp.einsum("nd,lde->nle", lead_own, ada_quarter, preferred_element_type=F32)
    mod_part = lax.psum_scatter(mod_part, "wide", scatter_dimension=0, tiled=True)
    modulation = lax.all_gather(mod_part, "narrow", axis=2, tiled=True)
    modulation = modulation.transpose(1, 0, 2) + ada_b[:, None, :]

    seg_row = seg_ids[0]
    seg_query = lax.dynamic_slice_in_dim(seg_row, n * local_len, local_len, 0)
    token_hot = (seg_query[:, None] == jnp.arange(SEGS, dtype=jnp.int32)[None, :]).astype(F32)
    same_seg = seg_row[:, None] == seg_row[None, :]

    qkv_own = own(qkv_weight.reshape(LAYERS, depth, 3, narrow, cols), 3).reshape(LAYERS, depth, 3 * cols)
    up_own = own(up_weight.reshape(LAYERS, depth, wide, narrow, hidden_own), 3).reshape(LAYERS, depth, -1)
    down_own = own(down_weight.reshape(LAYERS, narrow, hidden_own, width), 1)

    def fetch(idx):
        out_full = lax.all_gather(out_weight[idx], "wide", axis=0, tiled=True)
        return (
            lax.all_gather(qkv_own[idx], "wide", axis=0, tiled=True),
            qkv_b[idx],
            lax.dynamic_slice_in_dim(out_full, n * cols, cols, 0),
            out_b[idx],
            lax.all_gather(up_own[idx], "wide", axis=0, tiled=True),
            up_b[idx],
            lax.all_gather(down_own[idx], "wide", axis=0, tiled=True),
            down_b[idx],
        )

    state = tokens[0].astype(F32)
    weights, mods, kept = [], [], []
    for idx in range(LAYERS):
        weights.append(fetch(idx))
        per_token = jnp.dot(token_hot, modulation[idx], precision=EXACT)
        mods.append(jnp.split(per_token, 6, axis=-1))
        state, saved = layer_forward(state, mods[idx], same_seg, weights[idx])
        kept.append(saved)
    result = state.astype(BF16)

    grad_state = cotangent[0].astype(F32)
    token_hot_t = token_hot.T
    reduced, bias_sums, mod_grads = [None] * LAYERS, [None] * LAYERS, [None] * LAYERS
    for idx in reversed(range(LAYERS)):
        grad_state, token_mod, grads, bias_grads = layer_backward(
            grad_state, kept[idx], mods[idx], weights[idx]
        )
        mod_grads[idx] = jnp.dot(token_hot_t, token_mod, precision=EXACT)
        qkv_g, out_g, up_g, down_g = [item.astype(BF16) for item in grads]
        qkv_g, up_g, down_g = [
            lax.psum_scatter(item, "wide", scatter_dimension=0, tiled=True)
            for item in (qkv_g, up_g, down_g)
        ]
        out_g = lax.psum(out_g, "wide")
        qkv_g = lax.all_gather(qkv_g.reshape(depth, 3, 1, cols), "narrow", axis=2, tiled=True)
        up_g = lax.all_gather(up_g.reshape(depth, wide, 1, hidden_own), "narrow", axis=2, tiled=True)
        down_g = lax.all_gather(down_g, "narrow", axis=0, tiled=True)
        out_g = lax.all_gather(out_g, "narrow", axis=0, tiled=True)
        out_g = lax.dynamic_slice_in_dim(out_g, w * depth, depth, 0)
        reduced[idx] = (
            qkv_g.reshape(depth, 3 * width),
            out_g,
            up_g.reshape(depth, -1),
            down_g,
        )
        spot = lax.broadcasted_iota(jnp.int32, (1, narrow, 1), 1) == n
        qkv_s = jnp.where(spot, bias_grads[0].reshape(3, 1, cols), 0.0).reshape(-1)
        up_s = jnp.where(spot, bias_grads[2].reshape(wide, 1, hidden_own), 0.0).reshape(-1)
        bias_sums[idx] = [
            item.reshape(wide, -1) for item in (qkv_s, bias_grads[1], up_s, bias_grads[3])
        ]
    sizes = [item.shape[1] for item in bias_sums[0]]
    bias_sum = jnp.stack([jnp.concatenate(item, axis=1) for item in bias_sums], axis=1)
    bias_sum = lax.psum_scatter(lax.psum(bias_sum, "narrow"), "wide", scatter_dimension=0, tiled=True)[0]
    bias_out = []
    at = 0
    for size in sizes:
        bias_out.append(bias_sum[:, at : at + size])
        at += size

    mod_grad = lax.psum(jnp.stack(mod_grads), "narrow").astype(BF16)
    mod_all = lax.all_gather(mod_grad, "wide", axis=1, tiled=True)
    ada_grad = jnp.einsum("nd,lne->lde", lead_own, mod_all, preferred_element_type=F32)
    ada_size = ada_bias.shape[1]
    ada_bias_grad = jnp.sum(
        lax.dynamic_slice_in_dim(mod_all, w * ada_size, ada_size, 2).astype(F32), axis=1
    )
    lead_grad = jnp.einsum("lne,lde->nd", mod_all, ada_weight, preferred_element_type=F32)
    lead_grad = lax.all_to_all(lead_grad.reshape(wide, SEGS, depth), "wide", 0, 0, tiled=False)
    lead_grad = lead_grad.transpose(1, 0, 2).reshape(SEGS, width)
    gate = jax.nn.sigmoid(chosen)
    chosen_grad = lead_grad * (gate * (1.0 + chosen * (1.0 - gate)))
    cond_grad = jnp.dot(cond_hot.T, chosen_grad, precision=EXACT)

    stacked = [
        jnp.stack([reduced[idx][pos].astype(F32) for idx in range(LAYERS)]) for pos in range(4)
    ]
    return (
        result[None], grad_state[None], cond_grad[None],
        ada_grad, ada_bias_grad,
        stacked[0], bias_out[0], stacked[1], bias_out[1],
        stacked[2], bias_out[2], stacked[3], bias_out[3],
    )


def solution(mesh):
    matrix, vector = P(None, "wide", None), P(None, "wide")
    rows, cond_rows = P("wide", "narrow", None), P("wide", None, None)
    return jax.shard_map(
        partial(per_device, mesh.shape["wide"], mesh.shape["narrow"]),
        mesh=mesh,
        in_specs=(rows, cond_rows, P("wide", None), P("wide", None), rows) + (matrix, vector) * 5,
        out_specs=(rows, rows, cond_rows) + (matrix, vector) * 5,
        check_vma=False,
    )
```

time: 3840 us -> 1800 us (0.47)
  waiting for transfers between devices: 3160 us -> 1210 us
  matrix products: 237 us -> 153 us
    reduce_scatter x12 -> x14, waiting for transfers between devices: 1740 us -> 497 us  [the longest x6 333 us: per_device(): lax.psum_scatter(item, 'wide', scatter_dimension=0, tiled=True)]
    all_gather x18 -> x22, waiting for transfers between devices: 1320 us -> 534 us  [the longest x8 114 us: gather_tokens(): return lax.all_gather(values, 'narrow', axis=0, tiled=True)]
    unnamed x3 -> x0, blocking collectives: 122 us -> none
    all_gather x4 -> x6, blocking collectives: 40.4 us -> 142 us  [the longest x1 45.6 us: per_device(): modulation = lax.all_gather(mod_part, 'narrow', axis=2, tiled=True)]
    dot_general x46 -> x43, matrix products: 226 us -> 142 us  [the longest x24 98.4 us: dot(): lax.dot_general(left, right, (dims, ((), ())), preferred_element_type=F32)]
    psum x1, waiting for transfers between devices: 1.52 us -> 83.9 us  [per_device(): out_g = lax.psum(out_g, 'wide')]
    unnamed x325 -> x151, local copies, waits for them, and re-layouts: 96.5 us -> 17.3 us
    unnamed x47 -> x41, waiting for transfers between devices: 102 us -> 100 us
  transfers between devices with their start and end apart: 43 -> 40, of which waited for: 30 -> 34; matrix products, arithmetic and copies ran while one was open for 11% -> 16% of each run, Pallas kernels for 0% -> 0%
where the time goes in v1:
time: 1800 us; the launch traced here: 1790 us
  waiting for transfers between devices  1210 us (67%)
  blocking collectives  160 us (9%)
  local copies, waits for them, and re-layouts  159 us (9%)
  matrix products  153 us (8%)
  other arithmetic  75.7 us (4%)
    reduce_scatter x6, waiting for transfers between devices, per_device(): lax.psum_scatter(item, 'wide', scatter_dimension=0, tiled=True)  333 us
    reduce_scatter x8, waiting for transfers between devices, scatter_tokens(): lax.psum_scatter(values.astype(BF16), 'narrow', scatter_dimension=0, tile...  164 us
    all_gather x8, waiting for transfers between devices, gather_tokens(): return lax.all_gather(values, 'narrow', axis=0, tiled=True)  114 us
    all_gather x2, waiting for transfers between devices, fetch(): lax.all_gather(down_own[idx], 'wide', axis=0, tiled=True)  101 us
    unnamed x41, waiting for transfers between devices  100 us
    dot_general x24, matrix products, dot(): lax.dot_general(left, right, (dims, ((), ())), preferred_element_type=F32)  98.4 us
    all_gather x2, waiting for transfers between devices, fetch(): lax.all_gather(up_own[idx], 'wide', axis=0, tiled=True)  94 us
    all_gather x2, waiting for transfers between devices, fetch(): lax.all_gather(qkv_own[idx], 'wide', axis=0, tiled=True)  89.8 us
  transfers between devices with their start and end apart: 40, of which 34 were waited for; matrix products, arithmetic and copies ran while one was open for 16% of the time, Pallas kernels for 0%

profile of v1, /device:TPU:17, one launch (start us, length us, event | category | flops | bytes accessed | tf_op | source)
XLA Modules:
  0.0 1790.8 jit_solution(12873050438018002960)
XLA Ops:
  9.3 20.3 %all-gather.5 = bf16[8,4,1152]{2,1,0:T(4,128)(2,1)S(1)} all-gather(bf16[1,4,1152]{2,1,0:T(4,128)(2,1)S(1)} %fusion.102), channel_id=1, replica_groups=mesh['wide'=8,'narrow'=4] {'wide'}, dimensions={0}, use_global_device_ids=true | all-gather | bytes 82944 | tf_op jit(solution)/shard_map/all_gather | solution.py:166
  33.2 24.8 %all-gather.6 = bf16[8,2160,2]{1,2,0:T(2,128)(2,1)S(1)} all-gather(bf16[1,2160,2]{1,2,0:T(2,128)(2,1)S(1)} %bitcast.258), channel_id=2, replica_groups=mesh['wide'=8,'narrow'=4] {'wide'}, dimensions={0}, use_global_device_ids=true | all-gather | bytes 77760 | tf_op jit(solution)/shard_map/all_gather | solution.py:153
  65.7 47.2 %all-reduce.9.cloned.1.call-done = f32[32,2,1728]{2,0,1:T(8,128)} async-done(((f32[32,2,1728]{2,0,1:T(8,128)}), f32[32,2,1728]{2,0,1:T(8,128)}) %all-reduce.9.cloned.1.call-update) | async-done | bytes 442384
  117.3 45.6 %all_gather.88 = f32[4,2,6912]{0,1,2:T(2,128)S(1)} all-gather(f32[4,2,1728]{0,1,2:T(2,128)} %copy.96), channel_id=1, replica_groups=mesh['wide'=8,'narrow'=4] {'narrow'}, dimensions={2}, use_global_device_ids=true | all-gather | bytes 276480 | tf_op jit(solution)/shard_map/all_gather | solution.py:171
  162.9 8.6 add_bitcast_fusion
  171.5 6.4 fusion.125
  185.9 7.0 dynamic-slice_reduce_fusion.2
  202.7 45.7 %all-gather.32.cloned.1.call-done = bf16[1152,864]{1,0:T(8,128)(2,1)} async-done(((bf16[144,864]{1,0:T(8,128)(2,1)}), bf16[1152,864]{1,0:T(8,128)(2,1)}) %all-gather.32.cloned.1.call-update) | async-done | bytes 1990672 | tf_op jit(solution)/shard_map/all_gather | solution.py:186
  261.4 43.3 %all-gather.66.cloned.1.call-done = bf16[1,1152,1152]{2,1,0:T(8,128)(2,1)} async-done(((bf16[1,144,1152]{2,1,0:T(8,128)(2,1)}), bf16[1,1152,1152]{2,1,0:T(8,128)(2,1)}) %all-gather.66.cloned.1.call-update) | async-done | bytes 2654224 | tf_op jit(solution)/shard_map/all_gather | solution.py:184
  307.8 9.8 reshape.373
  317.6 10.6 dynamic-slice_reduce_fusion
  344.4 45.5 %all-gather.36.cloned.1.call-done = bf16[1152,1152]{1,0:T(8,128)(2,1)} async-done(((bf16[144,1152]{1,0:T(8,128)(2,1)}), bf16[1152,1152]{1,0:T(8,128)(2,1)}) %all-gather.36.cloned.1.call-update) | async-done | bytes 2654224 | tf_op jit(solution)/shard_map/all_gather | solution.py:190
  389.9 19.8 %all-gather.34.cloned.1.call-done = bf16[512,1152]{1,0:T(8,128)(2,1)} async-done(((bf16[128,1152]{1,0:T(8,128)(2,1)}), bf16[512,1152]{1,0:T(8,128)(2,1)}) %all-gather.34.cloned.1.call-update) | async-done | bytes 1179664 | tf_op jit(solution)/shard_map/all_gather | solution.py:38
  415.0 50.9 %all-gather.68.cloned.1.call-done = bf16[1,1,1152,1152]{3,2,1,0:T(8,128)(2,1)} async-done(((bf16[1,1,144,1152]{3,2,1,0:T(8,128)(2,1)}), bf16[1,1,1152,1152]{3,2,1,0:T(8,128)(2,1)}) %all-gather.68.cloned.1.call-update) | async-done | bytes 2654224 | tf_op jit(solution)/shard_map/all_gather | solution.py:192
  480.4 16.9 reduce-scatter.18.cloned.1.call-done
  504.2 44.1 %all-gather.40.cloned.1.call-done = bf16[1152,864]{1,0:T(8,128)(2,1)} async-done(((bf16[144,864]{1,0:T(8,128)(2,1)}), bf16[1152,864]{1,0:T(8,128)(2,1)}) %all-gather.40.cloned.1.call-update) | async-done | bytes 1990672 | tf_op jit(solution)/shard_map/all_gather | solution.py:186
  548.3 19.7 %all-gather.38.cloned.1.call-done = bf16[512,1152]{1,0:T(8,128)(2,1)} async-done(((bf16[128,1152]{1,0:T(8,128)(2,1)}), bf16[512,1152]{1,0:T(8,128)(2,1)}) %all-gather.38.cloned.1.call-update) | async-done | bytes 1179664 | tf_op jit(solution)/shard_map/all_gather | solution.py:38
  581.3 42.4 %all-gather.70.cloned.1.call-done = bf16[1,1152,1152]{2,1,0:T(8,128)(2,1)} async-done(((bf16[1,144,1152]{2,1,0:T(8,128)(2,1)}), bf16[1,1152,1152]{2,1,0:T(8,128)(2,1)}) %all-gather.70.cloned.1.call-update) | async-done | bytes 2654224 | tf_op jit(solution)/shard_map/all_gather | solution.py:184
  630.7 21.7 %reduce-scatter.20.cloned.1.call-done = bf16[128,1152]{1,0:T(8,128)(2,1)} async-done(((bf16[512,1152]{1,0:T(8,128)(2,1)}), bf16[128,1152]{1,0:T(8,128)(2,1)}) %reduce-scatter.20.cloned.1.call-update) | async-done | bytes 294928 | tf_op jit(solution)/shard_map/reduce_scatter | solution.py:42
  660.5 48.4 %all-gather.44.cloned.1.call-done = bf16[1152,1152]{1,0:T(8,128)(2,1)} async-done(((bf16[144,1152]{1,0:T(8,128)(2,1)}), bf16[1152,1152]{1,0:T(8,128)(2,1)}) %all-gather.44.cloned.1.call-update) | async-done | bytes 2654224 | tf_op jit(solution)/shard_map/all_gather | solution.py:190
  708.9 19.7 %all-gather.42.cloned.1.call-done = bf16[512,1152]{1,0:T(8,128)(2,1)} async-done(((bf16[128,1152]{1,0:T(8,128)(2,1)}), bf16[512,1152]{1,0:T(8,128)(2,1)}) %all-gather.42.cloned.1.call-update) | async-done | bytes 1179664 | tf_op jit(solution)/shard_map/all_gather | solution.py:38
  733.9 50.2 %all-gather.72.cloned.1.call-done = bf16[1,1,1152,1152]{3,2,1,0:T(8,128)(2,1)} async-done(((bf16[1,1,144,1152]{3,2,1,0:T(8,128)(2,1)}), bf16[1,1,1152,1152]{3,2,1,0:T(8,128)(2,1)}) %all-gather.72.cloned.1.call-update) | async-done | bytes 2654224 | tf_op jit(solution)/shard_map/all_gather | solution.py:192
  784.0 19.7 %all-gather.46.cloned.1.call-done = bf16[512,1152]{1,0:T(8,128)(2,1)} async-done(((bf16[128,1152]{1,0:T(8,128)(2,1)}), bf16[512,1152]{1,0:T(8,128)(2,1)}) %all-gather.46.cloned.1.call-update) | async-done | bytes 1179664 | tf_op jit(solution)/shard_map/all_gather | solution.py:38
  803.7 6.2 convert_reduce_fusion
  821.0 18.3 %reduce-scatter.24.cloned.1.call-done = bf16[128,1152]{1,0:T(8,128)(2,1)} async-done(((bf16[512,1152]{1,0:T(8,128)(2,1)}), bf16[128,1152]{1,0:T(8,128)(2,1)}) %reduce-scatter.24.cloned.1.call-update) | async-done | bytes 294928 | tf_op jit(solution)/shard_map/reduce_scatter | solution.py:42
  841.9 26.5 %reduce-scatter.22.cloned.1.call-done = bf16[128,1152]{1,0:T(8,128)(2,1)} async-done(((bf16[512,1152]{1,0:T(8,128)(2,1)}), bf16[128,1152]{1,0:T(8,128)(2,1)}) %reduce-scatter.22.cloned.1.call-update) | async-done | bytes 294928 | tf_op jit(solution)/shard_map/reduce_scatter | solution.py:42
  872.7 17.5 all-gather.48.cloned.1.call-done
  903.1 25.4 %reduce-scatter.26.cloned.1.call-done = bf16[128,1152]{1,0:T(8,128)(2,1)} async-done(((bf16[512,1152]{1,0:T(8,128)(2,1)}), bf16[128,1152]{1,0:T(8,128)(2,1)}) %reduce-scatter.26.cloned.1.call-update) | async-done | bytes 294928 | tf_op jit(solution)/shard_map/reduce_scatter | solution.py:42
  935.1 18.0 %all-gather.50.cloned.1.call-done = bf16[512,1152]{1,0:T(8,128)(2,1)} async-done(((bf16[128,1152]{1,0:T(8,128)(2,1)}), bf16[512,1152]{1,0:T(8,128)(2,1)}) %all-gather.50.cloned.1.call-update) | async-done | bytes 1179664 | tf_op jit(solution)/shard_map/all_gather | solution.py:38
  953.0 6.2 convert_reduce_fusion.1
  963.2 25.4 %reduce-scatter.28.cloned.1.call-done = bf16[128,1152]{1,0:T(8,128)(2,1)} async-done(((bf16[512,1152]{1,0:T(8,128)(2,1)}), bf16[128,1152]{1,0:T(8,128)(2,1)}) %reduce-scatter.28.cloned.1.call-update) | async-done | bytes 294928 | tf_op jit(solution)/shard_map/reduce_scatter | solution.py:42
  1019.9 63.7 %reduce-scatter.38.cloned.1.call-done = bf16[144,1152]{1,0:T(8,128)(2,1)} async-done(((bf16[1152,1152]{1,0:T(8,128)(2,1)}), bf16[144,1152]{1,0:T(8,128)(2,1)}) %reduce-scatter.38.cloned.1.call-update) | async-done | bytes 331792 | tf_op jit(solution)/shard_map/reduce_scatter | solution.py:216
  1139.4 18.6 %reduce-scatter.36.cloned.1.call-done = bf16[144,1152]{1,0:T(8,128)(2,1)} async-done(((bf16[1152,1152]{1,0:T(8,128)(2,1)}), bf16[144,1152]{1,0:T(8,128)(2,1)}) %reduce-scatter.36.cloned.1.call-update) | async-done | bytes 331792 | tf_op jit(solution)/shard_map/reduce_scatter | solution.py:216
  1160.7 70.3 %reduce-scatter.42.cloned.1.call-done = bf16[144,1152]{1,0:T(8,128)(2,1)} async-done(((bf16[1152,1152]{1,0:T(8,128)(2,1)}), bf16[144,1152]{1,0:T(8,128)(2,1)}) %reduce-scatter.42.cloned.1.call-update) | async-done | bytes 331792 | tf_op jit(solution)/shard_map/reduce_scatter | solution.py:216
  1231.0 73.6 %reduce-scatter.40.cloned.1.call-done = bf16[144,1152]{1,0:T(8,128)(2,1)} async-done(((bf16[1152,1152]{1,0:T(8,128)(2,1)}), bf16[144,1152]{1,0:T(8,128)(2,1)}) %reduce-scatter.40.cloned.1.call-update) | async-done | bytes 331792 | tf_op jit(solution)/shard_map/reduce_scatter | solution.py:216
  1309.0 83.9 %all-reduce.13.cloned.1.call-done = (bf16[288,1152]{1,0:T(8,128)(2,1)}, bf16[288,1152]{1,0:T(8,128)(2,1)}) async-done(((bf16[288,1152]{1,0:T(8,128)(2,1)}, bf16[288,1152]{1,0:T(8,128)(2,1)}), (bf16[288,1152]{1,0:T(8,128)(2,1)}, bf16[288,1152]{1,0:T(8,128)(2,1)})) %all-reduce.13.cloned.1.call-update) | async-done | bytes 1327120 | tf_op jit(solution)/shard_map/psum | solution.py:219
  1403.3 15.5 all-gather.60.cloned.1.call-done
  1430.5 56.8 %reduce-scatter.34.cloned.1.call-done = bf16[144,864]{1,0:T(8,128)(2,1)} async-done(((bf16[1152,864]{1,0:T(8,128)(2,1)}), bf16[144,864]{1,0:T(8,128)(2,1)}) %reduce-scatter.34.cloned.1.call-update) | async-done | bytes 248848 | tf_op jit(solution)/shard_map/reduce_scatter | solution.py:216
  1490.6 13.5 all_gather.109
  1508.6 50.7 %all-reduce.11.cloned.1.call-done = f32[8,2,1296]{2,1,0:T(2,128)} async-done(((f32[8,2,1296]{2,1,0:T(2,128)}), f32[8,2,1296]{2,1,0:T(2,128)}) %all-reduce.11.cloned.1.call-update) | async-done | bytes 82960
  1561.3 28.3 %reduce-scatter.30.cloned.1.call-done = bf16[128,1152]{1,0:T(8,128)(2,1)} async-done(((bf16[512,1152]{1,0:T(8,128)(2,1)}), bf16[128,1152]{1,0:T(8,128)(2,1)}) %reduce-scatter.30.cloned.1.call-update) | async-done | bytes 294928 | tf_op jit(solution)/shard_map/reduce_scatter | solution.py:42
  1595.4 17.5 all-reduce.14
  1613.0 23.2 %all_gather.107 = bf16[2,32,6912]{2,0,1:T(2,128)(2,1)S(1)} all-gather(bf16[2,4,6912]{2,0,1:T(2,128)(2,1)S(1)} %copy.109), channel_id=1, replica_groups=mesh['wide'=8,'narrow'=4] {'wide'}, dimensions={1}, use_global_device_ids=true | all-gather | bytes 995328 | tf_op jit(solution)/shard_map/all_gather | solution.py:247
  1640.4 9.3 all-to-all-start
  1675.1 50.0 %reduce-scatter.32.cloned.1.call-done = bf16[144,864]{1,0:T(8,128)(2,1)} async-done(((bf16[1152,864]{1,0:T(8,128)(2,1)}), bf16[144,864]{1,0:T(8,128)(2,1)}) %reduce-scatter.32.cloned.1.call-update) | async-done | bytes 248848 | tf_op jit(solution)/shard_map/reduce_scatter | solution.py:216
  1726.8 14.7 all_gather.108
  1747.1 7.9 all-gather.54.cloned.1.call-done
  1756.1 25.6 %all-gather.56.cloned.1.call-done = bf16[1152,1152]{1,0:T(8,128)(2,1)} async-done(((bf16[288,1152]{1,0:T(8,128)(2,1)}), bf16[1152,1152]{1,0:T(8,128)(2,1)}) %all-gather.56.cloned.1.call-update) | async-done | bytes 2654224 | tf_op jit(solution)/shard_map/all_gather | solution.py:223
  (414 shorter events, 339.4 us)
Async XLA Ops:
  7.2 105.7 %all-reduce.9.cloned.1.call-start = ((), (), s32[]{:S(2)}) async-start(), calls=%async_computation.51 | async-start | bytes 917504
  32.3 30.9 %copy-start.70 = (u32[32]{0:T(128)S(1)}, u32[32]{0:T(128)}, u32[]{:S(2)}) copy-start(u32[32]{0:T(128)} %constant.103) | copy-start | bytes 388
  32.3 32.1 %copy-start.53 = (s32[1,512]{1,0:T(1,128)S(1)}, s32[1,512]{1,0:T(1,128)}, u32[]{:S(2)}) copy-start(s32[1,512]{1,0:T(1,128)} %param.17) | copy-start | bytes 6148
  32.3 170.4 %all-gather.30.cloned.1.call-start = ((), (), s32[]{:S(2)}) async-start(), calls=%async_computation.15 | async-start | bytes 1474560 | tf_op jit(solution)/shard_map/all_gather | solution.py:38
  63.2 116.9 %copy-start.60 = (f32[128]{0:T(128)}, f32[128]{0:T(128)S(1)}, u32[]{:S(2)}) copy-start(f32[128]{0:T(128)S(1)} %broadcast_multiply_fusion.11) | copy-start | bytes 1540
  64.5 113.5 %copy-start.54 = (s32[128]{0:T(128)}, s32[128]{0:T(128)S(1)}, u32[]{:S(2)}) copy-start(s32[128]{0:T(128)S(1)} %fusion.114) | copy-start | bytes 1540
  65.7 114.4 %copy-start.63 = (f32[128]{0:T(128)}, f32[128]{0:T(128)S(1)}, u32[]{:S(2)}) copy-start(f32[128]{0:T(128)S(1)} %add_rsqrt_fusion.3) | copy-start | bytes 1540
  181.1 67.3 %all-gather.32.cloned.1.call-start = ((), (), s32[]{:S(2)}) async-start(), calls=%async_computation.16 | async-start | bytes 2322432 | tf_op jit(solution)/shard_map/all_gather | solution.py:186
  194.9 109.8 %all-gather.66.cloned.1.call-start = ((), (), s32[]{:S(2)}) async-start(), calls=%async_computation.47 | async-start | bytes 2985984 | tf_op jit(solution)/shard_map/all_gather | solution.py:184
  197.4 136.0 %reduce-scatter.16.cloned.1.call-start = ((), (), s32[]{:S(2)}) async-start(), calls=%async_computation.17 | async-start | bytes 1474560 | tf_op jit(solution)/shard_map/reduce_scatter | solution.py:42
  307.8 82.1 %all-gather.36.cloned.1.call-start = ((), (), s32[]{:S(2)}) async-start(), calls=%async_computation.19 | async-start | bytes 2985984 | tf_op jit(solution)/shard_map/all_gather | solution.py:190
  330.6 79.1 %all-gather.34.cloned.1.call-start = ((), (), s32[]{:S(2)}) async-start(), calls=%async_computation.18 | async-start | bytes 1474560 | tf_op jit(solution)/shard_map/all_gather | solution.py:38
  337.1 128.8 %all-gather.68.cloned.1.call-start = ((), (), s32[]{:S(2)}) async-start(), calls=%async_computation.48 | async-start | bytes 2985984 | tf_op jit(solution)/shard_map/all_gather | solution.py:192
  339.1 158.2 %reduce-scatter.18.cloned.1.call-start = ((), (), s32[]{:S(2)}) async-start(), calls=%async_computation.20 | async-start | bytes 1474560 | tf_op jit(solution)/shard_map/reduce_scatter | solution.py:42
  471.6 76.7 %all-gather.40.cloned.1.call-start = ((), (), s32[]{:S(2)}) async-start(), calls=%async_computation.22 | async-start | bytes 2322432 | tf_op jit(solution)/shard_map/all_gather | solution.py:186
  473.7 94.2 %all-gather.38.cloned.1.call-start = ((), (), s32[]{:S(2)}) async-start(), calls=%async_computation.21 | async-start | bytes 1474560 | tf_op jit(solution)/shard_map/all_gather | solution.py:38
  502.2 121.4 %all-gather.70.cloned.1.call-start = ((), (), s32[]{:S(2)}) async-start(), calls=%async_computation.49 | async-start | bytes 2985984 | tf_op jit(solution)/shard_map/all_gather | solution.py:184
  502.8 149.7 %reduce-scatter.20.cloned.1.call-start = ((), (), s32[]{:S(2)}) async-start(), calls=%async_computation.23 | async-start | bytes 1474560 | tf_op jit(solution)/shard_map/reduce_scatter | solution.py:42
  626.7 82.2 %all-gather.44.cloned.1.call-start = ((), (), s32[]{:S(2)}) async-start(), calls=%async_computation.25 | async-start | bytes 2985984 | tf_op jit(solution)/shard_map/all_gather | solution.py:190
  629.1 99.4 %all-gather.42.cloned.1.call-start = ((), (), s32[]{:S(2)}) async-start(), calls=%async_computation.24 | async-start | bytes 1474560 | tf_op jit(solution)/shard_map/all_gather | solution.py:38
  657.9 126.2 %all-gather.72.cloned.1.call-start = ((), (), s32[]{:S(2)}) async-start(), calls=%async_computation.50 | async-start | bytes 2985984 | tf_op jit(solution)/shard_map/all_gather | solution.py:192
  658.5 145.2 %all-gather.46.cloned.1.call-start = ((), (), s32[]{:S(2)}) async-start(), calls=%async_computation.27 | async-start | bytes 1474560 | tf_op jit(solution)/shard_map/all_gather | solution.py:38
  659.0 180.2 %reduce-scatter.24.cloned.1.call-start = ((), (), s32[]{:S(2)}) async-start(), calls=%async_computation.28 | async-start | bytes 1474560 | tf_op jit(solution)/shard_map/reduce_scatter | solution.py:42
  813.8 54.5 %reduce-scatter.22.cloned.1.call-start = ((), (), s32[]{:S(2)}) async-start(), calls=%async_computation.26 | async-start | bytes 1474560 | tf_op jit(solution)/shard_map/reduce_scatter | solution.py:42
  819.5 70.7 %all-gather.48.cloned.1.call-start = ((), (), s32[]{:S(2)}) async-start(), calls=%async_computation.29 | async-start | bytes 1474560 | tf_op jit(solution)/shard_map/all_gather | solution.py:38
  872.2 56.3 %reduce-scatter.26.cloned.1.call-start = ((), (), s32[]{:S(2)}) async-start(), calls=%async_computation.30 | async-start | bytes 1474560 | tf_op jit(solution)/shard_map/reduce_scatter | solution.py:42
  903.0 50.0 %all-gather.50.cloned.1.call-start = ((), (), s32[]{:S(2)}) async-start(), calls=%async_computation.31 | async-start | bytes 1474560 | tf_op jit(solution)/shard_map/all_gather | solution.py:38
  935.0 53.6 %reduce-scatter.28.cloned.1.call-start = ((), (), s32[]{:S(2)}) async-start(), calls=%async_computation.32 | async-start | bytes 1474560 | tf_op jit(solution)/shard_map/reduce_scatter | solution.py:42
  963.2 53.9 %all-gather.52.cloned.1.call-start = ((), (), s32[]{:S(2)}) async-start(), calls=%async_computation.33 | async-start | bytes 1474560 | tf_op jit(solution)/shard_map/all_gather | solution.py:38
  993.2 90.4 %reduce-scatter.38.cloned.1.call-start = ((), (), s32[]{:S(2)}) async-start(), calls=%async_computation.41 | async-start | bytes 2985984 | tf_op jit(solution)/shard_map/reduce_scatter | solution.py:216
  998.1 159.9 %reduce-scatter.36.cloned.1.call-start = ((), (), s32[]{:S(2)}) async-start(), calls=%async_computation.39 | async-start | bytes 2985984 | tf_op jit(solution)/shard_map/reduce_scatter | solution.py:216
  1003.3 227.7 %reduce-scatter.42.cloned.1.call-start = ((), (), s32[]{:S(2)}) async-start(), calls=%async_computation.45 | async-start | bytes 2985984 | tf_op jit(solution)/shard_map/reduce_scatter | solution.py:216
  1008.7 295.9 %reduce-scatter.40.cloned.1.call-start = ((), (), s32[]{:S(2)}) async-start(), calls=%async_computation.43 | async-start | bytes 2985984 | tf_op jit(solution)/shard_map/reduce_scatter | solution.py:216
  1014.3 378.6 %all-reduce.13.cloned.1.call-start = ((), (), s32[]{:S(2)}) async-start(), calls=%async_computation.53 | async-start | bytes 2654208 | tf_op jit(solution)/shard_map/psum | solution.py:219
  1019.9 399.0 %all-gather.60.cloned.1.call-start = ((), (), s32[]{:S(2)}) async-start(), calls=%async_computation.42 | async-start | bytes 2949120 | tf_op jit(solution)/shard_map/all_gather | solution.py:221
  1086.2 401.1 %reduce-scatter.34.cloned.1.call-start = ((), (), s32[]{:S(2)}) async-start(), calls=%async_computation.36 | async-start | bytes 2322432 | tf_op jit(solution)/shard_map/reduce_scatter | solution.py:216
  1090.5 468.8 %all-reduce.11.cloned.1.call-start = ((), (), s32[]{:S(2)}) async-start(), calls=%async_computation.52 | async-start | bytes 180224
  1134.9 454.7 %reduce-scatter.30.cloned.1.call-start = ((), (), s32[]{:S(2)}) async-start(), calls=%async_computation.34 | async-start | bytes 1474560 | tf_op jit(solution)/shard_map/reduce_scatter | solution.py:42
  1139.4 519.3 %all-gather.58.cloned.1.call-start = ((), (), s32[]{:S(2)}) async-start(), calls=%async_computation.40 | async-start | bytes 2949120 | tf_op jit(solution)/shard_map/all_gather | solution.py:221
  1160.7 507.0 %all-gather.64.cloned.1.call-start = ((), (), s32[]{:S(2)}) async-start(), calls=%async_computation.46 | async-start | bytes 1658880 | tf_op jit(solution)/shard_map/all_gather | solution.py:222
  1231.0 436.6 %all-gather.62.cloned.1.call-start = ((), (), s32[]{:S(2)}) async-start(), calls=%async_computation.44 | async-start | bytes 1658880 | tf_op jit(solution)/shard_map/all_gather | solution.py:222
  1304.6 420.5 %reduce-scatter.32.cloned.1.call-start = ((), (), s32[]{:S(2)}) async-start(), calls=%async_computation.35 | async-start | bytes 2322432 | tf_op jit(solution)/shard_map/reduce_scatter | solution.py:216
  1308.9 446.1 %all-gather.54.cloned.1.call-start = ((), (), s32[]{:S(2)}) async-start(), calls=%async_computation.37 | async-start | bytes 3317760 | tf_op jit(solution)/shard_map/all_gather | solution.py:223
  1392.9 388.7 %all-gather.56.cloned.1.call-start = ((), (), s32[]{:S(2)}) async-start(), calls=%async_computation.38 | async-start | bytes 3317760 | tf_op jit(solution)/shard_map/all_gather | solution.py:223
  1640.4 17.3 all-to-all-start
  1649.6 8.2 copy-start.43
  1649.6 8.2 copy-start.69
  1743.7 40.1 %copy-start.1 = (bf16[1,4,1152]{2,1,0:T(4,128)(2,1)S(1)}, bf16[1,4,1152]{2,1,0:T(4,128)(2,1)}, u32[]{:S(2)}) copy-start(bf16[1,4,1152]{2,1,0:T(4,128)(2,1)} %param.16) | copy-start | bytes 27652
  (65 other events, 151.8 us)
Sparse Core Ops, SparseCore 0:
  32.4 80.4 all-reduce.8
  181.3 16.6 all-gather.29
  200.9 47.5 all-gather.31
  251.3 53.3 all-gather.65
  307.9 25.5 reduce-scatter.15
  336.0 53.8 all-gather.35
  392.0 17.6 all-gather.33
  412.4 53.4 all-gather.67
  471.7 25.5 reduce-scatter.17
  500.1 48.0 all-gather.39
  550.5 17.3 all-gather.37
  570.2 53.4 all-gather.69
  626.9 25.4 reduce-scatter.19
  655.0 53.8 all-gather.43
  710.9 17.6 all-gather.41
  730.6 53.4 all-gather.71
  786.0 17.6 all-gather.45
  813.9 25.2 reduce-scatter.23
  842.6 25.7 reduce-scatter.21
  872.4 17.8 all-gather.47
  903.2 25.3 reduce-scatter.25
  935.2 17.8 all-gather.49
  963.3 25.3 reduce-scatter.27
  993.3 17.8 all-gather.51
  1015.4 68.1 reduce-scatter.37
  1088.2 69.8 reduce-scatter.35
  1161.5 69.3 reduce-scatter.41
  1235.0 69.5 reduce-scatter.39
  1308.8 84.0 all-reduce.12
  1394.4 24.4 all-gather.59
  1423.4 63.9 reduce-scatter.33
  1491.1 68.1 all-reduce.10
  1561.9 27.6 reduce-scatter.29
  1591.1 27.3 all-gather.57
  1620.1 18.2 all-gather.63
  1639.8 18.3 all-gather.61
  1661.6 63.5 reduce-scatter.31
  1726.7 28.3 all-gather.53
  1756.5 25.0 all-gather.55

commit v2 on v1

--- a/solution.py
+++ b/solution.py
@@ -1,9 +1,12 @@
 from functools import partial
 import math
+from types import SimpleNamespace
 
 import jax
 import jax.numpy as jnp
 from jax import lax
+from jax.experimental import pallas as pl
+from jax.experimental.pallas import tpu as pltpu
 from jax.sharding import PartitionSpec as P
 
 HEADS = 16
@@ -131,7 +134,7 @@
     return grad_state, token_mod, (grad_qkv_w, grad_out_w, grad_up_w, grad_down_w), bias_grads
 
 
-def per_device(
+def plain_device(
     wide, narrow,
     tokens, cond, seg_ids, cond_index, cotangent,
     ada_weight, ada_bias, qkv_weight, qkv_bias, out_weight, out_bias,
@@ -268,11 +271,1151 @@
     )
 
 
+QKV, OUT, UP, DOWN = range(4)
+PLANES = 4
+PAIR = 2
+LANES = 128
+STEP = 32
+MESH = pl.DeviceIdType.MESH
+
+
+def mod_start(tiles, parts, part):
+    return tiles * part // parts
+
+
+def block_kernel(cfg, *refs):
+    r = SimpleNamespace(**dict(zip(cfg.names, refs)))
+    wide, narrow, width, depth = cfg.wide, cfg.narrow, cfg.width, cfg.depth
+    local, cols, mod_cols, tiles = cfg.local, cfg.cols, cfg.mod_cols, cfg.tiles
+    half = local // 2
+    own_heads = cols // HEAD
+    scale_inv = 1.0 / math.sqrt(HEAD)
+    w = lax.axis_index("wide")
+    n = lax.axis_index("narrow")
+    z, x = w // PAIR, w % PAIR
+    y, c = n // 2, n % 2
+    n_core = n + 1 - 2 * c
+    n_side = n + 2 - 4 * y
+    n_far = 3 - n
+    core, side, far = (w, n_core), (w, n_side), (w, n_far)
+    beside = (w + 1 - 2 * x, n)
+
+    def plane_of(j):
+        return (z + j) % PLANES
+
+    def plane(j):
+        return (plane_of(j) * PAIR + x, n)
+
+    def wide_peer(j):
+        return ((w + j) % wide, n)
+
+    def remote(src, dst, sems, device):
+        return pltpu.make_async_remote_copy(
+            src_ref=src, dst_ref=dst, send_sem=sems[0], recv_sem=sems[1],
+            device_id=device, device_id_type=MESH,
+        )
+
+    def span(start, size, step=16):
+        return pl.ds(pl.multiple_of(start, step), size)
+
+    barrier = pltpu.get_barrier_semaphore()
+    partners = [core, side, far] + [wide_peer(j) for j in range(1, wide)]
+    for partner in partners:
+        pl.semaphore_signal(barrier, inc=1, device_id=partner, device_id_type=MESH)
+    pl.semaphore_wait(barrier, len(partners))
+
+    shards = (r.qkv_s, r.out_s, r.up_s, r.down_s)
+    full = (r.qkv_h, r.out_h, r.up_h, r.down_h)
+    loaded = (r.qkv_v, r.out_v, r.up_v, r.down_v)
+
+    def w_rows(which, plane_idx, col):
+        if which == OUT:
+            return span(col * depth, depth)
+        return span((plane_idx * PAIR + col) * depth, depth)
+
+    def w_block(which, layer, plane_idx, col):
+        return full[which].at[layer, w_rows(which, plane_idx, col)]
+
+    def w_z(which, layer, j):
+        slot = layer * 4 + which
+        k = 0 if which == OUT else j - 1
+        return remote(
+            shards[which].at[layer], w_block(which, layer, z, x),
+            (r.wz_s.at[slot, j - 1], r.wz_r.at[slot, k]), plane(j),
+        )
+
+    def w_z_in(which, layer, j):
+        slot = layer * 4 + which
+        src_plane = n if which == OUT else (z - j + PLANES) % PLANES
+        k = 0 if which == OUT else j - 1
+        block = w_block(which, layer, src_plane, x)
+        return remote(block, block, (r.wz_s.at[slot, k], r.wz_r.at[slot, k]), plane(j)), src_plane
+
+    def w_x(which, layer, j, src, plane_idx, col):
+        slot = layer * 4 + which
+        return remote(
+            src, w_block(which, layer, plane_idx, col),
+            (r.wx_s.at[slot, j], r.wx_r.at[slot, j]), beside,
+        )
+
+    def w_own(which, layer):
+        return pltpu.make_async_copy(
+            shards[which].at[layer], w_block(which, layer, z, x), r.w_own.at[layer * 4 + which]
+        )
+
+    def weights_start(which, layer):
+        def go():
+            w_own(which, layer).start()
+            for j in range(1, PLANES):
+                w_z(which, layer, j).start()
+
+        if which == OUT:
+            pl.when(z == n)(go)
+        else:
+            go()
+
+    def weights_forward(which, layer):
+        def own():
+            w_x(which, layer, 0, shards[which].at[layer], z, x).start()
+
+        def passed(j):
+            arrived, src_plane = w_z_in(which, layer, j)
+            arrived.wait_recv()
+            k = 0 if which == OUT else j
+            w_x(which, layer, k, w_block(which, layer, src_plane, x), src_plane, x).start()
+
+        if which == OUT:
+            pl.when(z == n)(own)
+            pl.when(z != n)(lambda: passed(1))
+        else:
+            own()
+            for j in range(1, PLANES):
+                passed(j)
+
+    def weights_finish(which, layer):
+        if which == OUT:
+            block = w_block(which, layer, n, 1 - x)
+            w_x(which, layer, 0, block, n, 1 - x).wait_recv()
+            pl.when(z == n)(lambda: w_own(which, layer).wait())
+        else:
+            for j in range(PLANES):
+                src_plane = (z - j + PLANES) % PLANES
+                block = w_block(which, layer, src_plane, 1 - x)
+                w_x(which, layer, j, block, src_plane, 1 - x).wait_recv()
+            w_own(which, layer).wait()
+
+    def weights_drain(which, layer):
+        if which == OUT:
+            w_x(which, layer, 0, shards[which].at[layer], z, x).wait_send()
+
+            @pl.when(z == n)
+            def _():
+                for j in range(1, PLANES):
+                    w_z(which, layer, j).wait_send()
+        else:
+            for j in range(PLANES):
+                w_x(which, layer, j, shards[which].at[layer], z, x).wait_send()
+            for j in range(1, PLANES):
+                w_z(which, layer, j).wait_send()
+
+    def load(which, layer):
+        return pltpu.make_async_copy(full[which].at[layer], loaded[which], r.load_sem.at[which])
+
+    def weights_ready(which, layer):
+        weights_finish(which, layer)
+        load(which, layer).start()
+        load(which, layer).wait()
+
+    def tok_rows(chunk, part):
+        return span(local * chunk + half * part, half)
+
+    def tok_copy(ref, kind, part, incoming=False):
+        chunk = ((n_core, n_side, n_far) if incoming else (n, n, n_side))[kind]
+        rows = ref.at[tok_rows(chunk, part)]
+        k = 2 * kind + part
+        return remote(rows, rows, (r.tok_s.at[k], r.tok_r.at[k]), side if kind == 1 else core)
+
+    def tok_send(ref, part):
+        tok_copy(ref, 1, part).start()
+        tok_copy(ref, 0, part).start()
+
+    def tok_own(ref):
+        for part in range(2):
+            tok_copy(ref, 0, part, True).wait_recv()
+
+    def tok_other(ref):
+        for part in range(2):
+            tok_copy(ref, 1, part, True).wait_recv()
+            tok_copy(ref, 2, part).start()
+        for part in range(2):
+            tok_copy(ref, 2, part, True).wait_recv()
+
+    def tok_drain(ref):
+        for kind in range(3):
+            for part in range(2):
+                tok_copy(ref, kind, part).wait_send()
+
+    def block_rows(block):
+        return span(2 * local * (y if block else 1 - y), 2 * local)
+
+    def sum_core(block):
+        return remote(
+            r.core_tx.at[block], r.core_rx.at[block], (r.sum_s.at[block], r.sum_r.at[block]), core
+        )
+
+    def sum_side(part):
+        rows = span(half * part, half)
+        return remote(
+            r.side_tx.at[rows], r.side_rx.at[rows], (r.sum_s.at[2 + part], r.sum_r.at[2 + part]), side
+        )
+
+    def sum_block(block):
+        r.core_tx[block] = r.part[block, span(local * (1 - c), local), :].astype(BF16)
+        sum_core(block).start()
+
+    def sum_cross():
+        sum_core(0).wait_recv()
+        for part in range(2):
+            rows = span(half * part, half)
+            mine = r.part[0, span(local * c + half * part, half), :]
+            r.side_tx[rows, :] = (mine + r.core_rx[0, rows, :].astype(F32)).astype(BF16)
+            sum_side(part).start()
+
+    def sum_wait(part):
+        if part == 0:
+            sum_core(1).wait_recv()
+        sum_side(part).wait_recv()
+        if part == 1:
+            for block in range(2):
+                sum_core(block).wait_send()
+                sum_side(block).wait_send()
+
+    def sum_take(start):
+        rows = span(start, STEP)
+        return (
+            r.part[1, span(local * c + start, STEP), :]
+            + r.core_rx[1, rows, :].astype(F32)
+            + r.side_rx[rows, :].astype(F32)
+        )
+
+    def each_step(part, body):
+        @pl.loop(0, half // STEP)
+        def _(i):
+            body(half * part + STEP * i)
+
+    def seg_of(start):
+        return r.seg_own[span(start, STEP), :]
+
+    def mod(layer, block, seg):
+        rows = r.mods[SEGS * layer : SEGS * layer + SEGS, width * block : width * (block + 1)]
+        out = rows[SEGS - 1 : SEGS]
+        for s in range(SEGS - 1):
+            out = jnp.where(seg == s, rows[s : s + 1], out)
+        return out
+
+    def mod_sum(layer, block, seg, values):
+        sums = [jnp.sum(jnp.where(seg == s, values, 0.0), 0, keepdims=True) for s in range(SEGS)]
+        at = (slice(SEGS * layer, SEGS * layer + SEGS), slice(width * block, width * (block + 1)))
+        r.mod_grad[at] += jnp.concatenate(sums, 0)
+
+    def lead_copy(j, incoming=False):
+        return remote(
+            r.lead.at[(w + j) % wide], r.lead_rx.at[(w - j + wide) % wide if incoming else w],
+            (r.lead_sem_s.at[j - 1], r.lead_sem_r.at[j - 1]), wide_peer(j),
+        )
+
+    def bias_copy(j, incoming=False):
+        return remote(
+            r.bias, r.bias_rx.at[(w - j + wide) % wide if incoming else w],
+            (r.bias_sem_s.at[j - 1], r.bias_sem_r.at[j - 1]), wide_peer(j),
+        )
+
+    def mod_copy(j, incoming=False):
+        return remote(
+            r.mod_tx.at[(w + j) % wide], r.mod_rx.at[(w - j + wide) % wide if incoming else w],
+            (r.mod_sem_s.at[j - 1], r.mod_sem_r.at[j - 1]), wide_peer(j),
+        )
+
+    narrow_peers = ((core, n_core), (side, n_side), (far, n_far))
+
+    def quarter_copy(k, incoming=False):
+        device, idx = narrow_peers[k]
+        return remote(
+            r.mod_q.at[n], r.mod_q.at[idx if incoming else n],
+            (r.quarter_s.at[k], r.quarter_r.at[k]), device,
+        )
+
+    ada_load = pltpu.make_async_copy(
+        r.ada.at[:, :, span(LANES * mod_start(tiles, narrow, n), mod_cols, LANES)], r.ada_v, r.ada_sem
+    )
+    ada_load.start()
+    for j in range(1, wide):
+        lead_copy(j).start()
+    weights_start(QKV, 0)
+    for j in range(1, wide):
+        bias_copy(j).start()
+    r.lead_rx[pl.ds(w, 1)] = r.lead[pl.ds(w, 1)]
+    r.bias_rx[pl.ds(w, 1)] = r.bias[...][None]
+    r.mod_grad[...] = jnp.zeros_like(r.mod_grad)
+    ada_load.wait()
+    for j in range(1, wide):
+        lead_copy(j, True).wait_recv()
+    lead_all = r.lead_rx[...].reshape(wide * 16, depth)
+    for layer in range(LAYERS):
+        product = dot(lead_all, r.ada_v[layer], ((1,), (0,)))
+        at = slice(SEGS * layer, SEGS * layer + SEGS)
+        for row in range(wide):
+            r.mod_tx[row, at, :] = product[16 * row : 16 * row + SEGS] + r.ada_bias[at, :]
+    for j in range(1, wide):
+        mod_copy(j).start()
+    r.mod_rx[pl.ds(w, 1)] = r.mod_tx[pl.ds(w, 1)]
+    for layer in range(LAYERS):
+        for which in (QKV, OUT, UP, DOWN):
+            if (which, layer) != (QKV, 0):
+                weights_start(which, layer)
+    weights_forward(QKV, 0)
+    for j in range(1, wide):
+        mod_copy(j, True).wait_recv()
+    r.mod_q[pl.ds(n, 1)] = jnp.sum(r.mod_rx[...], 0, keepdims=True)
+    for k in range(3):
+        quarter_copy(k).start()
+    weights_forward(OUT, 0)
+    for j in range(1, wide):
+        bias_copy(j, True).wait_recv()
+    r.bias_sum[...] = jnp.sum(r.bias_rx[...], 0)
+    for k in range(3):
+        quarter_copy(k, True).wait_recv()
+    for part in range(narrow):
+        at = LANES * mod_start(tiles, narrow, part)
+        r.mods[:, at : at + mod_cols] = r.mod_q[part]
+
+    def bias_row(layer, which, size):
+        return r.bias_sum[4 * layer + which : 4 * layer + which + 1, :size]
+
+    def gather_norm(layer, hid, shift, scale, take, before):
+        for part in range(2):
+            before(part)
+
+            def step(start):
+                seg = seg_of(start)
+                unit, _ = norm(take(start, seg))
+                hidden = unit * (1.0 + mod(layer, scale, seg)) + mod(layer, shift, seg)
+                hid[span(local * n + start, STEP), :] = hidden.astype(BF16)
+
+            each_step(part, step)
+            tok_send(hid, part)
+
+    def qkv_block(layer, block):
+        rows = block_rows(block)
+        out = dot(r.hid_attn[layer, rows, :], r.qkv_v[...], ((1,), (0,)))
+        out = (out + bias_row(layer, QKV, 3 * cols)).astype(BF16)
+        for j in range(3 * own_heads):
+            r.heads[layer, j, rows, :HEAD] = out[:, HEAD * j : HEAD * (j + 1)]
+
+    def attend(layer):
+        for head in range(own_heads):
+
+            @pl.loop(0, narrow)
+            def _(i):
+                rows = span(local * i, local)
+                query = r.heads[layer, head, rows, :HEAD]
+                key = r.heads[layer, own_heads + head, :, :HEAD]
+                value = r.heads[layer, 2 * own_heads + head, :, :HEAD]
+                scores = dot(query, key, ((1,), (1,))) * scale_inv
+                scores = jnp.where(r.seg_col[rows, :] == r.seg_row[...], scores, -1e30)
+                top = jnp.max(scores, -1, keepdims=True)
+                power = jnp.exp(scores - top)
+                total = jnp.sum(power, -1, keepdims=True)
+                probs = (power / total).astype(BF16)
+                mixed = dot(probs, value, ((1,), (0,)))
+                r.mixed[layer, rows, HEAD * head : HEAD * (head + 1)] = mixed.astype(BF16)
+                r.log_sum[layer, rows, head : head + 1] = top + jnp.log(total)
+
+    def mlp_block(layer, block):
+        rows = block_rows(block)
+        hidden = r.hid_mlp[layer, rows, :]
+        for at in range(0, width, 3 * LANES):
+            tile = slice(at, at + 3 * LANES)
+            up = dot(hidden, r.up_v[:, tile], ((1,), (0,)))
+            up = up + r.bias_sum[4 * layer + UP : 4 * layer + UP + 1, tile]
+            r.up[layer, rows, tile] = up.astype(BF16)
+            r.act[layer, rows, tile] = gelu(up).astype(BF16)
+        r.part[block] = dot(r.act[layer, rows, :], r.down_v[...], ((1,), (0,)))
+
+    def state_of(layer, start):
+        rows = span(start, STEP)
+        return r.tok[rows, :].astype(F32) if layer == 0 else r.state[rows, :]
+
+    def after_attn(layer):
+        def take(start, seg):
+            rows = span(start, STEP)
+            branch = sum_take(start) + bias_row(layer, OUT, width)
+            r.branch[layer, rows, :] = branch
+            middle = state_of(layer, start) + mod(layer, 2, seg) * branch
+            r.middle[layer, rows, :] = middle
+            return middle
+
+        return take
+
+    def after_mlp(layer):
+        def take(start, seg):
+            rows = span(start, STEP)
+            down = sum_take(start) + bias_row(layer, DOWN, width)
+            r.down[layer, rows, :] = down
+            result = r.middle[layer, rows, :] + mod(layer, 5, seg) * down
+            if layer == 0:
+                r.state[rows, :] = result
+            else:
+                r.mixed_o[rows, :] = result.astype(BF16)
+            return result
+
+        return take
+
+    for layer in range(LAYERS):
+        hid = r.hid_attn.at[layer]
+        if layer == 0:
+            gather_norm(0, hid, 0, 1, lambda start, seg: state_of(0, start), lambda part: None)
+        else:
+            gather_norm(layer, hid, 0, 1, after_mlp(layer - 1), sum_wait)
+        weights_ready(QKV, layer)
+        tok_own(hid)
+        qkv_block(layer, 1)
+        tok_other(hid)
+        qkv_block(layer, 0)
+        if layer == 1:
+            weights_forward(OUT, 1)
+        attend(layer)
+        weights_ready(OUT, layer)
+        tok_drain(hid)
+        for block in range(2):
+            r.part[block] = dot(r.mixed[layer, block_rows(block), :], r.out_v[...], ((1,), (0,)))
+            sum_block(block)
+            if block == 0:
+                sum_cross()
+        weights_forward(UP, layer)
+        hid = r.hid_mlp.at[layer]
+        gather_norm(layer, hid, 3, 4, after_attn(layer), sum_wait)
+        weights_ready(UP, layer)
+        weights_forward(DOWN, layer)
+        weights_ready(DOWN, layer)
+        tok_own(hid)
+        mlp_block(layer, 1)
+        sum_block(1)
+        tok_other(hid)
+        mlp_block(layer, 0)
+        sum_block(0)
+        sum_cross()
+        tok_drain(hid)
+        if layer == 0:
+            weights_forward(QKV, 1)
+    for part in range(2):
+        sum_wait(part)
+        finish = after_mlp(LAYERS - 1)
+
+        def last(start):
+            finish(start, seg_of(start))
+
+        each_step(part, last)
+
+    sums = (r.qkv_d, r.out_d, r.up_d, r.down_d)
+    from_x = (r.qkv_xr, r.out_xr, r.up_xr, r.down_xr)
+    from_z = (r.qkv_zr, r.out_zr, r.up_zr, r.down_zr)
+    final = (r.qkv_f, r.out_f, r.up_f, r.down_f)
+    grads_o = (r.qkv_o, r.out_o, r.up_o, r.down_o)
+    same_y, same_c = y == z // 2, c == z % 2
+
+    def d_rows(which, plane_idx, col):
+        return w_rows(which, plane_idx, col)
+
+    def d_x(which, plane_idx, incoming=False):
+        k = 0 if which == OUT else plane_idx
+        src = sums[which].at[d_rows(which, plane_idx, 1 - x)]
+        return remote(
+            src, from_x[which].at[k], (r.dx_s.at[which, k], r.dx_r.at[which, k]), beside
+        )
+
+    def d_z(which, j):
+        dest = n if which == OUT else plane_of(j)
+        k = 0 if which == OUT else j - 1
+        src = sums[which].at[d_rows(which, dest, x)]
+        return remote(
+            src, from_z[which].at[j - 1], (r.dz_s.at[which, k], r.dz_r.at[which, j - 1]), plane(j)
+        )
+
+    def grad_product(which, layer):
+        left, right = (
+            (r.hid_attn, r.grad_qkv), (r.mixed, r.grad_branch),
+            (r.hid_mlp, r.grad_up), (r.act, r.grad_down),
+        )[which]
+        if which == OUT:
+            product = dot(left[layer], right[...], ((0,), (0,)))
+            sums[which][...] = product.astype(BF16)
+        else:
+
+            @pl.loop(0, width // (3 * LANES))
+            def _(i):
+                tile = span(3 * LANES * i, 3 * LANES, LANES)
+                product = dot(left[layer, :, tile], right[...], ((0,), (0,)))
+                sums[which][tile, :] = product.astype(BF16)
+
+        if layer == 0:
+            pl.semaphore_wait(r.credit_x.at[which], 1)
+        for plane_idx in range(1 if which == OUT else PLANES):
+            d_x(which, plane_idx).start()
+
+    def grad_beside(which, layer):
+        if which == OUT:
+            d_x(which, 0).wait_recv()
+            rows = d_rows(which, n, x)
+            total = sums[which][rows, :].astype(F32) + from_x[which][0].astype(F32)
+            sums[which][rows, :] = total.astype(BF16)
+
+            @pl.when(z != n)
+            def _():
+                if layer == 0:
+                    pl.semaphore_wait(r.credit_z.at[which], 1)
+                d_z(which, (n - z + PLANES) % PLANES).start()
+
+            d_x(which, 0).wait_send()
+        else:
+            for j in (1, 2, 3, 0):
+                idx = plane_of(j)
+                d_x(which, idx).wait_recv()
+                rows = d_rows(which, idx, x)
+                total = sums[which][rows, :].astype(F32) + from_x[which][idx].astype(F32)
+                sums[which][rows, :] = total.astype(BF16)
+                if layer == 0 and j == 1:
+                    pl.semaphore_wait(r.credit_z.at[which], PLANES - 1)
+                if j:
+                    d_z(which, j).start()
+            for idx in range(PLANES):
+                d_x(which, idx).wait_send()
+        if layer == 1:
+            pl.semaphore_signal(
+                r.credit_x.at[which], inc=1, device_id=beside, device_id_type=MESH
+            )
+
+    def grad_planes(which, layer):
+        def add():
+            for j in range(1, PLANES):
+                d_z(which, j).wait_recv()
+            rows = d_rows(which, z, x)
+            total = sums[which][rows, :].astype(F32)
+            for j in range(PLANES - 1):
+                total = total + from_z[which][j].astype(F32)
+            final[which][layer] = total.astype(BF16)
+            if layer == 1:
+                for j in range(1, PLANES):
+                    pl.semaphore_signal(
+                        r.credit_z.at[which], inc=1, device_id=plane(j), device_id_type=MESH
+                    )
+
+        if which == OUT:
+            pl.when(z == n)(add)
+
+            @pl.when(z != n)
+            def _():
+                d_z(which, (n - z + PLANES) % PLANES).wait_send()
+        else:
+            add()
+            for j in range(1, PLANES):
+                d_z(which, j).wait_send()
+
+    def spread(which, layer, kind, source=None):
+        slot = layer * 4 + which
+        if which == OUT:
+            dst = grads_o[which].at[layer]
+        else:
+            dst = grads_o[which].at[layer, n if source is None else source]
+        src = final[which].at[layer] if kind < 2 else dst
+        return remote(
+            src, dst, (r.spread_s.at[slot, kind], r.spread_r.at[slot, kind]), side if kind == 1 else core
+        )
+
+    def spread_own(which, layer):
+        dst = grads_o[which].at[layer] if which == OUT else grads_o[which].at[layer, n]
+        return pltpu.make_async_copy(final[which].at[layer], dst, r.spread_l.at[layer * 4 + which])
+
+    def grad_spread(which, layer):
+        def go():
+            spread(which, layer, 1).start()
+            spread(which, layer, 0).start()
+            spread_own(which, layer).start()
+
+        if which == OUT:
+            pl.when(jnp.logical_and(same_y, same_c))(go)
+        else:
+            go()
+
+    def grad_pass(which, layer):
+        def go():
+            spread(which, layer, 1, n_side).wait_recv()
+            spread(which, layer, 2, n_side).start()
+
+        if which == OUT:
+            pl.when(jnp.logical_and(jnp.logical_not(same_y), same_c))(go)
+        else:
+            go()
+
+    def grad_end(which, layer):
+        if which == OUT:
+
+            @pl.when(jnp.logical_and(same_y, same_c))
+            def _():
+                spread(which, layer, 1).wait_send()
+                spread(which, layer, 0).wait_send()
+                spread_own(which, layer).wait()
+
+            @pl.when(jnp.logical_and(jnp.logical_not(same_y), same_c))
+            def _():
+                spread(which, layer, 2).wait_send()
+
+            @pl.when(jnp.logical_and(same_y, jnp.logical_not(same_c)))
+            def _():
+                spread(which, layer, 0).wait_recv()
+
+            @pl.when(jnp.logical_and(jnp.logical_not(same_y), jnp.logical_not(same_c)))
+            def _():
+                spread(which, layer, 2).wait_recv()
+        else:
+            spread(which, layer, 0, n_core).wait_recv()
+            spread(which, layer, 2, n_far).wait_recv()
+            spread(which, layer, 2, n_side).wait_send()
+            spread(which, layer, 1).wait_send()
+            spread(which, layer, 0).wait_send()
+            spread_own(which, layer).wait()
+
+    def bias_grad(layer, which, values):
+        at = 4 * layer + which
+        r.bias_grad[at : at + 1, : values.shape[1]] = jnp.sum(
+            values.astype(F32), 0, keepdims=True
+        )
+
+    def back_mlp_block(layer, block):
+        rows = block_rows(block)
+        grad_down = r.grad_down[rows, :]
+        for at in range(0, width, 3 * LANES):
+            tile = slice(at, at + 3 * LANES)
+            grad_act = dot(grad_down, r.down_v[tile, :], ((1,), (1,)))
+            up = r.up[layer, rows, tile].astype(F32)
+            r.grad_up[rows, tile] = (grad_act * gelu_slope(up)).astype(BF16)
+        r.part[block] = dot(r.grad_up[rows, :], r.up_v[...], ((1,), (1,)))
+
+    def back_attn_block(layer, block):
+        rows = block_rows(block)
+        out = dot(r.grad_branch[rows, :], r.out_v[...], ((1,), (1,))).astype(BF16)
+        for j in range(own_heads):
+            r.grad_heads[j, rows, :HEAD] = out[:, HEAD * j : HEAD * (j + 1)]
+
+    def back_attend(layer, head):
+        @pl.loop(0, narrow)
+        def _(i):
+            rows = span(local * i, local)
+            query = r.heads[layer, head, rows, :HEAD]
+            key = r.heads[layer, own_heads + head, :, :HEAD]
+            value = r.heads[layer, 2 * own_heads + head, :, :HEAD]
+            grad = r.grad_heads[head, rows, :HEAD]
+            scores = dot(query, key, ((1,), (1,))) * scale_inv
+            probs = jnp.exp(scores - r.log_sum[layer, rows, head : head + 1])
+            probs = jnp.where(r.seg_col[rows, :] == r.seg_row[...], probs, 0.0)
+            grad_probs = dot(grad, value, ((1,), (1,)))
+            inner = jnp.sum(probs * grad_probs, -1, keepdims=True)
+            grad_scores = (probs * (grad_probs - inner)).astype(BF16)
+            grad_query = dot(grad_scores, key, ((1,), (0,))) * scale_inv
+            r.grad_qkv[rows, HEAD * head : HEAD * (head + 1)] = grad_query.astype(BF16)
+            grad_key = dot(grad_scores, query, ((0,), (0,)))
+            grad_value = dot(probs.astype(BF16), grad, ((0,), (0,)))
+
+            @pl.when(i == 0)
+            def _():
+                r.key_sum[:, :HEAD] = grad_key
+                r.value_sum[:, :HEAD] = grad_value
+
+            @pl.when(i > 0)
+            def _():
+                r.key_sum[:, :HEAD] += grad_key
+                r.value_sum[:, :HEAD] += grad_value
+
+        at = cols + HEAD * head
+        r.grad_qkv[:, at : at + HEAD] = (r.key_sum[:, :HEAD] * scale_inv).astype(BF16)
+        r.grad_qkv[:, cols + at : cols + at + HEAD] = r.value_sum[:, :HEAD].astype(BF16)
+
+    for part in range(2):
+        def first(start):
+            rows = span(start, STEP)
+            r.grad[rows, :] = r.cot[rows, :].astype(F32)
+
+        each_step(part, first)
+
+    def both(body):
+        for part in range(2):
+            each_step(part, body)
+
+    for layer in reversed(range(LAYERS)):
+        older = layer + 1
+        for part in range(2):
+            if layer < LAYERS - 1:
+                sum_wait(part)
+
+            def start_down(start):
+                rows = span(start, STEP)
+                seg = seg_of(start)
+                if layer < LAYERS - 1:
+                    grad_hidden = sum_take(start)
+                    unit, inv = norm(state_of(older, start))
+                    r.grad_hid[rows, :] = grad_hidden
+                    r.grad[rows, :] += norm_back(
+                        grad_hidden * (1.0 + mod(older, 1, seg)), unit, inv
+                    )
+                grad_down = (mod(layer, 5, seg) * r.grad[rows, :]).astype(BF16)
+                r.grad_down[span(local * n + start, STEP), :] = grad_down
+
+            each_step(part, start_down)
+            tok_send(r.grad_down, part)
+
+        def sums_attn(idx):
+            def body(start):
+                rows = span(start, STEP)
+                seg = seg_of(start)
+                unit, _ = norm(state_of(idx, start))
+                grad_hidden = r.grad_hid[rows, :]
+                mod_sum(idx, 0, seg, grad_hidden)
+                mod_sum(idx, 1, seg, grad_hidden * unit)
+
+            return body
+
+        if layer < LAYERS - 1:
+            both(sums_attn(older))
+            load(DOWN, layer).wait()
+            load(UP, layer).wait()
+
+        def sums_gate_mlp(start):
+            rows = span(start, STEP)
+            mod_sum(layer, 5, seg_of(start), r.down[layer, rows, :] * r.grad[rows, :])
+
+        both(sums_gate_mlp)
+        bias_grad(layer, DOWN, r.grad_down[span(local * n, local), :])
+        tok_own(r.grad_down)
+        back_mlp_block(layer, 1)
+        sum_block(1)
+        tok_other(r.grad_down)
+        back_mlp_block(layer, 0)
+        sum_block(0)
+        sum_cross()
+        if layer > 0:
+            load(DOWN, layer - 1).start()
+            load(UP, layer - 1).start()
+        if layer == 1:
+            grad_product(DOWN, 1)
+            grad_product(UP, 1)
+        else:
+            grad_beside(UP, 1)
+            grad_beside(OUT, 1)
+            grad_planes(DOWN, 1)
+            grad_product(DOWN, 0)
+        bias_grad(layer, UP, r.grad_up[...])
+        tok_drain(r.grad_down)
+        for part in range(2):
+            sum_wait(part)
+
+            def start_branch(start):
+                rows = span(start, STEP)
+                seg = seg_of(start)
+                grad_hidden = sum_take(start)
+                unit, inv = norm(r.middle[layer, rows, :])
+                r.grad_hid[rows, :] = grad_hidden
+                grad = r.grad[rows, :] + norm_back(
+                    grad_hidden * (1.0 + mod(layer, 4, seg)), unit, inv
+                )
+                r.grad[rows, :] = grad
+                grad_branch = (mod(layer, 2, seg) * grad).astype(BF16)
+                r.grad_branch[span(local * n + start, STEP), :] = grad_branch
+
+            each_step(part, start_branch)
+            tok_send(r.grad_branch, part)
+
+        def sums_mlp(start):
+            rows = span(start, STEP)
+            seg = seg_of(start)
+            unit, _ = norm(r.middle[layer, rows, :])
+            grad_hidden = r.grad_hid[rows, :]
+            mod_sum(layer, 3, seg, grad_hidden)
+            mod_sum(layer, 4, seg, grad_hidden * unit)
+            mod_sum(layer, 2, seg, r.branch[layer, rows, :] * r.grad[rows, :])
+
+        both(sums_mlp)
+        bias_grad(layer, OUT, r.grad_branch[span(local * n, local), :])
+        if layer < LAYERS - 1:
+            load(OUT, layer).wait()
+            load(QKV, layer).wait()
+        tok_own(r.grad_branch)
+        back_attn_block(layer, 1)
+        tok_other(r.grad_branch)
+        back_attn_block(layer, 0)
+        if layer > 0:
+            load(OUT, layer - 1).start()
+        if layer == 0:
+            grad_spread(DOWN, 1)
+            grad_beside(QKV, 1)
+        for head in range(own_heads):
+            back_attend(layer, head)
+        for block in range(2):
+            rows = block_rows(block)
+            r.part[block] = dot(r.grad_qkv[rows, :], r.qkv_v[...], ((1,), (1,)))
+            sum_block(block)
+            if block == 0:
+                sum_cross()
+        tok_drain(r.grad_branch)
+        if layer > 0:
+            load(QKV, layer - 1).start()
+        if layer == 1:
+            grad_product(OUT, 1)
+            grad_product(QKV, 1)
+            grad_beside(DOWN, 1)
+        else:
+            grad_planes(UP, 1)
+            grad_product(UP, 0)
+            grad_planes(OUT, 1)
+            grad_product(OUT, 0)
+            grad_planes(QKV, 1)
+            grad_product(QKV, 0)
+        bias_grad(layer, QKV, r.grad_qkv[...])
+    for part in range(2):
+        sum_wait(part)
+
+        def finish_grad(start):
+            rows = span(start, STEP)
+            seg = seg_of(start)
+            grad_hidden = sum_take(start)
+            unit, inv = norm(state_of(0, start))
+            grad = r.grad[rows, :] + norm_back(grad_hidden * (1.0 + mod(0, 1, seg)), unit, inv)
+            r.token_o[rows, :] = grad
+            mod_sum(0, 0, seg, grad_hidden)
+            mod_sum(0, 1, seg, grad_hidden * unit)
+
+        each_step(part, finish_grad)
+
+    def quarter_back(k, incoming=False):
+        device, idx = narrow_peers[k]
+        at = span(LANES * mod_start(tiles, narrow, idx), mod_cols, LANES)
+        return remote(
+            r.mod_grad.at[:, at], r.quarter_rx.at[k], (r.back_s.at[k], r.back_r.at[k]), device
+        )
+
+    def wide_back(j, incoming=False):
+        return remote(
+            r.quarter_sum, r.quarter_all.at[(w - j + wide) % wide if incoming else w],
+            (r.wide_s.at[j - 1], r.wide_r.at[j - 1]), wide_peer(j),
+        )
+
+    def bias_wide(j, incoming=False):
+        return remote(
+            r.bias_grad, r.bias_all.at[(w - j + wide) % wide if incoming else w],
+            (r.bias_wide_s.at[j - 1], r.bias_wide_r.at[j - 1]), wide_peer(j),
+        )
+
+    def bias_narrow(k, incoming=False):
+        device, idx = narrow_peers[k]
+        return remote(
+            r.bias_row, r.bias_o.at[idx if incoming else n],
+            (r.bias_narrow_s.at[k], r.bias_narrow_r.at[k]), device,
+        )
+
+    def mod_narrow(k, incoming=False):
+        device, idx = narrow_peers[k]
+        return remote(
+            r.mod_all, r.mod_o.at[idx if incoming else n],
+            (r.mod_narrow_s.at[k], r.mod_narrow_r.at[k]), device,
+        )
+
+    for k in range(3):
+        quarter_back(k).start()
+    grad_beside(DOWN, 0)
+    grad_spread(UP, 1)
+    grad_spread(OUT, 1)
+    own_at = span(LANES * mod_start(tiles, narrow, n), mod_cols, LANES)
+    total = r.mod_grad[:, own_at]
+    for k in range(3):
+        quarter_back(k, True).wait_recv()
+        total = total + r.quarter_rx[k]
+    r.quarter_sum[...] = total
+    for j in range(1, wide):
+        wide_back(j).start()
+    for j in range(1, wide):
+        bias_wide(j).start()
+    r.quarter_all[pl.ds(w, 1)] = total[None]
+    r.bias_all[pl.ds(w, 1)] = r.bias_grad[...][None]
+    grad_spread(QKV, 1)
+    grad_beside(UP, 0)
+    grad_beside(OUT, 0)
+    for which in (DOWN, UP, OUT, QKV):
+        grad_pass(which, 1)
+    grad_planes(DOWN, 0)
+    grad_spread(DOWN, 0)
+    grad_beside(QKV, 0)
+    for j in range(1, wide):
+        wide_back(j, True).wait_recv()
+    r.mod_all[...] = r.quarter_all[...].reshape(wide * 2 * SEGS, mod_cols).astype(BF16)
+    mod_own = pltpu.make_async_copy(r.mod_all, r.mod_o.at[n], r.mod_own_sem)
+    mod_own.start()
+    for k in range(3):
+        mod_narrow(k).start()
+    for j in range(1, wide):
+        bias_wide(j, True).wait_recv()
+    r.bias_row[...] = jnp.sum(r.bias_all[...], 0)
+    bias_own = pltpu.make_async_copy(r.bias_row, r.bias_o.at[n], r.bias_own_sem)
+    bias_own.start()
+    for k in range(3):
+        bias_narrow(k).start()
+    grad_planes(UP, 0)
+    grad_spread(UP, 0)
+    grad_planes(OUT, 0)
+    grad_spread(OUT, 0)
+    grad_pass(DOWN, 0)
+    grad_planes(QKV, 0)
+    grad_spread(QKV, 0)
+    for which in (UP, OUT, QKV):
+        grad_pass(which, 0)
+
+    for layer in range(LAYERS):
+        for which in range(4):
+            weights_drain(which, layer)
+            grad_end(which, layer)
+    for j in range(1, wide):
+        for copy in (lead_copy, bias_copy, mod_copy, wide_back, bias_wide):
+            copy(j).wait_send()
+    for k in range(3):
+        for copy in (quarter_copy, quarter_back, mod_narrow, bias_narrow):
+            copy(k).wait_send()
+        mod_narrow(k, True).wait_recv()
+        bias_narrow(k, True).wait_recv()
+    mod_own.wait()
+    bias_own.wait()
+
+
+def gelu_slope(values):
+    rate = math.sqrt(2.0 / math.pi)
+    bent = jnp.tanh(rate * (values + 0.044715 * values * values * values))
+    inner = rate * (1.0 + 3.0 * 0.044715 * values * values)
+    return 0.5 * (1.0 + bent) + 0.5 * values * (1.0 - bent * bent) * inner
+
+
+def fused_device(
+    wide, narrow,
+    tokens, cond, seg_ids, cond_index, cotangent,
+    ada_weight, ada_bias, qkv_weight, qkv_bias, out_weight, out_bias,
+    up_weight, up_bias, down_weight, down_bias,
+):
+    w = lax.axis_index("wide")
+    n = lax.axis_index("narrow")
+    local, width = tokens.shape[1:]
+    row_len = seg_ids.shape[1]
+    depth, cols = width // wide, width // narrow
+    hidden_own = up_weight.shape[-1] // wide // narrow
+    hidden = wide * hidden_own
+    tiles = ada_weight.shape[-1] // LANES
+    mod_cols = LANES * -(-tiles // narrow)
+
+    def own(values, axis):
+        return lax.dynamic_index_in_dim(values, n, axis, keepdims=False)
+
+    def placed(values):
+        spot = jnp.arange(wide)[None, :, None] == w
+        return jnp.where(spot, values.astype(F32)[:, None, :], 0.0).reshape(LAYERS, -1)
+
+    ada_b = lax.dynamic_slice_in_dim(
+        placed(ada_bias), LANES * mod_start(tiles, narrow, n), mod_cols, 1
+    )
+    ada_b = jnp.repeat(ada_b, SEGS, axis=0)
+    qkv_b = own(placed(qkv_bias).reshape(LAYERS, 3, narrow, cols), 2).reshape(LAYERS, -1)
+    qkv_b = jnp.pad(qkv_b, ((0, 0), (0, width - 3 * cols)))
+    up_b = own(placed(up_bias).reshape(LAYERS, wide, narrow, hidden_own), 2).reshape(LAYERS, -1)
+    bias = jnp.stack([qkv_b, placed(out_bias), up_b, placed(down_bias)], 1).reshape(-1, width)
+
+    cond_hot = (cond_index[0, :, None] == jnp.arange(SEGS, dtype=jnp.int32)[None, :]).astype(F32)
+    chosen = jnp.dot(cond_hot, cond[0].astype(F32), precision=EXACT)
+    lead = (chosen * jax.nn.sigmoid(chosen)).astype(BF16)
+    lead = lead.reshape(SEGS, wide, depth).transpose(1, 0, 2)
+    lead = jnp.pad(lead, ((0, 0), (0, 16 - SEGS), (0, 0)))
+
+    seg_row = seg_ids[0]
+    seg_own = lax.dynamic_slice_in_dim(seg_row, n * local, local, 0)
+
+    qkv_own = jnp.concatenate(
+        [
+            lax.dynamic_slice_in_dim(qkv_weight, width * j + n * cols, cols, 2) for j in range(3)
+        ],
+        axis=2,
+    )
+    up_own = jnp.concatenate(
+        [
+            lax.dynamic_slice_in_dim(up_weight, (j * narrow + n) * hidden_own, hidden_own, 2)
+            for j in range(wide)
+        ],
+        axis=2,
+    )
+    down_own = lax.dynamic_slice_in_dim(down_weight, n * hidden_own, hidden_own, 1)
+
+    inputs = dict(
+        tok=tokens[0], lead=lead, bias=bias, ada_bias=ada_b,
+        seg_own=seg_own[:, None], seg_col=seg_row[:, None], seg_row=seg_row[None, :],
+        cot=cotangent[0], ada=ada_weight, qkv_s=qkv_own, out_s=out_weight, up_s=up_own, down_s=down_own,
+    )
+    in_hbm = ("ada", "qkv_s", "out_s", "up_s", "down_s")
+    shape = jax.ShapeDtypeStruct
+    outputs = dict(
+        mixed_o=shape((local, width), BF16), token_o=shape((local, width), F32),
+        qkv_o=shape((LAYERS, narrow, depth, 3 * cols), BF16),
+        out_o=shape((LAYERS, depth, width), BF16),
+        up_o=shape((LAYERS, narrow, depth, hidden), BF16),
+        down_o=shape((LAYERS, narrow, hidden_own, width), BF16),
+        bias_o=shape((narrow, 4 * LAYERS, width), F32),
+        mod_o=shape((narrow, wide * LAYERS * SEGS, mod_cols), BF16),
+        qkv_h=shape((LAYERS, width, 3 * cols), BF16), out_h=shape((LAYERS, cols, width), BF16),
+        up_h=shape((LAYERS, width, hidden), BF16), down_h=shape((LAYERS, hidden, width), BF16),
+    )
+    out_vmem = ("mixed_o", "token_o")
+    vmem, dma = pltpu.VMEM, pltpu.SemaphoreType.DMA
+    heads = cols // HEAD
+    scratch = dict(
+        qkv_v=vmem((width, 3 * cols), BF16), out_v=vmem((cols, width), BF16),
+        up_v=vmem((width, hidden), BF16), down_v=vmem((hidden, width), BF16),
+        hid_attn=vmem((LAYERS, row_len, width), BF16), hid_mlp=vmem((LAYERS, row_len, width), BF16),
+        heads=vmem((LAYERS, 3 * heads, row_len, LANES), BF16),
+        mixed=vmem((LAYERS, row_len, cols), BF16), log_sum=vmem((LAYERS, row_len, heads), F32),
+        up=vmem((LAYERS, row_len, hidden), BF16), act=vmem((LAYERS, row_len, hidden), BF16),
+        state=vmem((local, width), F32), middle=vmem((LAYERS, local, width), F32),
+        branch=vmem((LAYERS, local, width), F32), down=vmem((LAYERS, local, width), F32),
+        grad=vmem((local, width), F32), grad_hid=vmem((local, width), F32),
+        grad_down=vmem((row_len, width), BF16), grad_branch=vmem((row_len, width), BF16),
+        grad_up=vmem((row_len, hidden), BF16), grad_qkv=vmem((row_len, 3 * cols), BF16),
+        grad_heads=vmem((heads, row_len, LANES), BF16),
+        key_sum=vmem((row_len, LANES), F32), value_sum=vmem((row_len, LANES), F32),
+        part=vmem((2, 2 * local, width), F32),
+        core_tx=vmem((2, local, width), BF16), core_rx=vmem((2, local, width), BF16),
+        side_tx=vmem((local, width), BF16), side_rx=vmem((local, width), BF16),
+        ada_v=vmem((LAYERS, depth, mod_cols), BF16),
+        lead_rx=vmem((wide, 16, depth), BF16), bias_rx=vmem((wide, 4 * LAYERS, width), F32),
+        bias_sum=vmem((4 * LAYERS, width), F32),
+        mod_tx=vmem((wide, LAYERS * SEGS, mod_cols), F32), mod_rx=vmem((wide, LAYERS * SEGS, mod_cols), F32),
+        mod_q=vmem((narrow, LAYERS * SEGS, mod_cols), F32),
+        mods=vmem((LAYERS * SEGS, tiles * LANES), F32),
+        mod_grad=vmem((LAYERS * SEGS, tiles * LANES), F32),
+        quarter_rx=vmem((3, LAYERS * SEGS, mod_cols), F32),
+        quarter_sum=vmem((LAYERS * SEGS, mod_cols), F32),
+        quarter_all=vmem((wide, LAYERS * SEGS, mod_cols), F32),
+        mod_all=vmem((wide * LAYERS * SEGS, mod_cols), BF16),
+        bias_grad=vmem((4 * LAYERS, width), F32), bias_all=vmem((wide, 4 * LAYERS, width), F32),
+        bias_row=vmem((4 * LAYERS, width), F32),
+        qkv_d=vmem((width, 3 * cols), BF16), out_d=vmem((cols, width), BF16),
+        up_d=vmem((width, hidden), BF16), down_d=vmem((hidden, width), BF16),
+        qkv_xr=vmem((PLANES, depth, 3 * cols), BF16), out_xr=vmem((1, depth, width), BF16),
+        up_xr=vmem((PLANES, depth, hidden), BF16), down_xr=vmem((PLANES, hidden_own, width), BF16),
+        qkv_zr=vmem((PLANES - 1, depth, 3 * cols), BF16), out_zr=vmem((PLANES - 1, depth, width), BF16),
+        up_zr=vmem((PLANES - 1, depth, hidden), BF16), down_zr=vmem((PLANES - 1, hidden_own, width), BF16),
+        qkv_f=vmem((LAYERS, depth, 3 * cols), BF16), out_f=vmem((LAYERS, depth, width), BF16),
+        up_f=vmem((LAYERS, depth, hidden), BF16), down_f=vmem((LAYERS, hidden_own, width), BF16),
+        wz_s=dma((8, 3)), wz_r=dma((8, 3)), wx_s=dma((8, 4)), wx_r=dma((8, 4)), w_own=dma((8,)),
+        load_sem=dma((4,)), tok_s=dma((6,)), tok_r=dma((6,)), sum_s=dma((4,)), sum_r=dma((4,)),
+        lead_sem_s=dma((wide - 1,)), lead_sem_r=dma((wide - 1,)),
+        bias_sem_s=dma((wide - 1,)), bias_sem_r=dma((wide - 1,)),
+        mod_sem_s=dma((wide - 1,)), mod_sem_r=dma((wide - 1,)),
+        quarter_s=dma((3,)), quarter_r=dma((3,)), ada_sem=dma,
+        dx_s=dma((4, 4)), dx_r=dma((4, 4)), dz_s=dma((4, 3)), dz_r=dma((4, 3)),
+        spread_s=dma((8, 3)), spread_r=dma((8, 3)), spread_l=dma((8,)),
+        back_s=dma((3,)), back_r=dma((3,)),
+        wide_s=dma((wide - 1,)), wide_r=dma((wide - 1,)),
+        bias_wide_s=dma((wide - 1,)), bias_wide_r=dma((wide - 1,)),
+        bias_narrow_s=dma((3,)), bias_narrow_r=dma((3,)),
+        mod_narrow_s=dma((3,)), mod_narrow_r=dma((3,)), mod_own_sem=dma, bias_own_sem=dma,
+        credit_x=pltpu.SemaphoreType.REGULAR((4,)), credit_z=pltpu.SemaphoreType.REGULAR((4,)),
+    )
+    cfg = SimpleNamespace(
+        names=[*inputs, *outputs, *scratch], wide=wide, narrow=narrow, width=width, depth=depth,
+        local=local, cols=cols, mod_cols=mod_cols, tiles=tiles,
+    )
+
+    def place(name, vmem_ok):
+        return pl.BlockSpec(memory_space=pltpu.VMEM if vmem_ok else pl.ANY)
+
+    results = pl.pallas_call(
+        partial(block_kernel, cfg),
+        out_shape=list(outputs.values()),
+        in_specs=[place(name, name not in in_hbm) for name in inputs],
+        out_specs=[place(name, name in out_vmem) for name in outputs],
+        scratch_shapes=list(scratch.values()),
+        compiler_params=pltpu.CompilerParams(
+            collective_id=0, has_side_effects=True, vmem_limit_bytes=62 * 2**20
+        ),
+    )(*inputs.values())
+    got = dict(zip(outputs, results))
+
+    qkv_g = got["qkv_o"].reshape(LAYERS, narrow, depth, 3, cols).transpose(0, 2, 3, 1, 4)
+    up_g = got["up_o"].reshape(LAYERS, narrow, depth, wide, hidden_own).transpose(0, 2, 3, 1, 4)
+    weight_grads = (
+        qkv_g.reshape(LAYERS, depth, -1).astype(F32),
+        got["out_o"].astype(F32),
+        up_g.reshape(LAYERS, depth, -1).astype(F32),
+        got["down_o"].reshape(LAYERS, -1, width).astype(F32),
+    )
+
+    bias_g = got["bias_o"].reshape(narrow, LAYERS, 4, width)
+    qkv_bg = bias_g[:, :, QKV, : 3 * cols].reshape(narrow, LAYERS, 3, cols).transpose(1, 2, 0, 3)
+    up_bg = bias_g[:, :, UP].reshape(narrow, LAYERS, wide, hidden_own).transpose(1, 2, 0, 3)
+    full_biases = (
+        qkv_bg.reshape(LAYERS, -1), jnp.sum(bias_g[:, :, OUT], 0),
+        up_bg.reshape(LAYERS, -1), jnp.sum(bias_g[:, :, DOWN], 0),
+    )
+    bias_grads = [
+        lax.dynamic_slice_in_dim(item, w * (item.shape[1] // wide), item.shape[1] // wide, 1)
+        for item in full_biases
+    ]
+
+    mod_parts = []
+    for part in range(narrow):
+        size = mod_start(tiles, narrow, part + 1) - mod_start(tiles, narrow, part)
+        mod_parts.append(got["mod_o"][part, :, : LANES * size])
+    mod_all = jnp.concatenate(mod_parts, axis=1).reshape(wide, LAYERS, SEGS, -1)
+    mod_all = mod_all.transpose(1, 0, 2, 3).reshape(LAYERS, wide * SEGS, -1)
+    return weight_grads, bias_grads, mod_all, got["mixed_o"], got["token_o"], chosen, cond_hot
+
+
+def fused_program(wide, narrow, *args):
+    tokens, cond, seg_ids, cond_index, cotangent, ada_weight, ada_bias = args[:7]
+    w = lax.axis_index("wide")
+    width = tokens.shape[-1]
+    depth = width // wide
+    weight_grads, bias_grads, mod_all, mixed, token_grad, chosen, cond_hot = fused_device(
+        wide, narrow, *args
+    )
+    lead = (chosen * jax.nn.sigmoid(chosen)).astype(BF16)
+    lead_own = lax.all_to_all(
+        lead.reshape(SEGS, wide, depth).transpose(1, 0, 2), "wide", 0, 0, tiled=False
+    ).reshape(wide * SEGS, depth)
+    ada_grad = jnp.einsum("nd,lne->lde", lead_own, mod_all, preferred_element_type=F32)
+    ada_size = ada_bias.shape[1]
+    ada_bias_grad = jnp.sum(
+        lax.dynamic_slice_in_dim(mod_all, w * ada_size, ada_size, 2).astype(F32), axis=1
+    )
+    lead_grad = jnp.einsum("lne,lde->nd", mod_all, ada_weight, preferred_element_type=F32)
+    lead_grad = lax.all_to_all(lead_grad.reshape(wide, SEGS, depth), "wide", 0, 0, tiled=False)
+    lead_grad = lead_grad.transpose(1, 0, 2).reshape(SEGS, width)
+    gate = jax.nn.sigmoid(chosen)
+    chosen_grad = lead_grad * (gate * (1.0 + chosen * (1.0 - gate)))
+    cond_grad = jnp.dot(cond_hot.T, chosen_grad, precision=EXACT)
+    out = [mixed[None], token_grad[None], cond_grad[None], ada_grad, ada_bias_grad]
+    for weight, bias in zip(weight_grads, bias_grads):
+        out += [weight, bias]
+    return tuple(out)
+
+
 def solution(mesh):
     matrix, vector = P(None, "wide", None), P(None, "wide")
     rows, cond_rows = P("wide", "narrow", None), P("wide", None, None)
+    wide, narrow = mesh.shape["wide"], mesh.shape["narrow"]
+    fused = wide == PLANES * PAIR and narrow == PLANES
     return jax.shard_map(
-        partial(per_device, mesh.shape["wide"], mesh.shape["narrow"]),
+        partial(fused_program if fused else plain_device, wide, narrow),
         mesh=mesh,
         in_specs=(rows, cond_rows, P("wide", None), P("wide", None), rows) + (matrix, vector) * 5,
         out_specs=(rows, rows, cond_rows) + (matrix, vector) * 5,

time: 1800 us -> 714 us (0.40)
  waiting for transfers between devices: 1210 us -> 0.01 us
  Pallas kernels: 0 us -> 572 us
  blocking collectives: 160 us -> 0 us
  matrix products: 153 us -> 12.1 us
  other arithmetic: 75.7 us -> 7.86 us
  local copies, waits for them, and re-layouts: 159 us -> 94 us
    pallas_call x0 -> x1, Pallas kernels: none -> 572 us  [fused_device(): pl.pallas_call(partial(block_kernel, cfg), out_shape=list(outputs.values(...]
    all_gather x22 -> x0, waiting for transfers between devices: 534 us -> none  [the longest x8 114 us: gather_tokens(): return lax.all_gather(values, 'narrow', axis=0, tiled=True)]
    reduce_scatter x14 -> x0, waiting for transfers between devices: 497 us -> none  [the longest x6 333 us: per_device(): lax.psum_scatter(item, 'wide', scatter_dimension=0, tiled=True)]
    all_gather x6 -> x0, blocking collectives: 142 us -> none  [the longest x1 45.6 us: per_device(): modulation = lax.all_gather(mod_part, 'narrow', axis=2, tiled=True)]
    dot_general x43 -> x4, matrix products: 142 us -> 12.1 us  [the longest x1 5.28 us: fused_program(): jnp.einsum('nd,lne->lde', lead_own, mod_all, preferred_element_type=F32)]
    unnamed x41 -> x0, waiting for transfers between devices: 100 us -> none
    psum x1 -> x0, waiting for transfers between devices: 83.9 us -> none  [per_device(): out_g = lax.psum(out_g, 'wide')]
    convert_element_type x8 -> x6, local copies, waits for them, and re-layouts: 19.7 us -> 54.3 us  [the longest x3 33.1 us: fused_device(): up_g.reshape(LAYERS, depth, -1).astype(F32)]
  transfers between devices with their start and end apart: 40 -> 2, of which waited for: 34 -> 0; matrix products, arithmetic and copies ran while one was open for 16% -> 15% of each run, Pallas kernels for 0% -> 82%
where the time goes in v2:
time: 714 us; the launch traced here: 701 us
  Pallas kernels  572 us (80%)
  local copies, waits for them, and re-layouts  94 us (13%)
  starting transfers between devices  13.3 us (2%)
  matrix products  12.1 us (2%)
  other arithmetic  7.86 us (1%)
    pallas_call x1, Pallas kernels, fused_device(): pl.pallas_call(partial(block_kernel, cfg), out_shape=list(outputs.values(...  572 us
    convert_element_type x3, local copies, waits for them, and re-layouts, fused_device(): up_g.reshape(LAYERS, depth, -1).astype(F32)  33.1 us
    convert_element_type x3, local copies, waits for them, and re-layouts, fused_device(): qkv_g.reshape(LAYERS, depth, -1).astype(F32)  21.2 us
  transfers between devices with their start and end apart: 2, of which 0 were waited for; matrix products, arithmetic and copies ran while one was open for 15% of the time, Pallas kernels for 82%

profile of v2, /device:TPU:17, one launch (start us, length us, event | category | flops | bytes accessed | tf_op | source)
XLA Modules:
  0.0 701.0 jit_solution(10435741249328665250)
XLA Ops:
  0.7 0.7 copy-done
  1.4 1.4 multiply_convert_fusion
  3.5 5.6 all-to-all-start.1
  9.3 0.7 broadcast_in_dim.161
  11.0 0.7 broadcast_in_dim.142
  12.0 0.8 reshape.181
  13.1 0.7 broadcast_in_dim.148
  13.9 0.7 broadcast_in_dim.156
  15.4 0.7 fusion.19
  16.0 0.7 copy.74.refs_4_
  16.8 1.4 pad.8.refs_1_
  18.1 1.5 copy.75.refs_5_
  19.7 2.0 constant_dynamic-slice_fusion.5.refs_12_
  21.6 1.4 constant_dynamic-slice_fusion.16
  23.1 1.0 pad_maximum_fusion.refs_9_
  24.1 2.1 constant_dynamic-slice_fusion.6
  26.2 1.4 concatenate.19.refs_11_
  27.5 572.4 %shard_map.246 = (bf16[128,1152]{1,0:T(8,128)(2,1)}, f32[128,1152]{1,0:T(8,128)}, bf16[2,4,144,864]{3,2,1,0:T(8,128)(2,1)}, bf16[2,144,1152]{2,1,0:T(8,128)(2,1)...) custom-call(bf16[128,1152]{1,0:T(8,128)(2,1)} %bitcast.69, ...), custom_call_target="tpu_custom_call" | custom-call | tf_op jit(solution)/shard_map/pallas_call | solution.py:1341
  600.0 1.1 fusion.22
  601.0 1.1 fusion.21
  602.1 1.0 reshape.178
  603.1 0.8 slice_reduce_fusion
  605.0 0.9 copy.108
  605.9 4.5 fusion.2
  610.4 2.9 bitcast_convert_fusion
  613.4 1.5 reshape_squeeze.7
  614.9 1.5 copy.106
  616.4 1.6 reshape.180
  618.0 1.4 copy.95
  619.3 1.5 reshape_squeeze.6
  620.8 1.4 copy.87
  622.2 1.5 reshape.179
  623.7 1.4 constant_dynamic-slice_fusion.2
  625.1 1.4 constant_dynamic-slice_fusion.4
  626.4 1.3 constant_dynamic-slice_fusion.1
  627.8 7.3 %reshape.186 = f32[2,4,144,8,144]{4,3,2,1,0:T(8,128)} reshape(bf16[2,4,144,1152]{3,2,1,0:T(8,128)(2,1)S(1)} %copy-done.2) | data formatting | bytes 7962624 | tf_op jit(solution)/shard_map/convert_element_type | solution.py:1358
  635.1 13.4 %copy.88 = f32[2,144,8,4,144]{4,3,2,1,0:T(4,128)} copy(f32[2,144,8,4,144]{4,2,1,3,0:T(8,128)} %bitcast.64) | data formatting | bytes 10616832 | tf_op jit(solution)/shard_map/convert_element_type | solution.py:1358
  648.5 12.4 %reshape.183 = f32[2,144,4608]{2,1,0:T(8,128)} reshape(f32[2,144,8,4,144]{4,3,2,1,0:T(4,128)} %copy.88) | data formatting | bytes 10616832 | tf_op jit(solution)/shard_map/convert_element_type | solution.py:1358
  660.9 6.2 reshape.185
  667.2 8.7 %copy.85 = f32[2,144,3,4,288]{4,3,2,1,0:T(4,128)} copy(f32[2,144,3,4,288]{4,2,1,3,0:T(4,128)} %bitcast.65) | data formatting | bytes 7962624 | tf_op jit(solution)/shard_map/convert_element_type | solution.py:1356
  675.9 6.2 reshape.182
  682.1 1.1 convert_element_type.69
  683.3 1.7 convert_reduce_fusion
  685.0 7.7 %all-to-all-start = ((f32[8,4,144]{2,1,0:T(4,128)}), f32[8,4,144]{2,1,0:T(4,128)S(1)}, u32[]{:S(2)}, u32[]{:S(2)}) async-start(f32[8,4,144]{2,1,0:T(4,128)} %fusion.2), calls=%async_computation | async-start | bytes 65536 | tf_op jit(solution)/shard_map/all_to_all | solution.py:1401
  692.7 5.3 convolution_bitcast_fusion
  698.1 0.9 convolution_bitcast_fusion.1
  699.0 0.7 copy.111
  699.7 0.8 copy.112
  (64 shorter events, 4.6 us)
Async XLA Ops:
  0.6 0.7 copy-start
  3.5 681.5 %all-to-all-start.1 = ((bf16[8,4,144]{2,1,0:T(4,128)(2,1)}), bf16[8,4,144]{2,1,0:T(4,128)(2,1)}, u32[]{:S(2)}, u32[]{:S(2)}) async-start(bf16[8,4,144]{2,1,0:T(4,128)(2,1)} %bitcast.63), calls=%async_computation.1 | async-start | bytes 32768 | tf_op jit(solution)/shard_map/all_to_all | solution.py:1392
  605.9 4.5 copy-start.5
  605.9 4.5 copy-start.3
  610.4 17.3 %copy-start.2 = (bf16[2,4,144,1152]{3,2,1,0:T(8,128)(2,1)S(1)}, bf16[2,4,144,1152]{3,2,1,0:T(8,128)(2,1)}, u32[]{:S(2)}) copy-start(bf16[2,4,144,1152]{3,2,1,0:T(8,128)(2,1)} %get-tuple-element.27) | copy-start | bytes 7962628
  648.5 12.4 %copy-start.4 = (bf16[2,4,144,864]{3,2,1,0:T(8,128)(2,1)S(1)}, bf16[2,4,144,864]{3,2,1,0:T(8,128)(2,1)}, u32[]{:S(2)}) copy-start(bf16[2,4,144,864]{3,2,1,0:T(8,128)(2,1)} %get-tuple-element.24) | copy-start | bytes 5971972
  675.9 6.2 copy-start.6
  685.0 13.0 %all-to-all-start = ((f32[8,4,144]{2,1,0:T(4,128)}), f32[8,4,144]{2,1,0:T(4,128)S(1)}, u32[]{:S(2)}, u32[]{:S(2)}) async-start(f32[8,4,144]{2,1,0:T(4,128)} %fusion.2), calls=%async_computation | async-start | bytes 65536 | tf_op jit(solution)/shard_map/all_to_all | solution.py:1401
  692.7 5.4 copy-start.9
  692.7 5.4 copy-start.10
  692.7 6.3 copy-start.8
  692.7 7.0 %copy-start.7 = (f32[128,1152]{1,0:T(8,128)S(1)}, f32[128,1152]{1,0:T(8,128)}, u32[]{:S(2)}) copy-start(f32[128,1152]{1,0:T(8,128)} %get-tuple-element.22) | copy-start | bytes 1769476
  692.7 7.8 %copy-start.1 = (bf16[1,4,1152]{2,1,0:T(4,128)(2,1)S(1)}, bf16[1,4,1152]{2,1,0:T(4,128)(2,1)}, u32[]{:S(2)}) copy-start(bf16[1,4,1152]{2,1,0:T(4,128)(2,1)} %param.16) | copy-start | bytes 27652

commit v3 on v2

--- a/solution.py
+++ b/solution.py
@@ -318,15 +318,61 @@
     def span(start, size, step=16):
         return pl.ds(pl.multiple_of(start, step), size)
 
+    ada_load = pltpu.make_async_copy(
+        r.ada.at[:, :, span(LANES * mod_start(tiles, narrow, n), mod_cols, LANES)], r.ada_v, r.ada_sem
+    )
+    hidden_own = r.up_w.shape[-1] // wide // narrow
+
+    def windows(which):
+        if which == QKV:
+            return [(width * j + cols * n, cols, 3 * LANES) for j in range(3)]
+        return [((j * narrow + n) * hidden_own, hidden_own, 2 * LANES) for j in range(wide)]
+
+    def raw(which, layer, k):
+        src, dst = ((r.qkv_w, r.qkv_raw), (r.up_w, r.up_raw))[which == UP]
+        start, _, window = windows(which)[k]
+        at = span(LANES * (start // LANES), window, LANES)
+        return pltpu.make_async_copy(
+            src.at[layer, :, at], dst.at[layer, k], r.raw_sem.at[layer, k + 3 * (which == UP)]
+        )
+
+    for layer in range(LAYERS):
+        for which in (QKV, UP):
+            for k in range(len(windows(which))):
+                raw(which, layer, k).start()
+        if layer == 0:
+            ada_load.start()
+    chosen = chosen_of(r.cond, r.cond_index)
+    lead = (chosen * jax.nn.sigmoid(chosen)).astype(BF16).astype(F32)
+    r.lead[...] = jnp.zeros_like(r.lead)
+    for row in range(wide):
+        tile = jnp.concatenate(
+            [lead[:, depth * row : depth * (row + 1)], jnp.zeros((16 - SEGS, depth), F32)], 0
+        )
+        r.lead[row] = tile.astype(BF16)
+    r.bias_tx[...] = jnp.zeros_like(r.bias_tx)
+    for layer in range(LAYERS):
+        for line, at, ref in (
+            (0, 0, r.ada_b), (1, 0, r.qkv_b), (1, 4 * LANES, r.out_b),
+            (2, 0, r.up_b), (2, 5 * LANES, r.down_b),
+        ):
+            size = ref.shape[1]
+            row = 3 * layer + line
+            r.bias_tx[row : row + 1, at : at + size] = ref[...].astype(F32)[layer : layer + 1]
+
     barrier = pltpu.get_barrier_semaphore()
     partners = [core, side, far] + [wide_peer(j) for j in range(1, wide)]
     for partner in partners:
         pl.semaphore_signal(barrier, inc=1, device_id=partner, device_id_type=MESH)
     pl.semaphore_wait(barrier, len(partners))
 
-    shards = (r.qkv_s, r.out_s, r.up_s, r.down_s)
     full = (r.qkv_h, r.out_h, r.up_h, r.down_h)
     loaded = (r.qkv_v, r.out_v, r.up_v, r.down_v)
+
+    def shard(which, layer):
+        if which == DOWN:
+            return r.down_w.at[layer, span(depth * n, depth)]
+        return (r.qkv_s, r.out_w, r.up_s)[which].at[layer]
 
     def w_rows(which, plane_idx, col):
         if which == OUT:
@@ -336,92 +382,121 @@
     def w_block(which, layer, plane_idx, col):
         return full[which].at[layer, w_rows(which, plane_idx, col)]
 
-    def w_z(which, layer, j):
+    def w_hop(which, layer, plane_idx, right, own=False):
         slot = layer * 4 + which
-        k = 0 if which == OUT else j - 1
-        return remote(
-            shards[which].at[layer], w_block(which, layer, z, x),
-            (r.wz_s.at[slot, j - 1], r.wz_r.at[slot, k]), plane(j),
-        )
-
-    def w_z_in(which, layer, j):
+        block = w_block(which, layer, plane_idx, x)
+        k = PLANES if own and not right else plane_idx
+        return remote(
+            shard(which, layer) if own else block, block,
+            (r.wz_s.at[slot, k], r.wz_r.at[slot, plane_idx]), plane(1 if right else PLANES - 1),
+        )
+
+    def w_x(which, layer, plane_idx, col, own=False):
         slot = layer * 4 + which
-        src_plane = n if which == OUT else (z - j + PLANES) % PLANES
-        k = 0 if which == OUT else j - 1
-        block = w_block(which, layer, src_plane, x)
-        return remote(block, block, (r.wz_s.at[slot, k], r.wz_r.at[slot, k]), plane(j)), src_plane
-
-    def w_x(which, layer, j, src, plane_idx, col):
-        slot = layer * 4 + which
-        return remote(
-            src, w_block(which, layer, plane_idx, col),
-            (r.wx_s.at[slot, j], r.wx_r.at[slot, j]), beside,
+        block = w_block(which, layer, plane_idx, col)
+        return remote(
+            shard(which, layer) if own else block, block,
+            (r.wx_s.at[slot, plane_idx], r.wx_r.at[slot, plane_idx]), beside,
         )
 
     def w_own(which, layer):
         return pltpu.make_async_copy(
-            shards[which].at[layer], w_block(which, layer, z, x), r.w_own.at[layer * 4 + which]
-        )
+            shard(which, layer), w_block(which, layer, z, x), r.w_own.at[layer * 4 + which]
+        )
+
+    last_plane = PLANES - 1
 
     def weights_start(which, layer):
         def go():
+            pl.when(z < last_plane)(lambda: w_hop(which, layer, z, True, True).start())
+            pl.when(z > 0)(lambda: w_hop(which, layer, z, False, True).start())
             w_own(which, layer).start()
-            for j in range(1, PLANES):
-                w_z(which, layer, j).start()
 
         if which == OUT:
             pl.when(z == n)(go)
         else:
             go()
 
-    def weights_forward(which, layer):
+    def weights_steps(which, layer):
         def own():
-            w_x(which, layer, 0, shards[which].at[layer], z, x).start()
-
-        def passed(j):
-            arrived, src_plane = w_z_in(which, layer, j)
-            arrived.wait_recv()
-            k = 0 if which == OUT else j
-            w_x(which, layer, k, w_block(which, layer, src_plane, x), src_plane, x).start()
+            w_x(which, layer, z, x, True).start()
+
+        def passed(plane_idx, right):
+            w_hop(which, layer, plane_idx, right).wait_recv()
+            onward = z < last_plane if right else z > 0
+            pl.when(onward)(lambda: w_hop(which, layer, plane_idx, right).start())
+            w_x(which, layer, plane_idx, x).start()
+
+        def first():
+            slot = layer * 4 + which + 1
+            if slot < 4 * LAYERS:
+                weights_start(slot % 4, slot // 4)
+            if which == OUT:
+                pl.when(z == n)(own)
+                pl.when(z > n)(lambda: passed(n, True))
+                pl.when(z < n)(lambda: passed(n, False))
+            else:
+                own()
+
+        def further(j):
+            pl.when(z >= j)(lambda: passed(z - j, True))
+            pl.when(z + j <= last_plane)(lambda: passed(z + j, False))
 
         if which == OUT:
+            return [first]
+        return [first] + [partial(further, j) for j in range(1, PLANES)]
+
+    steps = [
+        (layer * 4 + which, step)
+        for layer in range(LAYERS)
+        for which in (QKV, OUT, UP, DOWN)
+        for step in weights_steps(which, layer)
+    ]
+
+    def pump(count):
+        for _ in range(min(count, len(steps))):
+            steps.pop(0)[1]()
+
+    def pump_through(which, layer):
+        while steps and steps[0][0] <= layer * 4 + which:
+            pump(1)
+
+    def weights_finish(which, layer):
+        if which == OUT:
+            w_x(which, layer, n, 1 - x).wait_recv()
+            pl.when(z == n)(lambda: w_own(which, layer).wait())
+        else:
+            for j in range(PLANES):
+                w_x(which, layer, plane_of(j), 1 - x).wait_recv()
+            w_own(which, layer).wait()
+
+    def weights_drain(which, layer):
+        def own():
+            pl.when(z < last_plane)(lambda: w_hop(which, layer, z, True, True).wait_send())
+            pl.when(z > 0)(lambda: w_hop(which, layer, z, False, True).wait_send())
+
+        def passed(plane_idx, right):
+            onward = z < last_plane if right else z > 0
+            pl.when(onward)(lambda: w_hop(which, layer, plane_idx, right).wait_send())
+
+        if which == OUT:
+            w_x(which, layer, n, x).wait_send()
             pl.when(z == n)(own)
-            pl.when(z != n)(lambda: passed(1))
+            pl.when(z > n)(lambda: passed(n, True))
+            pl.when(z < n)(lambda: passed(n, False))
         else:
             own()
             for j in range(1, PLANES):
-                passed(j)
-
-    def weights_finish(which, layer):
-        if which == OUT:
-            block = w_block(which, layer, n, 1 - x)
-            w_x(which, layer, 0, block, n, 1 - x).wait_recv()
-            pl.when(z == n)(lambda: w_own(which, layer).wait())
-        else:
+                pl.when(z >= j)(lambda: passed(z - j, True))
+                pl.when(z + j <= last_plane)(lambda: passed(z + j, False))
             for j in range(PLANES):
-                src_plane = (z - j + PLANES) % PLANES
-                block = w_block(which, layer, src_plane, 1 - x)
-                w_x(which, layer, j, block, src_plane, 1 - x).wait_recv()
-            w_own(which, layer).wait()
-
-    def weights_drain(which, layer):
-        if which == OUT:
-            w_x(which, layer, 0, shards[which].at[layer], z, x).wait_send()
-
-            @pl.when(z == n)
-            def _():
-                for j in range(1, PLANES):
-                    w_z(which, layer, j).wait_send()
-        else:
-            for j in range(PLANES):
-                w_x(which, layer, j, shards[which].at[layer], z, x).wait_send()
-            for j in range(1, PLANES):
-                w_z(which, layer, j).wait_send()
+                w_x(which, layer, plane_of(j), x).wait_send()
 
     def load(which, layer):
         return pltpu.make_async_copy(full[which].at[layer], loaded[which], r.load_sem.at[which])
 
     def weights_ready(which, layer):
+        pump_through(which, layer)
         weights_finish(which, layer)
         load(which, layer).start()
         load(which, layer).wait()
@@ -504,7 +579,7 @@
             body(half * part + STEP * i)
 
     def seg_of(start):
-        return r.seg_own[span(start, STEP), :]
+        return r.seg_col[span(local * n + start, STEP), :]
 
     def mod(layer, block, seg):
         rows = r.mods[SEGS * layer : SEGS * layer + SEGS, width * block : width * (block + 1)]
@@ -518,6 +593,31 @@
         at = (slice(SEGS * layer, SEGS * layer + SEGS), slice(width * block, width * (block + 1)))
         r.mod_grad[at] += jnp.concatenate(sums, 0)
 
+    seg_cols = jnp.transpose(jnp.broadcast_to(r.seg_row[...].astype(F32), (8, narrow * local)))
+    r.seg_col[...] = seg_cols[:, :1].astype(jnp.int32)
+
+    def shifted(values, rest, size):
+        window = values.shape[1]
+        return pltpu.roll(values.astype(F32), (window - rest) % window, 1)[:, :size]
+
+    def pick(ref, start, size, window):
+        return shifted(ref[0, :, span(LANES * (start // LANES), window, LANES)], start % LANES, size)
+
+    def pack(dst, pieces):
+        at = 0
+        for piece in pieces:
+            size = piece.shape[1]
+            dst[..., at : at + size] = piece.astype(dst.dtype)
+            at += size
+
+    def pack_shard(which, layer):
+        dst, pieces = (r.qkv_s if which == QKV else r.up_s).at[layer], []
+        for k, (start, size, _) in enumerate(windows(which)):
+            raw(which, layer, k).wait()
+            buffer = r.qkv_raw if which == QKV else r.up_raw
+            pieces.append(shifted(buffer[layer, k], start % LANES, size))
+        pack(dst, pieces)
+
     def lead_copy(j, incoming=False):
         return remote(
             r.lead.at[(w + j) % wide], r.lead_rx.at[(w - j + wide) % wide if incoming else w],
@@ -526,7 +626,7 @@
 
     def bias_copy(j, incoming=False):
         return remote(
-            r.bias, r.bias_rx.at[(w - j + wide) % wide if incoming else w],
+            r.bias_tx, r.bias_rx.at[(w - j + wide) % wide if incoming else w],
             (r.bias_sem_s.at[j - 1], r.bias_sem_r.at[j - 1]), wide_peer(j),
         )
 
@@ -545,44 +645,68 @@
             (r.quarter_s.at[k], r.quarter_r.at[k]), device,
         )
 
-    ada_load = pltpu.make_async_copy(
-        r.ada.at[:, :, span(LANES * mod_start(tiles, narrow, n), mod_cols, LANES)], r.ada_v, r.ada_sem
-    )
-    ada_load.start()
     for j in range(1, wide):
         lead_copy(j).start()
+    pack_shard(QKV, 0)
     weights_start(QKV, 0)
     for j in range(1, wide):
         bias_copy(j).start()
     r.lead_rx[pl.ds(w, 1)] = r.lead[pl.ds(w, 1)]
-    r.bias_rx[pl.ds(w, 1)] = r.bias[...][None]
-    r.mod_grad[...] = jnp.zeros_like(r.mod_grad)
+    r.bias_rx[pl.ds(w, 1)] = r.bias_tx[...][None]
     ada_load.wait()
     for j in range(1, wide):
         lead_copy(j, True).wait_recv()
     lead_all = r.lead_rx[...].reshape(wide * 16, depth)
     for layer in range(LAYERS):
         product = dot(lead_all, r.ada_v[layer], ((1,), (0,)))
-        at = slice(SEGS * layer, SEGS * layer + SEGS)
         for row in range(wide):
-            r.mod_tx[row, at, :] = product[16 * row : 16 * row + SEGS] + r.ada_bias[at, :]
+            at = slice(SEGS * layer, SEGS * layer + SEGS)
+            r.mod_tx[row, at, :] = product[16 * row : 16 * row + SEGS]
     for j in range(1, wide):
         mod_copy(j).start()
     r.mod_rx[pl.ds(w, 1)] = r.mod_tx[pl.ds(w, 1)]
+    for which, layer in ((UP, 0), (QKV, 1), (UP, 1)):
+        pack_shard(which, layer)
+    pump_through(QKV, 0)
+    r.mod_grad[...] = jnp.zeros_like(r.mod_grad)
+    r.lead_t[...] = jnp.zeros_like(r.lead_t)
     for layer in range(LAYERS):
-        for which in (QKV, OUT, UP, DOWN):
-            if (which, layer) != (QKV, 0):
-                weights_start(which, layer)
-    weights_forward(QKV, 0)
+        for row in range(wide):
+            at = (row * LAYERS + layer) * SEGS
+            r.lead_t[layer, at : at + SEGS, :] = r.lead_rx[row].astype(F32)[:SEGS]
+        r.lead_o[layer] = jnp.transpose(r.lead_t[layer]).astype(BF16)
+
+    for j in range(1, wide):
+        bias_copy(j, True).wait_recv()
+    for row in range(wide):
+        for line, at, ref in (
+            (0, 0, r.ada_full), (1, 0, r.qkv_full), (1, 4 * LANES, r.out_full),
+            (2, 0, r.up_full), (2, 5 * LANES, r.down_full),
+        ):
+            size = ref.shape[-1] // wide
+            for layer in range(LAYERS):
+                piece = r.bias_rx[row, 3 * layer + line : 3 * layer + line + 1, at : at + size]
+                ref[0, layer : layer + 1, size * row : size * (row + 1)] = piece
+    for which, ref in ((QKV, r.qkv_full), (UP, r.up_full)):
+        pieces = [pick(ref, *window) for window in windows(which)]
+        for layer in range(LAYERS):
+            at = 4 * layer + which
+            pack(r.bias_sum.at[at : at + 1], [piece[layer : layer + 1] for piece in pieces])
+    for layer in range(LAYERS):
+        at = 4 * layer
+        r.bias_sum[at + OUT : at + OUT + 1] = r.out_full[0, layer : layer + 1]
+        r.bias_sum[at + DOWN : at + DOWN + 1] = r.down_full[0, layer : layer + 1]
+
     for j in range(1, wide):
         mod_copy(j, True).wait_recv()
-    r.mod_q[pl.ds(n, 1)] = jnp.sum(r.mod_rx[...], 0, keepdims=True)
+    ada_own = r.ada_full[0, :, span(LANES * mod_start(tiles, narrow, n), mod_cols, LANES)]
+    total = jnp.sum(r.mod_rx[...], 0)
+    for layer in range(LAYERS):
+        at = slice(SEGS * layer, SEGS * layer + SEGS)
+        r.mod_q[pl.ds(n, 1), at, :] = (total[at] + ada_own[layer : layer + 1])[None]
     for k in range(3):
         quarter_copy(k).start()
-    weights_forward(OUT, 0)
-    for j in range(1, wide):
-        bias_copy(j, True).wait_recv()
-    r.bias_sum[...] = jnp.sum(r.bias_rx[...], 0)
+    pump(2)
     for k in range(3):
         quarter_copy(k, True).wait_recv()
     for part in range(narrow):
@@ -631,6 +755,9 @@
                 r.mixed[layer, rows, HEAD * head : HEAD * (head + 1)] = mixed.astype(BF16)
                 r.log_sum[layer, rows, head : head + 1] = top + jnp.log(total)
 
+            if head % 2:
+                pump(1)
+
     def mlp_block(layer, block):
         rows = block_rows(block)
         hidden = r.hid_mlp[layer, rows, :]
@@ -650,7 +777,7 @@
         def take(start, seg):
             rows = span(start, STEP)
             branch = sum_take(start) + bias_row(layer, OUT, width)
-            r.branch[layer, rows, :] = branch
+            r.branch[layer, rows, :] = branch.astype(BF16)
             middle = state_of(layer, start) + mod(layer, 2, seg) * branch
             r.middle[layer, rows, :] = middle
             return middle
@@ -661,7 +788,7 @@
         def take(start, seg):
             rows = span(start, STEP)
             down = sum_take(start) + bias_row(layer, DOWN, width)
-            r.down[layer, rows, :] = down
+            r.down[layer, rows, :] = down.astype(BF16)
             result = r.middle[layer, rows, :] + mod(layer, 5, seg) * down
             if layer == 0:
                 r.state[rows, :] = result
@@ -677,13 +804,13 @@
             gather_norm(0, hid, 0, 1, lambda start, seg: state_of(0, start), lambda part: None)
         else:
             gather_norm(layer, hid, 0, 1, after_mlp(layer - 1), sum_wait)
+        pump(1)
         weights_ready(QKV, layer)
         tok_own(hid)
         qkv_block(layer, 1)
         tok_other(hid)
         qkv_block(layer, 0)
-        if layer == 1:
-            weights_forward(OUT, 1)
+        pump(1)
         attend(layer)
         weights_ready(OUT, layer)
         tok_drain(hid)
@@ -692,22 +819,22 @@
             sum_block(block)
             if block == 0:
                 sum_cross()
-        weights_forward(UP, layer)
+        pump(1)
         hid = r.hid_mlp.at[layer]
         gather_norm(layer, hid, 3, 4, after_attn(layer), sum_wait)
+        pump(1)
         weights_ready(UP, layer)
-        weights_forward(DOWN, layer)
         weights_ready(DOWN, layer)
         tok_own(hid)
         mlp_block(layer, 1)
         sum_block(1)
+        pump(1)
         tok_other(hid)
         mlp_block(layer, 0)
         sum_block(0)
         sum_cross()
         tok_drain(hid)
-        if layer == 0:
-            weights_forward(QKV, 1)
+        pump(1)
     for part in range(2):
         sum_wait(part)
         finish = after_mlp(LAYERS - 1)
@@ -803,7 +930,9 @@
             total = sums[which][rows, :].astype(F32)
             for j in range(PLANES - 1):
                 total = total + from_z[which][j].astype(F32)
-            final[which][layer] = total.astype(BF16)
+            if layer == 0:
+                spread_sent(which, 1)
+            final[which][...] = total.astype(BF16)
             if layer == 1:
                 for j in range(1, PLANES):
                     pl.semaphore_signal(
@@ -827,14 +956,19 @@
             dst = grads_o[which].at[layer]
         else:
             dst = grads_o[which].at[layer, n if source is None else source]
-        src = final[which].at[layer] if kind < 2 else dst
+        src = final[which] if kind < 2 else dst
         return remote(
             src, dst, (r.spread_s.at[slot, kind], r.spread_r.at[slot, kind]), side if kind == 1 else core
         )
 
     def spread_own(which, layer):
         dst = grads_o[which].at[layer] if which == OUT else grads_o[which].at[layer, n]
-        return pltpu.make_async_copy(final[which].at[layer], dst, r.spread_l.at[layer * 4 + which])
+        return pltpu.make_async_copy(final[which], dst, r.spread_l.at[layer * 4 + which])
+
+    def spread_sent(which, layer):
+        spread(which, layer, 1).wait_send()
+        spread(which, layer, 0).wait_send()
+        spread_own(which, layer).wait()
 
     def grad_spread(which, layer):
         def go():
@@ -859,12 +993,8 @@
 
     def grad_end(which, layer):
         if which == OUT:
-
-            @pl.when(jnp.logical_and(same_y, same_c))
-            def _():
-                spread(which, layer, 1).wait_send()
-                spread(which, layer, 0).wait_send()
-                spread_own(which, layer).wait()
+            if layer == 0:
+                pl.when(jnp.logical_and(same_y, same_c))(lambda: spread_sent(which, layer))
 
             @pl.when(jnp.logical_and(jnp.logical_not(same_y), same_c))
             def _():
@@ -881,9 +1011,8 @@
             spread(which, layer, 0, n_core).wait_recv()
             spread(which, layer, 2, n_far).wait_recv()
             spread(which, layer, 2, n_side).wait_send()
-            spread(which, layer, 1).wait_send()
-            spread(which, layer, 0).wait_send()
-            spread_own(which, layer).wait()
+            if layer == 0:
+                spread_sent(which, layer)
 
     def bias_grad(layer, which, values):
         at = 4 * layer + which
@@ -943,7 +1072,7 @@
     for part in range(2):
         def first(start):
             rows = span(start, STEP)
-            r.grad[rows, :] = r.cot[rows, :].astype(F32)
+            r.token_o[rows, :] = r.cot[rows, :].astype(F32)
 
         each_step(part, first)
 
@@ -964,10 +1093,10 @@
                     grad_hidden = sum_take(start)
                     unit, inv = norm(state_of(older, start))
                     r.grad_hid[rows, :] = grad_hidden
-                    r.grad[rows, :] += norm_back(
+                    r.token_o[rows, :] += norm_back(
                         grad_hidden * (1.0 + mod(older, 1, seg)), unit, inv
                     )
-                grad_down = (mod(layer, 5, seg) * r.grad[rows, :]).astype(BF16)
+                grad_down = (mod(layer, 5, seg) * r.token_o[rows, :]).astype(BF16)
                 r.grad_down[span(local * n + start, STEP), :] = grad_down
 
             each_step(part, start_down)
@@ -991,7 +1120,7 @@
 
         def sums_gate_mlp(start):
             rows = span(start, STEP)
-            mod_sum(layer, 5, seg_of(start), r.down[layer, rows, :] * r.grad[rows, :])
+            mod_sum(layer, 5, seg_of(start), r.down[layer, rows, :].astype(F32) * r.token_o[rows, :])
 
         both(sums_gate_mlp)
         bias_grad(layer, DOWN, r.grad_down[span(local * n, local), :])
@@ -1024,10 +1153,10 @@
                 grad_hidden = sum_take(start)
                 unit, inv = norm(r.middle[layer, rows, :])
                 r.grad_hid[rows, :] = grad_hidden
-                grad = r.grad[rows, :] + norm_back(
+                grad = r.token_o[rows, :] + norm_back(
                     grad_hidden * (1.0 + mod(layer, 4, seg)), unit, inv
                 )
-                r.grad[rows, :] = grad
+                r.token_o[rows, :] = grad
                 grad_branch = (mod(layer, 2, seg) * grad).astype(BF16)
                 r.grad_branch[span(local * n + start, STEP), :] = grad_branch
 
@@ -1041,7 +1170,7 @@
             grad_hidden = r.grad_hid[rows, :]
             mod_sum(layer, 3, seg, grad_hidden)
             mod_sum(layer, 4, seg, grad_hidden * unit)
-            mod_sum(layer, 2, seg, r.branch[layer, rows, :] * r.grad[rows, :])
+            mod_sum(layer, 2, seg, r.branch[layer, rows, :].astype(F32) * r.token_o[rows, :])
 
         both(sums_mlp)
         bias_grad(layer, OUT, r.grad_branch[span(local * n, local), :])
@@ -1088,7 +1217,7 @@
             seg = seg_of(start)
             grad_hidden = sum_take(start)
             unit, inv = norm(state_of(0, start))
-            grad = r.grad[rows, :] + norm_back(grad_hidden * (1.0 + mod(0, 1, seg)), unit, inv)
+            grad = r.token_o[rows, :] + norm_back(grad_hidden * (1.0 + mod(0, 1, seg)), unit, inv)
             r.token_o[rows, :] = grad
             mod_sum(0, 0, seg, grad_hidden)
             mod_sum(0, 1, seg, grad_hidden * unit)
@@ -1126,6 +1255,19 @@
         return remote(
             r.mod_all, r.mod_o.at[idx if incoming else n],
             (r.mod_narrow_s.at[k], r.mod_narrow_r.at[k]), device,
+        )
+
+    def lead_back(j, incoming=False):
+        return remote(
+            r.lead_tx.at[(w + j) % wide], r.lead_back.at[(w - j + wide) % wide if incoming else w],
+            (r.lead_back_s.at[j - 1], r.lead_back_r.at[j - 1]), wide_peer(j),
+        )
+
+    def lead_narrow(k, incoming=False):
+        device, idx = narrow_peers[k]
+        return remote(
+            r.lead_back, r.lead_g.at[idx if incoming else n],
+            (r.lead_narrow_s.at[k], r.lead_narrow_r.at[k]), device,
         )
 
     for k in range(3):
@@ -1155,11 +1297,21 @@
     grad_beside(QKV, 0)
     for j in range(1, wide):
         wide_back(j, True).wait_recv()
-    r.mod_all[...] = r.quarter_all[...].reshape(wide * 2 * SEGS, mod_cols).astype(BF16)
+    r.mod_all[...] = r.quarter_all[...].reshape(wide * LAYERS * SEGS, mod_cols).astype(BF16)
     mod_own = pltpu.make_async_copy(r.mod_all, r.mod_o.at[n], r.mod_own_sem)
     mod_own.start()
     for k in range(3):
         mod_narrow(k).start()
+    owned = LANES * (mod_start(tiles, narrow, n + 1) - mod_start(tiles, narrow, n))
+    lane = lax.broadcasted_iota(jnp.int32, r.mod_all.shape, 1)
+    own_grads = jnp.where(lane < owned, r.mod_all[...].astype(F32), 0.0).astype(BF16)
+    lead_parts = [dot(own_grads, r.ada_v[layer], ((1,), (1,))) for layer in range(LAYERS)]
+    for row in range(wide):
+        at = row * LAYERS * SEGS
+        r.lead_tx[row] = lead_parts[0][at : at + SEGS] + lead_parts[1][at + SEGS : at + 2 * SEGS]
+    for j in range(1, wide):
+        lead_back(j).start()
+    r.lead_back[pl.ds(w, 1)] = r.lead_tx[pl.ds(w, 1)]
     for j in range(1, wide):
         bias_wide(j, True).wait_recv()
     r.bias_row[...] = jnp.sum(r.bias_all[...], 0)
@@ -1167,6 +1319,12 @@
     bias_own.start()
     for k in range(3):
         bias_narrow(k).start()
+    for j in range(1, wide):
+        lead_back(j, True).wait_recv()
+    lead_own = pltpu.make_async_copy(r.lead_back, r.lead_g.at[n], r.lead_own_sem)
+    lead_own.start()
+    for k in range(3):
+        lead_narrow(k).start()
     grad_planes(UP, 0)
     grad_spread(UP, 0)
     grad_planes(OUT, 0)
@@ -1182,14 +1340,16 @@
             weights_drain(which, layer)
             grad_end(which, layer)
     for j in range(1, wide):
-        for copy in (lead_copy, bias_copy, mod_copy, wide_back, bias_wide):
+        for copy in (lead_copy, bias_copy, mod_copy, wide_back, bias_wide, lead_back):
             copy(j).wait_send()
     for k in range(3):
-        for copy in (quarter_copy, quarter_back, mod_narrow, bias_narrow):
+        for copy in (quarter_copy, quarter_back, mod_narrow, bias_narrow, lead_narrow):
             copy(k).wait_send()
         mod_narrow(k, True).wait_recv()
         bias_narrow(k, True).wait_recv()
+        lead_narrow(k, True).wait_recv()
     mod_own.wait()
+    lead_own.wait()
     bias_own.wait()
 
 
@@ -1198,6 +1358,143 @@
     bent = jnp.tanh(rate * (values + 0.044715 * values * values * values))
     inner = rate * (1.0 + 3.0 * 0.044715 * values * values)
     return 0.5 * (1.0 + bent) + 0.5 * values * (1.0 - bent * bent) * inner
+
+
+def chosen_of(cond, index):
+    values = cond[...].astype(F32)
+    rows = index[...]
+    chosen = jnp.zeros(values.shape, F32)
+    for k in range(SEGS):
+        chosen = jnp.where(rows == k, values[k : k + 1], chosen)
+    return chosen
+
+
+def finish_kernel(cfg, *refs):
+    r = SimpleNamespace(**dict(zip(cfg.names, refs)))
+    wide, narrow, width, depth, cols = cfg.wide, cfg.narrow, cfg.width, cfg.depth, cfg.cols
+    tiles, hidden_own = cfg.tiles, cfg.hidden_own
+    w = lax.axis_index("wide")
+
+    for part in range(narrow):
+        values = r.qkv_i[0, part].astype(F32)
+        for j in range(3):
+            at = width * j + cols * part
+            r.qkv_g[0, :, at : at + cols] = values[:, cols * j : cols * (j + 1)]
+        values = r.up_i[0, part].astype(F32)
+        for j in range(wide):
+            at = (j * narrow + part) * hidden_own
+            r.up_g[0, :, at : at + hidden_own] = values[:, hidden_own * j : hidden_own * (j + 1)]
+        at, end = [LANES * mod_start(tiles, narrow, part + k) for k in range(2)]
+        r.ada_g[0, :, at:end] = dot(r.lead_i[0], r.mod_i[part, :, : end - at], ((1,), (0,)))
+    r.out_g[...] = r.out_i[...].astype(F32)
+    r.down_g[...] = r.down_i[...].astype(F32)
+
+    def pick(ref, size):
+        start = size * w
+        window = LANES * (-(-size // LANES) + 1)
+        tile, rest = start // LANES, start % LANES
+        values = ref[:, pl.ds(pl.multiple_of(LANES * tile, LANES), window)]
+        return pltpu.roll(values, (window - rest) % window, 1)[:, :size]
+
+    @pl.when(pl.program_id(0) + pl.program_id(1) == 0)
+    def _():
+        for part in range(narrow):
+            values = r.bias_i[part]
+            for j in range(3):
+                at = width * j + cols * part
+                r.qkv_t[:, at : at + cols] = values[:, cols * j : cols * (j + 1)]
+            for j in range(wide):
+                at = (j * narrow + part) * hidden_own
+                r.up_t[:, at : at + hidden_own] = values[:, hidden_own * j : hidden_own * (j + 1)]
+            at, end = [LANES * mod_start(tiles, narrow, part + k) for k in range(2)]
+            values = r.mod_i[part, :, : end - at].astype(F32)
+            layer_of = lax.broadcasted_iota(jnp.int32, values.shape, 0) // SEGS % LAYERS
+            for layer in range(LAYERS):
+                sums = jnp.sum(jnp.where(layer_of == layer, values, 0.0), 0, keepdims=True)
+                r.ada_t[layer : layer + 1, at:end] = sums
+        r.row_t[:, :width] = jnp.sum(r.bias_i[...], 0)
+        for dst, ref, line, step in (
+            (r.ada_bg, r.ada_t, 0, 1), (r.qkv_bg, r.qkv_t, QKV, 4), (r.out_bg, r.row_t, OUT, 4),
+            (r.up_bg, r.up_t, UP, 4), (r.down_bg, r.row_t, DOWN, 4),
+        ):
+            values = pick(ref, dst.shape[1])
+            for layer in range(LAYERS):
+                at = step * layer + line
+                dst[layer : layer + 1, :] = values[at : at + 1]
+        chosen = chosen_of(r.cond, r.cond_index)
+        gate = jax.nn.sigmoid(chosen)
+        slope = gate * (1.0 + chosen * (1.0 - gate))
+        lead_grad = jnp.sum(r.lead_i2[...], 0)
+        for row in range(wide):
+            at = slice(depth * row, depth * (row + 1))
+            grad = lead_grad[row] * slope[:, at]
+            for k in range(SEGS):
+                r.cond_g[k : k + 1, at] = jnp.sum(
+                    jnp.where(r.cond_index[...] == k, grad, 0.0), 0, keepdims=True
+                )
+
+
+def finish(wide, narrow, got, cond, cond_index, tiles, mod_cols, w):
+    width = cond.shape[1]
+    depth, cols = width // wide, width // narrow
+    hidden_own = got["up_o"].shape[-1] // wide
+    hidden_all = got["up_o"].shape[-1] * narrow
+    down_rows = narrow * hidden_own
+    bands = depth // 16
+    shape, vmem = jax.ShapeDtypeStruct, pltpu.VMEM
+
+    def whole(values):
+        return pl.BlockSpec(values.shape, lambda i, j: (0,) * values.ndim)
+
+    def band(*dims):
+        return pl.BlockSpec(
+            (1, *dims), lambda i, j: (i, 0, j, 0) if len(dims) == 3 else (i, j, 0)
+        )
+
+    down_i = got["down_o"].reshape(LAYERS, down_rows, width)
+    inputs = dict(
+        qkv_i=got["qkv_o"], up_i=got["up_o"], out_i=got["out_o"], down_i=down_i,
+        lead_i=got["lead_o"], mod_i=got["mod_o"], bias_i=got["bias_o"], lead_i2=got["lead_g"],
+        cond=cond, cond_index=cond_index,
+    )
+    in_specs = [
+        band(narrow, 16, 3 * cols), band(narrow, 16, wide * hidden_own), band(16, width),
+        band(down_rows // bands, width), band(16, got["lead_o"].shape[-1]),
+        *[whole(inputs[name]) for name in ("mod_i", "bias_i", "lead_i2", "cond", "cond_index")],
+    ]
+    outputs = dict(
+        ada_g=shape((LAYERS, depth, tiles * LANES), F32), qkv_g=shape((LAYERS, depth, 3 * width), F32),
+        out_g=shape((LAYERS, depth, width), F32), up_g=shape((LAYERS, depth, hidden_all), F32),
+        down_g=shape((LAYERS, down_rows, width), F32),
+        ada_bg=shape((LAYERS, tiles * LANES // wide), F32), qkv_bg=shape((LAYERS, 3 * width // wide), F32),
+        out_bg=shape((LAYERS, depth), F32), up_bg=shape((LAYERS, hidden_all // wide), F32),
+        down_bg=shape((LAYERS, depth), F32), cond_g=shape((SEGS, width), F32),
+    )
+    out_specs = [
+        band(16, tiles * LANES), band(16, 3 * width), band(16, width), band(16, hidden_all),
+        band(down_rows // bands, width),
+        *[whole(outputs[name]) for name in ("ada_bg", "qkv_bg", "out_bg", "up_bg", "down_bg", "cond_g")],
+    ]
+    scratch = dict(
+        ada_t=vmem((8, (tiles + 2) * LANES), F32), qkv_t=vmem((8, 3 * width + 2 * LANES), F32),
+        up_t=vmem((8, hidden_all + 2 * LANES), F32), row_t=vmem((8, width + 2 * LANES), F32),
+    )
+    cfg = SimpleNamespace(
+        names=[*inputs, *outputs, *scratch], wide=wide, narrow=narrow, width=width, depth=depth,
+        cols=cols, tiles=tiles, hidden_own=hidden_own,
+    )
+    results = pl.pallas_call(
+        partial(finish_kernel, cfg),
+        grid=(LAYERS, bands),
+        out_shape=list(outputs.values()), in_specs=in_specs, out_specs=out_specs,
+        scratch_shapes=list(scratch.values()),
+        compiler_params=pltpu.CompilerParams(vmem_limit_bytes=48 * 2**20),
+    )(*inputs.values())
+    done = dict(zip(outputs, results))
+    out = [got["mixed_o"][None], got["token_o"][None], done["cond_g"][None]]
+    for name in ("ada", "qkv", "out", "up", "down"):
+        out += [done[name + "_g"], done[name + "_bg"]]
+    return tuple(out)
 
 
 def fused_device(
@@ -1216,52 +1513,12 @@
     tiles = ada_weight.shape[-1] // LANES
     mod_cols = LANES * -(-tiles // narrow)
 
-    def own(values, axis):
-        return lax.dynamic_index_in_dim(values, n, axis, keepdims=False)
-
-    def placed(values):
-        spot = jnp.arange(wide)[None, :, None] == w
-        return jnp.where(spot, values.astype(F32)[:, None, :], 0.0).reshape(LAYERS, -1)
-
-    ada_b = lax.dynamic_slice_in_dim(
-        placed(ada_bias), LANES * mod_start(tiles, narrow, n), mod_cols, 1
-    )
-    ada_b = jnp.repeat(ada_b, SEGS, axis=0)
-    qkv_b = own(placed(qkv_bias).reshape(LAYERS, 3, narrow, cols), 2).reshape(LAYERS, -1)
-    qkv_b = jnp.pad(qkv_b, ((0, 0), (0, width - 3 * cols)))
-    up_b = own(placed(up_bias).reshape(LAYERS, wide, narrow, hidden_own), 2).reshape(LAYERS, -1)
-    bias = jnp.stack([qkv_b, placed(out_bias), up_b, placed(down_bias)], 1).reshape(-1, width)
-
-    cond_hot = (cond_index[0, :, None] == jnp.arange(SEGS, dtype=jnp.int32)[None, :]).astype(F32)
-    chosen = jnp.dot(cond_hot, cond[0].astype(F32), precision=EXACT)
-    lead = (chosen * jax.nn.sigmoid(chosen)).astype(BF16)
-    lead = lead.reshape(SEGS, wide, depth).transpose(1, 0, 2)
-    lead = jnp.pad(lead, ((0, 0), (0, 16 - SEGS), (0, 0)))
-
-    seg_row = seg_ids[0]
-    seg_own = lax.dynamic_slice_in_dim(seg_row, n * local, local, 0)
-
-    qkv_own = jnp.concatenate(
-        [
-            lax.dynamic_slice_in_dim(qkv_weight, width * j + n * cols, cols, 2) for j in range(3)
-        ],
-        axis=2,
-    )
-    up_own = jnp.concatenate(
-        [
-            lax.dynamic_slice_in_dim(up_weight, (j * narrow + n) * hidden_own, hidden_own, 2)
-            for j in range(wide)
-        ],
-        axis=2,
-    )
-    down_own = lax.dynamic_slice_in_dim(down_weight, n * hidden_own, hidden_own, 1)
-
     inputs = dict(
-        tok=tokens[0], lead=lead, bias=bias, ada_bias=ada_b,
-        seg_own=seg_own[:, None], seg_col=seg_row[:, None], seg_row=seg_row[None, :],
-        cot=cotangent[0], ada=ada_weight, qkv_s=qkv_own, out_s=out_weight, up_s=up_own, down_s=down_own,
-    )
-    in_hbm = ("ada", "qkv_s", "out_s", "up_s", "down_s")
+        tok=tokens[0], cond=cond[0], cond_index=cond_index.reshape(SEGS, 1), seg_row=seg_ids,
+        cot=cotangent[0], ada_b=ada_bias, qkv_b=qkv_bias, out_b=out_bias, up_b=up_bias, down_b=down_bias,
+        ada=ada_weight, qkv_w=qkv_weight, out_w=out_weight, up_w=up_weight, down_w=down_weight,
+    )
+    in_hbm = ("ada", "qkv_w", "out_w", "up_w", "down_w")
     shape = jax.ShapeDtypeStruct
     outputs = dict(
         mixed_o=shape((local, width), BF16), token_o=shape((local, width), F32),
@@ -1271,10 +1528,12 @@
         down_o=shape((LAYERS, narrow, hidden_own, width), BF16),
         bias_o=shape((narrow, 4 * LAYERS, width), F32),
         mod_o=shape((narrow, wide * LAYERS * SEGS, mod_cols), BF16),
+        lead_o=shape((LAYERS, depth, wide * LAYERS * SEGS), BF16),
+        lead_g=shape((narrow, wide, SEGS, depth), F32),
         qkv_h=shape((LAYERS, width, 3 * cols), BF16), out_h=shape((LAYERS, cols, width), BF16),
         up_h=shape((LAYERS, width, hidden), BF16), down_h=shape((LAYERS, hidden, width), BF16),
     )
-    out_vmem = ("mixed_o", "token_o")
+    out_vmem = ("mixed_o", "token_o", "lead_o")
     vmem, dma = pltpu.VMEM, pltpu.SemaphoreType.DMA
     heads = cols // HEAD
     scratch = dict(
@@ -1285,8 +1544,8 @@
         mixed=vmem((LAYERS, row_len, cols), BF16), log_sum=vmem((LAYERS, row_len, heads), F32),
         up=vmem((LAYERS, row_len, hidden), BF16), act=vmem((LAYERS, row_len, hidden), BF16),
         state=vmem((local, width), F32), middle=vmem((LAYERS, local, width), F32),
-        branch=vmem((LAYERS, local, width), F32), down=vmem((LAYERS, local, width), F32),
-        grad=vmem((local, width), F32), grad_hid=vmem((local, width), F32),
+        branch=vmem((LAYERS, local, width), BF16), down=vmem((LAYERS, local, width), BF16),
+        grad_hid=vmem((local, width), F32),
         grad_down=vmem((row_len, width), BF16), grad_branch=vmem((row_len, width), BF16),
         grad_up=vmem((row_len, hidden), BF16), grad_qkv=vmem((row_len, 3 * cols), BF16),
         grad_heads=vmem((heads, row_len, LANES), BF16),
@@ -1295,7 +1554,15 @@
         core_tx=vmem((2, local, width), BF16), core_rx=vmem((2, local, width), BF16),
         side_tx=vmem((local, width), BF16), side_rx=vmem((local, width), BF16),
         ada_v=vmem((LAYERS, depth, mod_cols), BF16),
-        lead_rx=vmem((wide, 16, depth), BF16), bias_rx=vmem((wide, 4 * LAYERS, width), F32),
+        lead=vmem((wide, 16, depth), BF16), lead_rx=vmem((wide, 16, depth), BF16),
+        bias_tx=vmem((8, 7 * LANES), F32), bias_rx=vmem((wide, 8, 7 * LANES), F32),
+        ada_full=vmem((1, LAYERS, tiles * LANES), F32), qkv_full=vmem((1, LAYERS, 3 * width), F32),
+        out_full=vmem((1, LAYERS, width), F32), up_full=vmem((1, LAYERS, narrow * hidden), F32),
+        down_full=vmem((1, LAYERS, width), F32), seg_col=vmem((row_len, 1), jnp.int32),
+        qkv_raw=vmem((LAYERS, 3, depth, 3 * LANES), BF16), up_raw=vmem((LAYERS, wide, depth, 2 * LANES), BF16),
+        qkv_s=vmem((LAYERS, depth, 3 * cols), BF16), up_s=vmem((LAYERS, depth, hidden), BF16),
+        lead_t=vmem((LAYERS, wide * LAYERS * SEGS, depth), F32),
+        lead_tx=vmem((wide, SEGS, depth), F32), lead_back=vmem((wide, SEGS, depth), F32),
         bias_sum=vmem((4 * LAYERS, width), F32),
         mod_tx=vmem((wide, LAYERS * SEGS, mod_cols), F32), mod_rx=vmem((wide, LAYERS * SEGS, mod_cols), F32),
         mod_q=vmem((narrow, LAYERS * SEGS, mod_cols), F32),
@@ -1313,14 +1580,16 @@
         up_xr=vmem((PLANES, depth, hidden), BF16), down_xr=vmem((PLANES, hidden_own, width), BF16),
         qkv_zr=vmem((PLANES - 1, depth, 3 * cols), BF16), out_zr=vmem((PLANES - 1, depth, width), BF16),
         up_zr=vmem((PLANES - 1, depth, hidden), BF16), down_zr=vmem((PLANES - 1, hidden_own, width), BF16),
-        qkv_f=vmem((LAYERS, depth, 3 * cols), BF16), out_f=vmem((LAYERS, depth, width), BF16),
-        up_f=vmem((LAYERS, depth, hidden), BF16), down_f=vmem((LAYERS, hidden_own, width), BF16),
-        wz_s=dma((8, 3)), wz_r=dma((8, 3)), wx_s=dma((8, 4)), wx_r=dma((8, 4)), w_own=dma((8,)),
+        qkv_f=vmem((depth, 3 * cols), BF16), out_f=vmem((depth, width), BF16),
+        up_f=vmem((depth, hidden), BF16), down_f=vmem((hidden_own, width), BF16),
+        wz_s=dma((8, 5)), wz_r=dma((8, 4)), wx_s=dma((8, 4)), wx_r=dma((8, 4)), w_own=dma((8,)),
         load_sem=dma((4,)), tok_s=dma((6,)), tok_r=dma((6,)), sum_s=dma((4,)), sum_r=dma((4,)),
         lead_sem_s=dma((wide - 1,)), lead_sem_r=dma((wide - 1,)),
         bias_sem_s=dma((wide - 1,)), bias_sem_r=dma((wide - 1,)),
         mod_sem_s=dma((wide - 1,)), mod_sem_r=dma((wide - 1,)),
-        quarter_s=dma((3,)), quarter_r=dma((3,)), ada_sem=dma,
+        quarter_s=dma((3,)), quarter_r=dma((3,)), ada_sem=dma, raw_sem=dma((LAYERS, 3 + wide)), lead_own_sem=dma,
+        lead_back_s=dma((wide - 1,)), lead_back_r=dma((wide - 1,)),
+        lead_narrow_s=dma((3,)), lead_narrow_r=dma((3,)),
         dx_s=dma((4, 4)), dx_r=dma((4, 4)), dz_s=dma((4, 3)), dz_r=dma((4, 3)),
         spread_s=dma((8, 3)), spread_r=dma((8, 3)), spread_l=dma((8,)),
         back_s=dma((3,)), back_r=dma((3,)),
@@ -1345,68 +1614,12 @@
         out_specs=[place(name, name in out_vmem) for name in outputs],
         scratch_shapes=list(scratch.values()),
         compiler_params=pltpu.CompilerParams(
-            collective_id=0, has_side_effects=True, vmem_limit_bytes=62 * 2**20
+            collective_id=0, has_side_effects=True, vmem_limit_bytes=63 * 2**20
         ),
     )(*inputs.values())
     got = dict(zip(outputs, results))
 
-    qkv_g = got["qkv_o"].reshape(LAYERS, narrow, depth, 3, cols).transpose(0, 2, 3, 1, 4)
-    up_g = got["up_o"].reshape(LAYERS, narrow, depth, wide, hidden_own).transpose(0, 2, 3, 1, 4)
-    weight_grads = (
-        qkv_g.reshape(LAYERS, depth, -1).astype(F32),
-        got["out_o"].astype(F32),
-        up_g.reshape(LAYERS, depth, -1).astype(F32),
-        got["down_o"].reshape(LAYERS, -1, width).astype(F32),
-    )
-
-    bias_g = got["bias_o"].reshape(narrow, LAYERS, 4, width)
-    qkv_bg = bias_g[:, :, QKV, : 3 * cols].reshape(narrow, LAYERS, 3, cols).transpose(1, 2, 0, 3)
-    up_bg = bias_g[:, :, UP].reshape(narrow, LAYERS, wide, hidden_own).transpose(1, 2, 0, 3)
-    full_biases = (
-        qkv_bg.reshape(LAYERS, -1), jnp.sum(bias_g[:, :, OUT], 0),
-        up_bg.reshape(LAYERS, -1), jnp.sum(bias_g[:, :, DOWN], 0),
-    )
-    bias_grads = [
-        lax.dynamic_slice_in_dim(item, w * (item.shape[1] // wide), item.shape[1] // wide, 1)
-        for item in full_biases
-    ]
-
-    mod_parts = []
-    for part in range(narrow):
-        size = mod_start(tiles, narrow, part + 1) - mod_start(tiles, narrow, part)
-        mod_parts.append(got["mod_o"][part, :, : LANES * size])
-    mod_all = jnp.concatenate(mod_parts, axis=1).reshape(wide, LAYERS, SEGS, -1)
-    mod_all = mod_all.transpose(1, 0, 2, 3).reshape(LAYERS, wide * SEGS, -1)
-    return weight_grads, bias_grads, mod_all, got["mixed_o"], got["token_o"], chosen, cond_hot
-
-
-def fused_program(wide, narrow, *args):
-    tokens, cond, seg_ids, cond_index, cotangent, ada_weight, ada_bias = args[:7]
-    w = lax.axis_index("wide")
-    width = tokens.shape[-1]
-    depth = width // wide
-    weight_grads, bias_grads, mod_all, mixed, token_grad, chosen, cond_hot = fused_device(
-        wide, narrow, *args
-    )
-    lead = (chosen * jax.nn.sigmoid(chosen)).astype(BF16)
-    lead_own = lax.all_to_all(
-        lead.reshape(SEGS, wide, depth).transpose(1, 0, 2), "wide", 0, 0, tiled=False
-    ).reshape(wide * SEGS, depth)
-    ada_grad = jnp.einsum("nd,lne->lde", lead_own, mod_all, preferred_element_type=F32)
-    ada_size = ada_bias.shape[1]
-    ada_bias_grad = jnp.sum(
-        lax.dynamic_slice_in_dim(mod_all, w * ada_size, ada_size, 2).astype(F32), axis=1
-    )
-    lead_grad = jnp.einsum("lne,lde->nd", mod_all, ada_weight, preferred_element_type=F32)
-    lead_grad = lax.all_to_all(lead_grad.reshape(wide, SEGS, depth), "wide", 0, 0, tiled=False)
-    lead_grad = lead_grad.transpose(1, 0, 2).reshape(SEGS, width)
-    gate = jax.nn.sigmoid(chosen)
-    chosen_grad = lead_grad * (gate * (1.0 + chosen * (1.0 - gate)))
-    cond_grad = jnp.dot(cond_hot.T, chosen_grad, precision=EXACT)
-    out = [mixed[None], token_grad[None], cond_grad[None], ada_grad, ada_bias_grad]
-    for weight, bias in zip(weight_grads, bias_grads):
-        out += [weight, bias]
-    return tuple(out)
+    return finish(wide, narrow, got, cond[0], inputs["cond_index"], tiles, mod_cols, w)
 
 
 def solution(mesh):
@@ -1415,7 +1628,7 @@
     wide, narrow = mesh.shape["wide"], mesh.shape["narrow"]
     fused = wide == PLANES * PAIR and narrow == PLANES
     return jax.shard_map(
-        partial(fused_program if fused else plain_device, wide, narrow),
+        partial(fused_device if fused else plain_device, wide, narrow),
         mesh=mesh,
         in_specs=(rows, cond_rows, P("wide", None), P("wide", None), rows) + (matrix, vector) * 5,
         out_specs=(rows, rows, cond_rows) + (matrix, vector) * 5,

time: 714 us -> 544 us (0.76); the launches traced: 701 us -> 541 us
  local copies, waits for them, and re-layouts: 94 us -> 9.4 us
  Pallas kernels: 572 us -> 530 us
  starting transfers between devices: 13.3 us -> 0 us
  matrix products: 12.1 us -> 0 us
  other arithmetic: 7.86 us -> 0 us
    pallas_call x1, Pallas kernels: 572 us -> 513 us  [fused_device(): pl.pallas_call(partial(block_kernel, cfg), out_shape=list(outputs.values(...]
    convert_element_type x6 -> x0, local copies, waits for them, and re-layouts: 54.3 us -> none  [the longest x3 33.1 us: fused_device(): up_g.reshape(LAYERS, depth, -1).astype(F32)]
    pallas_call x0 -> x1, Pallas kernels: none -> 17.7 us  [finish(): pl.pallas_call(partial(finish_kernel, cfg), grid=(LAYERS, bands), out_sha...]
    all_to_all x2 -> x0, starting transfers between devices: 13.3 us -> none  [the longest x1 7.73 us: fused_program(): lax.all_to_all(lead_grad.reshape(wide, SEGS, depth), 'wide', 0, 0, tiled=...]
    dot_general x4 -> x0, matrix products: 12.1 us -> none  [the longest x1 5.28 us: fused_program(): jnp.einsum('nd,lne->lde', lead_own, mod_all, preferred_element_type=F32)]
    dynamic_slice x9 -> x0, local copies, waits for them, and re-layouts: 9.67 us -> none  [the longest x3 4.05 us: fused_device(): lax.dynamic_slice_in_dim(item, w * (item.shape[1] // wide), item.shape[1]...]
  transfers between devices with their start and end apart: 2 -> 0, of which waited for: 0 -> 0; matrix products, arithmetic and copies ran while one was open for 15% -> 0% of each run, Pallas kernels for 82% -> 0%
where the time goes in v3:
time: 544 us; the launch traced here: 541 us
  Pallas kernels  530 us (97%)
  local copies, waits for them, and re-layouts  9.4 us (2%)
    pallas_call x1, Pallas kernels, fused_device(): pl.pallas_call(partial(block_kernel, cfg), out_shape=list(outputs.values(...  513 us
    pallas_call x1, Pallas kernels, finish(): pl.pallas_call(partial(finish_kernel, cfg), grid=(LAYERS, bands), out_sha...  17.7 us

profile of v3, /device:TPU:17, one launch (start us, length us, event | category | flops | bytes accessed | tf_op | source)
XLA Modules:
  0.0 540.6 jit_solution(16314211283658444905)
XLA Ops:
  0.6 1.3 copy.28.refs_2_.refs_9_
  2.0 0.0 copy-start.6
  2.0 0.0 copy-start.7
  2.0 512.6 %shard_map.246 = (bf16[128,1152]{1,0:T(8,128)(2,1)}, f32[128,1152]{1,0:T(8,128)}, bf16[2,4,144,864]{3,2,1,0:T(8,128)(2,1)}, bf16[2,144,1152]{2,1,0:T(8,128)(2,1)...) custom-call(bf16[128,1152]{1,0:T(8,128)(2,1)} %bitcast.12, ...), custom_call_target="tpu_custom_call" | custom-call | tf_op jit(solution)/shard_map/pallas_call | solution.py:1610
  514.6 0.0 copy-done.6
  514.6 0.0 copy-done.7
  514.6 0.0 copy-start
  514.6 1.6 copy-done
  516.2 0.0 copy-start.1
  516.2 1.2 copy-done.1
  517.4 0.0 copy-start.2
  517.4 1.1 copy-done.2
  518.5 0.0 copy-start.3
  518.5 0.9 copy-done.3
  519.4 0.0 copy-start.4
  519.4 0.9 copy-done.4
  520.3 0.0 copy-start.5
  520.3 0.9 copy-done.5
  521.2 0.0 copy-start.9
  521.2 0.0 copy-start.8
  521.2 17.7 %shard_map.247 = (f32[2,144,6912]{2,1,0:T(8,128)}, f32[2,144,3456]{2,1,0:T(8,128)}, f32[2,144,1152]{2,1,0:T(8,128)}, f32[2,144,4608]{2,1,0:T(8,128)}, f32[2,576,...) custom-call(bf16[2,4,144,864]{3,2,1,0:T(8,128)(2,1)S(1)} %copy-done,, ...), custom_call_target="tpu_custom_call" | custom-call | tf_op jit(solution)/shard_map/pallas_call | solution.py:1486
  538.9 0.0 copy-done.9
  538.9 0.7 copy.32
  539.6 0.0 copy-done.8
  539.6 0.8 copy.33
Async XLA Ops:
  2.0 512.6 %copy-start.6 = (bf16[1,4,1152]{2,1,0:T(4,128)(2,1)S(1)}, bf16[1,4,1152]{2,1,0:T(4,128)(2,1)}, u32[]{:S(2)}) copy-start(bf16[1,4,1152]{2,1,0:T(4,128)(2,1)} %param.16) | copy-start | bytes 27652
  2.0 512.6 %copy-start.7 = (s32[4,1]{1,0:T(4,128)S(1)}, s32[4,1]{1,0:T(4,128)}, u32[]{:S(2)}) copy-start(s32[4,1]{1,0:T(4,128)} %copy.28.refs_2_.refs_9_) | copy-start | bytes 52
  514.6 1.6 copy-start
  516.2 1.2 copy-start.1
  517.4 1.1 copy-start.2
  518.5 0.9 copy-start.3
  519.4 0.9 copy-start.4
  520.3 0.9 copy-start.5
  521.2 17.7 %copy-start.9 = (bf16[128,1152]{1,0:T(8,128)(2,1)S(1)}, bf16[128,1152]{1,0:T(8,128)(2,1)}, u32[]{:S(2)}) copy-start(bf16[128,1152]{1,0:T(8,128)(2,1)} %get-tuple-element.34) | copy-start | bytes 884740
  521.2 18.4 %copy-start.8 = (f32[128,1152]{1,0:T(8,128)S(1)}, f32[128,1152]{1,0:T(8,128)}, u32[]{:S(2)}) copy-start(f32[128,1152]{1,0:T(8,128)} %get-tuple-element.35) | copy-start | bytes 1769476

commit v4 on v3

--- a/solution.py
+++ b/solution.py
@@ -300,11 +300,12 @@
     core, side, far = (w, n_core), (w, n_side), (w, n_far)
     beside = (w + 1 - 2 * x, n)
 
-    def plane_of(j):
-        return (z + j) % PLANES
-
-    def plane(j):
-        return (plane_of(j) * PAIR + x, n)
+    z_half = z // 2
+    z_partner, z_inner, z_outer = z + 1 - 2 * (z % 2), 2 - z_half, 3 - 3 * z_half
+    is_inner = jnp.logical_or(z == 1, z == 2)
+
+    def at_plane(idx):
+        return (idx * PAIR + x, n)
 
     def wide_peer(j):
         return ((w + j) % wide, n)
@@ -350,15 +351,20 @@
             [lead[:, depth * row : depth * (row + 1)], jnp.zeros((16 - SEGS, depth), F32)], 0
         )
         r.lead[row] = tile.astype(BF16)
-    r.bias_tx[...] = jnp.zeros_like(r.bias_tx)
+    bias_refs = (r.ada_b, r.qkv_b, r.out_b, r.up_b, r.down_b)
+    bias_places, row = [], 0
+    for k, ref in enumerate(bias_refs):
+        for start in range(0, ref.shape[1], 3 * LANES):
+            size = min(3 * LANES, ref.shape[1] - start)
+            bias_places.append((k, row, start, size))
+            row += 1
+    r.bias_rows[...] = jnp.zeros_like(r.bias_rows)
     for layer in range(LAYERS):
-        for line, at, ref in (
-            (0, 0, r.ada_b), (1, 0, r.qkv_b), (1, 4 * LANES, r.out_b),
-            (2, 0, r.up_b), (2, 5 * LANES, r.down_b),
-        ):
-            size = ref.shape[1]
-            row = 3 * layer + line
-            r.bias_tx[row : row + 1, at : at + size] = ref[...].astype(F32)[layer : layer + 1]
+        for k, row, start, size in bias_places:
+            line = r.bias_rows.shape[0] // LAYERS * layer + row
+            values = bias_refs[k][...].astype(F32)[layer : layer + 1, start : start + size]
+            r.bias_rows[line : line + 1, :size] = values
+    r.bias_tx[...] = r.bias_rows[...].astype(BF16)
 
     barrier = pltpu.get_barrier_semaphore()
     partners = [core, side, far] + [wide_peer(j) for j in range(1, wide)]
@@ -382,13 +388,13 @@
     def w_block(which, layer, plane_idx, col):
         return full[which].at[layer, w_rows(which, plane_idx, col)]
 
-    def w_hop(which, layer, plane_idx, right, own=False):
+    def w_z(which, layer, kind, plane_idx, own=False):
         slot = layer * 4 + which
         block = w_block(which, layer, plane_idx, x)
-        k = PLANES if own and not right else plane_idx
         return remote(
             shard(which, layer) if own else block, block,
-            (r.wz_s.at[slot, k], r.wz_r.at[slot, plane_idx]), plane(1 if right else PLANES - 1),
+            (r.wz_s.at[slot, kind], r.wz_r.at[slot, plane_idx]),
+            at_plane(z_inner if kind == 1 else z_partner),
         )
 
     def w_x(which, layer, plane_idx, col, own=False):
@@ -404,12 +410,11 @@
             shard(which, layer), w_block(which, layer, z, x), r.w_own.at[layer * 4 + which]
         )
 
-    last_plane = PLANES - 1
-
     def weights_start(which, layer):
         def go():
-            pl.when(z < last_plane)(lambda: w_hop(which, layer, z, True, True).start())
-            pl.when(z > 0)(lambda: w_hop(which, layer, z, False, True).start())
+            w_z(which, layer, 1, z, True).start()
+            w_z(which, layer, 0, z, True).start()
+            w_x(which, layer, z, x, True).start()
             w_own(which, layer).start()
 
         if which == OUT:
@@ -417,34 +422,32 @@
         else:
             go()
 
+    passes_out = jnp.logical_and(is_inner, z_half != n // 2)
+
     def weights_steps(which, layer):
-        def own():
-            w_x(which, layer, z, x, True).start()
-
-        def passed(plane_idx, right):
-            w_hop(which, layer, plane_idx, right).wait_recv()
-            onward = z < last_plane if right else z > 0
-            pl.when(onward)(lambda: w_hop(which, layer, plane_idx, right).start())
+        def passed(plane_idx, kind):
+            w_z(which, layer, 0, plane_idx).wait_recv()
+            if kind:
+                onward = passes_out if which == OUT else is_inner
+                pl.when(onward)(lambda: w_z(which, layer, kind, plane_idx).start())
             w_x(which, layer, plane_idx, x).start()
 
-        def first():
-            slot = layer * 4 + which + 1
-            if slot < 4 * LAYERS:
+        def step(plane_idx, kind):
+            passed(plane_idx, kind)
+            slot = layer * 4 + which + 2
+            if kind == 2 and 2 < slot < 4 * LAYERS:
                 weights_start(slot % 4, slot // 4)
-            if which == OUT:
-                pl.when(z == n)(own)
-                pl.when(z > n)(lambda: passed(n, True))
-                pl.when(z < n)(lambda: passed(n, False))
-            else:
-                own()
-
-        def further(j):
-            pl.when(z >= j)(lambda: passed(z - j, True))
-            pl.when(z + j <= last_plane)(lambda: passed(z + j, False))
+
+        def only():
+            pl.when(z != n)(lambda: passed(n, 2))
+            slot = layer * 4 + which + 2
+            weights_start(slot % 4, slot // 4)
 
         if which == OUT:
-            return [first]
-        return [first] + [partial(further, j) for j in range(1, PLANES)]
+            return [only]
+        return [
+            partial(step, idx, kind) for idx, kind in ((z_partner, 0), (z_inner, 2), (z_outer, 3))
+        ]
 
     steps = [
         (layer * 4 + which, step)
@@ -466,31 +469,28 @@
             w_x(which, layer, n, 1 - x).wait_recv()
             pl.when(z == n)(lambda: w_own(which, layer).wait())
         else:
-            for j in range(PLANES):
-                w_x(which, layer, plane_of(j), 1 - x).wait_recv()
+            for idx in range(PLANES):
+                w_x(which, layer, idx, 1 - x).wait_recv()
             w_own(which, layer).wait()
 
     def weights_drain(which, layer):
         def own():
-            pl.when(z < last_plane)(lambda: w_hop(which, layer, z, True, True).wait_send())
-            pl.when(z > 0)(lambda: w_hop(which, layer, z, False, True).wait_send())
-
-        def passed(plane_idx, right):
-            onward = z < last_plane if right else z > 0
-            pl.when(onward)(lambda: w_hop(which, layer, plane_idx, right).wait_send())
+            for kind in range(2):
+                w_z(which, layer, kind, z, True).wait_send()
 
         if which == OUT:
             w_x(which, layer, n, x).wait_send()
             pl.when(z == n)(own)
-            pl.when(z > n)(lambda: passed(n, True))
-            pl.when(z < n)(lambda: passed(n, False))
+            pl.when(passes_out)(lambda: w_z(which, layer, 2, n).wait_send())
         else:
             own()
-            for j in range(1, PLANES):
-                pl.when(z >= j)(lambda: passed(z - j, True))
-                pl.when(z + j <= last_plane)(lambda: passed(z + j, False))
-            for j in range(PLANES):
-                w_x(which, layer, plane_of(j), x).wait_send()
+            for idx in range(PLANES):
+                w_x(which, layer, idx, x).wait_send()
+
+            @pl.when(is_inner)
+            def _():
+                w_z(which, layer, 2, z_inner).wait_send()
+                w_z(which, layer, 3, z_outer).wait_send()
 
     def load(which, layer):
         return pltpu.make_async_copy(full[which].at[layer], loaded[which], r.load_sem.at[which])
@@ -504,31 +504,31 @@
     def tok_rows(chunk, part):
         return span(local * chunk + half * part, half)
 
-    def tok_copy(ref, kind, part, incoming=False):
+    def tok_copy(ref, kind, part, incoming=False, early=False):
         chunk = ((n_core, n_side, n_far) if incoming else (n, n, n_side))[kind]
         rows = ref.at[tok_rows(chunk, part)]
-        k = 2 * kind + part
+        k = 2 * kind + part + 6 * early
         return remote(rows, rows, (r.tok_s.at[k], r.tok_r.at[k]), side if kind == 1 else core)
 
-    def tok_send(ref, part):
-        tok_copy(ref, 1, part).start()
-        tok_copy(ref, 0, part).start()
-
-    def tok_own(ref):
+    def tok_send(ref, part, early=False):
+        tok_copy(ref, 1, part, early=early).start()
+        tok_copy(ref, 0, part, early=early).start()
+
+    def tok_own(ref, early=False):
         for part in range(2):
-            tok_copy(ref, 0, part, True).wait_recv()
-
-    def tok_other(ref):
+            tok_copy(ref, 0, part, True, early).wait_recv()
+
+    def tok_other(ref, early=False):
         for part in range(2):
-            tok_copy(ref, 1, part, True).wait_recv()
-            tok_copy(ref, 2, part).start()
+            tok_copy(ref, 1, part, True, early).wait_recv()
+            tok_copy(ref, 2, part, early=early).start()
         for part in range(2):
-            tok_copy(ref, 2, part, True).wait_recv()
-
-    def tok_drain(ref):
+            tok_copy(ref, 2, part, True, early).wait_recv()
+
+    def tok_drain(ref, early=False):
         for kind in range(3):
             for part in range(2):
-                tok_copy(ref, kind, part).wait_send()
+                tok_copy(ref, kind, part, early=early).wait_send()
 
     def block_rows(block):
         return span(2 * local * (y if block else 1 - y), 2 * local)
@@ -618,6 +618,16 @@
             pieces.append(shifted(buffer[layer, k], start % LANES, size))
         pack(dst, pieces)
 
+    def folded(values, size):
+        rest = values[:, size:]
+        if rest.shape[1] < size:
+            rest = jnp.concatenate([rest, jnp.zeros((8, size - rest.shape[1]), F32)], 1)
+        return jnp.concatenate([values[:, :size], rest], 0).astype(BF16)
+
+    def unfolded(values, size):
+        values = values.astype(F32)
+        return jnp.concatenate([values[:8], values[8:]], 1)[:, :size]
+
     def lead_copy(j, incoming=False):
         return remote(
             r.lead.at[(w + j) % wide], r.lead_rx.at[(w - j + wide) % wide if incoming else w],
@@ -632,9 +642,13 @@
 
     def mod_copy(j, incoming=False):
         return remote(
-            r.mod_tx.at[(w + j) % wide], r.mod_rx.at[(w - j + wide) % wide if incoming else w],
+            r.mod_part.at[(w + j) % wide], r.mod_rx.at[(w - j + wide) % wide if incoming else w],
             (r.mod_sem_s.at[j - 1], r.mod_sem_r.at[j - 1]), wide_peer(j),
         )
+
+    def wait_all(copy, count=wide):
+        for j in range(1, count):
+            copy(j, True).wait_recv()
 
     narrow_peers = ((core, n_core), (side, n_side), (far, n_far))
 
@@ -647,27 +661,28 @@
 
     for j in range(1, wide):
         lead_copy(j).start()
+    for j in range(1, wide):
+        bias_copy(j).start()
+    r.bias_rx[pl.ds(w, 1)] = r.bias_tx[...][None]
     pack_shard(QKV, 0)
     weights_start(QKV, 0)
-    for j in range(1, wide):
-        bias_copy(j).start()
     r.lead_rx[pl.ds(w, 1)] = r.lead[pl.ds(w, 1)]
-    r.bias_rx[pl.ds(w, 1)] = r.bias_tx[...][None]
     ada_load.wait()
-    for j in range(1, wide):
-        lead_copy(j, True).wait_recv()
+    wait_all(lead_copy)
     lead_all = r.lead_rx[...].reshape(wide * 16, depth)
     for layer in range(LAYERS):
         product = dot(lead_all, r.ada_v[layer], ((1,), (0,)))
         for row in range(wide):
             at = slice(SEGS * layer, SEGS * layer + SEGS)
-            r.mod_tx[row, at, :] = product[16 * row : 16 * row + SEGS]
+            r.mod_part[row, at, :] = product[16 * row : 16 * row + SEGS]
     for j in range(1, wide):
         mod_copy(j).start()
-    r.mod_rx[pl.ds(w, 1)] = r.mod_tx[pl.ds(w, 1)]
+    weights_start(OUT, 0)
+    r.mod_rx[pl.ds(w, 1)] = r.mod_part[pl.ds(w, 1)]
     for which, layer in ((UP, 0), (QKV, 1), (UP, 1)):
         pack_shard(which, layer)
     pump_through(QKV, 0)
+    weights_start(UP, 0)
     r.mod_grad[...] = jnp.zeros_like(r.mod_grad)
     r.lead_t[...] = jnp.zeros_like(r.lead_t)
     for layer in range(LAYERS):
@@ -676,17 +691,15 @@
             r.lead_t[layer, at : at + SEGS, :] = r.lead_rx[row].astype(F32)[:SEGS]
         r.lead_o[layer] = jnp.transpose(r.lead_t[layer]).astype(BF16)
 
-    for j in range(1, wide):
-        bias_copy(j, True).wait_recv()
-    for row in range(wide):
-        for line, at, ref in (
-            (0, 0, r.ada_full), (1, 0, r.qkv_full), (1, 4 * LANES, r.out_full),
-            (2, 0, r.up_full), (2, 5 * LANES, r.down_full),
-        ):
-            size = ref.shape[-1] // wide
-            for layer in range(LAYERS):
-                piece = r.bias_rx[row, 3 * layer + line : 3 * layer + line + 1, at : at + size]
-                ref[0, layer : layer + 1, size * row : size * (row + 1)] = piece
+    wait_all(bias_copy)
+    bias_full = (r.ada_full, r.qkv_full, r.out_full, r.up_full, r.down_full)
+    for peer in range(wide):
+        values = r.bias_rx[peer].astype(F32)
+        for layer in range(LAYERS):
+            for k, row, start, size in bias_places:
+                line = values.shape[0] // LAYERS * layer + row
+                at = bias_refs[k].shape[1] * peer + start
+                bias_full[k][0, layer : layer + 1, at : at + size] = values[line : line + 1, :size]
     for which, ref in ((QKV, r.qkv_full), (UP, r.up_full)):
         pieces = [pick(ref, *window) for window in windows(which)]
         for layer in range(LAYERS):
@@ -697,8 +710,7 @@
         r.bias_sum[at + OUT : at + OUT + 1] = r.out_full[0, layer : layer + 1]
         r.bias_sum[at + DOWN : at + DOWN + 1] = r.down_full[0, layer : layer + 1]
 
-    for j in range(1, wide):
-        mod_copy(j, True).wait_recv()
+    wait_all(mod_copy)
     ada_own = r.ada_full[0, :, span(LANES * mod_start(tiles, narrow, n), mod_cols, LANES)]
     total = jnp.sum(r.mod_rx[...], 0)
     for layer in range(LAYERS):
@@ -706,7 +718,6 @@
         r.mod_q[pl.ds(n, 1), at, :] = (total[at] + ada_own[layer : layer + 1])[None]
     for k in range(3):
         quarter_copy(k).start()
-    pump(2)
     for k in range(3):
         quarter_copy(k, True).wait_recv()
     for part in range(narrow):
@@ -758,7 +769,7 @@
             if head % 2:
                 pump(1)
 
-    def mlp_block(layer, block):
+    def up_block(layer, block):
         rows = block_rows(block)
         hidden = r.hid_mlp[layer, rows, :]
         for at in range(0, width, 3 * LANES):
@@ -767,7 +778,9 @@
             up = up + r.bias_sum[4 * layer + UP : 4 * layer + UP + 1, tile]
             r.up[layer, rows, tile] = up.astype(BF16)
             r.act[layer, rows, tile] = gelu(up).astype(BF16)
-        r.part[block] = dot(r.act[layer, rows, :], r.down_v[...], ((1,), (0,)))
+
+    def down_block(layer, block):
+        r.part[block] = dot(r.act[layer, block_rows(block), :], r.down_v[...], ((1,), (0,)))
 
     def state_of(layer, start):
         rows = span(start, STEP)
@@ -798,19 +811,22 @@
 
         return take
 
-    for layer in range(LAYERS):
+    def attn_forward(layer, take, before):
         hid = r.hid_attn.at[layer]
+        gather_norm(layer, hid, 0, 1, take, before)
         if layer == 0:
-            gather_norm(0, hid, 0, 1, lambda start, seg: state_of(0, start), lambda part: None)
-        else:
-            gather_norm(layer, hid, 0, 1, after_mlp(layer - 1), sum_wait)
+            early_grad()
         pump(1)
         weights_ready(QKV, layer)
         tok_own(hid)
         qkv_block(layer, 1)
+        pump(1)
         tok_other(hid)
         qkv_block(layer, 0)
         pump(1)
+        if layer == 0:
+            tok_own(r.grad_down, True)
+            tok_other(r.grad_down, True)
         attend(layer)
         weights_ready(OUT, layer)
         tok_drain(hid)
@@ -820,29 +836,39 @@
             if block == 0:
                 sum_cross()
         pump(1)
-        hid = r.hid_mlp.at[layer]
-        gather_norm(layer, hid, 3, 4, after_attn(layer), sum_wait)
+        gather_norm(layer, r.hid_mlp.at[layer], 3, 4, after_attn(layer), sum_wait)
         pump(1)
         weights_ready(UP, layer)
-        weights_ready(DOWN, layer)
-        tok_own(hid)
-        mlp_block(layer, 1)
-        sum_block(1)
-        pump(1)
-        tok_other(hid)
-        mlp_block(layer, 0)
-        sum_block(0)
-        sum_cross()
-        tok_drain(hid)
-        pump(1)
-    for part in range(2):
-        sum_wait(part)
-        finish = after_mlp(LAYERS - 1)
-
-        def last(start):
-            finish(start, seg_of(start))
-
-        each_step(part, last)
+
+    def early_grad():
+        for part in range(2):
+
+            def step(start):
+                rows = span(start, STEP)
+                grad = r.cot[rows, :].astype(F32)
+                r.token_o[rows, :] = grad
+                grad_down = (mod(LAYERS - 1, 5, seg_of(start)) * grad).astype(BF16)
+                r.grad_down[span(local * n + start, STEP), :] = grad_down
+
+            each_step(part, step)
+            tok_send(r.grad_down, part, True)
+
+    attn_forward(0, lambda start, seg: state_of(0, start), lambda part: None)
+    weights_ready(DOWN, 0)
+    hid = r.hid_mlp.at[0]
+    tok_own(hid)
+    up_block(0, 1)
+    down_block(0, 1)
+    sum_block(1)
+    pump(1)
+    tok_other(hid)
+    up_block(0, 0)
+    down_block(0, 0)
+    sum_block(0)
+    sum_cross()
+    tok_drain(hid)
+    pump(2)
+    attn_forward(1, after_mlp(0), sum_wait)
 
     sums = (r.qkv_d, r.out_d, r.up_d, r.down_d)
     from_x = (r.qkv_xr, r.out_xr, r.up_xr, r.down_xr)
@@ -861,13 +887,21 @@
             src, from_x[which].at[k], (r.dx_s.at[which, k], r.dx_r.at[which, k]), beside
         )
 
-    def d_z(which, j):
-        dest = n if which == OUT else plane_of(j)
-        k = 0 if which == OUT else j - 1
-        src = sums[which].at[d_rows(which, dest, x)]
-        return remote(
-            src, from_z[which].at[j - 1], (r.dz_s.at[which, k], r.dz_r.at[which, j - 1]), plane(j)
-        )
+    def d_z(which, kind):
+        idx = 0 if which == OUT else (z_partner, z_inner, z_outer)[kind]
+        src = from_x[which].at[idx]
+
+        def send(slot, plane_idx):
+            return remote(
+                src, from_z[which].at[slot], (r.dz_s.at[which, kind], r.dz_r.at[which, slot]),
+                at_plane(plane_idx),
+            )
+
+        return send
+
+    def d_z_in(which, slot):
+        ref = from_z[which].at[slot]
+        return remote(ref, ref, (r.dz_s.at[which, 0], r.dz_r.at[which, slot]), at_plane(z_partner))
 
     def grad_product(which, layer):
         left, right = (
@@ -885,70 +919,106 @@
                 product = dot(left[layer, :, tile], right[...], ((0,), (0,)))
                 sums[which][tile, :] = product.astype(BF16)
 
+    def grad_send(which, layer):
         if layer == 0:
             pl.semaphore_wait(r.credit_x.at[which], 1)
-        for plane_idx in range(1 if which == OUT else PLANES):
-            d_x(which, plane_idx).start()
+        if which == OUT:
+            d_x(which, 0).start()
+        else:
+            for idx in (z_outer, z_inner, z_partner, z):
+                d_x(which, idx).start()
+
+    out_home = z == n
+    out_near = z_partner == n
+    out_far = z_half != n // 2
+
+    def credit(sem, device):
+        pl.semaphore_signal(sem, inc=1, device_id=device, device_id_type=MESH)
 
     def grad_beside(which, layer):
+        def add(slot, rows):
+            total = sums[which][rows, :].astype(F32) + from_x[which][slot].astype(F32)
+            from_x[which][slot] = total.astype(BF16)
+
         if which == OUT:
             d_x(which, 0).wait_recv()
-            rows = d_rows(which, n, x)
-            total = sums[which][rows, :].astype(F32) + from_x[which][0].astype(F32)
-            sums[which][rows, :] = total.astype(BF16)
-
-            @pl.when(z != n)
+            add(0, d_rows(which, n, x))
+            outer_far = jnp.logical_and(out_far, jnp.logical_not(is_inner))
+
+            @pl.when(jnp.logical_or(out_near, outer_far))
             def _():
                 if layer == 0:
-                    pl.semaphore_wait(r.credit_z.at[which], 1)
-                d_z(which, (n - z + PLANES) % PLANES).start()
-
+                    pl.semaphore_wait(r.credit_z.at[which, 0], 1)
+
+            pl.when(out_near)(lambda: d_z(which, 0)(0, z_partner).start())
+            pl.when(outer_far)(lambda: d_z(which, 0)(2, z_partner).start())
             d_x(which, 0).wait_send()
         else:
-            for j in (1, 2, 3, 0):
-                idx = plane_of(j)
+            for k, idx in ((2, z_outer), (1, z_inner), (0, z_partner), (None, z)):
                 d_x(which, idx).wait_recv()
-                rows = d_rows(which, idx, x)
-                total = sums[which][rows, :].astype(F32) + from_x[which][idx].astype(F32)
-                sums[which][rows, :] = total.astype(BF16)
-                if layer == 0 and j == 1:
-                    pl.semaphore_wait(r.credit_z.at[which], PLANES - 1)
-                if j:
-                    d_z(which, j).start()
+                add(idx, d_rows(which, idx, x))
+                if k == 0:
+                    if layer == 0:
+                        pl.semaphore_wait(r.credit_z.at[which, 0], 1)
+
+                    @pl.when(jnp.logical_not(is_inner))
+                    def _():
+                        d_z(which, 2)(3, z_partner).start()
+                        d_z(which, 1)(2, z_partner).start()
+
+                    d_z(which, 0)(0, z_partner).start()
             for idx in range(PLANES):
                 d_x(which, idx).wait_send()
-        if layer == 1:
-            pl.semaphore_signal(
-                r.credit_x.at[which], inc=1, device_id=beside, device_id_type=MESH
-            )
+
+    def grad_join(which, layer):
+        def add(slot, idx):
+            d_z_in(which, slot).wait_recv()
+            total = from_x[which][idx].astype(F32) + from_z[which][slot].astype(F32)
+            from_x[which][idx] = total.astype(BF16)
+
+        if which == OUT:
+
+            @pl.when(jnp.logical_and(out_far, is_inner))
+            def _():
+                add(2, 0)
+                if layer == 0:
+                    pl.semaphore_wait(r.credit_z.at[which, 1], 1)
+                else:
+                    credit(r.credit_z.at[which, 0], at_plane(z_partner))
+                d_z(which, 0)(1, n).start()
+        else:
+
+            @pl.when(is_inner)
+            def _():
+                if layer == 0:
+                    pl.semaphore_wait(r.credit_z.at[which, 1], 2)
+                add(3, z_outer)
+                d_z(which, 2)(1, z_outer).start()
+                add(2, z_inner)
+                d_z(which, 1)(1, z_inner).start()
 
     def grad_planes(which, layer):
         def add():
-            for j in range(1, PLANES):
-                d_z(which, j).wait_recv()
-            rows = d_rows(which, z, x)
-            total = sums[which][rows, :].astype(F32)
-            for j in range(PLANES - 1):
-                total = total + from_z[which][j].astype(F32)
+            d_z_in(which, 0).wait_recv()
+            d_z_in(which, 1).wait_recv()
+            total = from_x[which][0 if which == OUT else z].astype(F32)
+            total = total + from_z[which][0].astype(F32) + from_z[which][1].astype(F32)
             if layer == 0:
                 spread_sent(which, 1)
             final[which][...] = total.astype(BF16)
             if layer == 1:
-                for j in range(1, PLANES):
-                    pl.semaphore_signal(
-                        r.credit_z.at[which], inc=1, device_id=plane(j), device_id_type=MESH
-                    )
+                credit(r.credit_z.at[which, 0], at_plane(z_partner))
+                credit(r.credit_z.at[which, 1], at_plane(z_inner))
 
         if which == OUT:
-            pl.when(z == n)(add)
-
-            @pl.when(z != n)
-            def _():
-                d_z(which, (n - z + PLANES) % PLANES).wait_send()
+            pl.when(out_home)(add)
+            pl.when(jnp.logical_not(out_home))(lambda: d_z(which, 0)(0, z_partner).wait_send())
         else:
             add()
-            for j in range(1, PLANES):
-                d_z(which, j).wait_send()
+            for kind in range(3):
+                d_z(which, kind)(0, z_partner).wait_send()
+        if layer == 1:
+            credit(r.credit_x.at[which], beside)
 
     def spread(which, layer, kind, source=None):
         slot = layer * 4 + which
@@ -1055,99 +1125,72 @@
             grad_key = dot(grad_scores, query, ((0,), (0,)))
             grad_value = dot(probs.astype(BF16), grad, ((0,), (0,)))
 
+            def tile(k):
+                return slice(LANES * k, LANES * k + HEAD)
+
             @pl.when(i == 0)
             def _():
-                r.key_sum[:, :HEAD] = grad_key
-                r.value_sum[:, :HEAD] = grad_value
+                for k in range(narrow):
+                    at = slice(local * k, local * (k + 1))
+                    r.grad_hid[:, tile(k)] = grad_key[at]
+                    r.grad_hid[:, tile(narrow + k)] = grad_value[at]
 
             @pl.when(i > 0)
             def _():
-                r.key_sum[:, :HEAD] += grad_key
-                r.value_sum[:, :HEAD] += grad_value
+                for k in range(narrow):
+                    at = slice(local * k, local * (k + 1))
+                    r.grad_hid[:, tile(k)] += grad_key[at]
+                    r.grad_hid[:, tile(narrow + k)] += grad_value[at]
 
         at = cols + HEAD * head
-        r.grad_qkv[:, at : at + HEAD] = (r.key_sum[:, :HEAD] * scale_inv).astype(BF16)
-        r.grad_qkv[:, cols + at : cols + at + HEAD] = r.value_sum[:, :HEAD].astype(BF16)
-
-    for part in range(2):
-        def first(start):
-            rows = span(start, STEP)
-            r.token_o[rows, :] = r.cot[rows, :].astype(F32)
-
-        each_step(part, first)
+        for k in range(narrow):
+            rows = slice(local * k, local * (k + 1))
+            key_sum = r.grad_hid[:, LANES * k : LANES * k + HEAD]
+            value_sum = r.grad_hid[:, LANES * (narrow + k) : LANES * (narrow + k) + HEAD]
+            r.grad_qkv[rows, at : at + HEAD] = (key_sum * scale_inv).astype(BF16)
+            r.grad_qkv[rows, cols + at : cols + at + HEAD] = value_sum.astype(BF16)
 
     def both(body):
         for part in range(2):
             each_step(part, body)
 
-    for layer in reversed(range(LAYERS)):
-        older = layer + 1
-        for part in range(2):
-            if layer < LAYERS - 1:
-                sum_wait(part)
-
-            def start_down(start):
-                rows = span(start, STEP)
-                seg = seg_of(start)
-                if layer < LAYERS - 1:
-                    grad_hidden = sum_take(start)
-                    unit, inv = norm(state_of(older, start))
-                    r.grad_hid[rows, :] = grad_hidden
-                    r.token_o[rows, :] += norm_back(
-                        grad_hidden * (1.0 + mod(older, 1, seg)), unit, inv
-                    )
-                grad_down = (mod(layer, 5, seg) * r.token_o[rows, :]).astype(BF16)
-                r.grad_down[span(local * n + start, STEP), :] = grad_down
-
-            each_step(part, start_down)
-            tok_send(r.grad_down, part)
-
-        def sums_attn(idx):
-            def body(start):
-                rows = span(start, STEP)
-                seg = seg_of(start)
-                unit, _ = norm(state_of(idx, start))
-                grad_hidden = r.grad_hid[rows, :]
-                mod_sum(idx, 0, seg, grad_hidden)
-                mod_sum(idx, 1, seg, grad_hidden * unit)
-
-            return body
-
-        if layer < LAYERS - 1:
-            both(sums_attn(older))
-            load(DOWN, layer).wait()
-            load(UP, layer).wait()
-
-        def sums_gate_mlp(start):
+    def sums_attn(layer):
+        def body(start):
             rows = span(start, STEP)
-            mod_sum(layer, 5, seg_of(start), r.down[layer, rows, :].astype(F32) * r.token_o[rows, :])
-
-        both(sums_gate_mlp)
-        bias_grad(layer, DOWN, r.grad_down[span(local * n, local), :])
-        tok_own(r.grad_down)
-        back_mlp_block(layer, 1)
-        sum_block(1)
-        tok_other(r.grad_down)
-        back_mlp_block(layer, 0)
-        sum_block(0)
-        sum_cross()
-        if layer > 0:
-            load(DOWN, layer - 1).start()
-            load(UP, layer - 1).start()
-        if layer == 1:
-            grad_product(DOWN, 1)
-            grad_product(UP, 1)
-        else:
-            grad_beside(UP, 1)
-            grad_beside(OUT, 1)
-            grad_planes(DOWN, 1)
-            grad_product(DOWN, 0)
-        bias_grad(layer, UP, r.grad_up[...])
-        tok_drain(r.grad_down)
+            seg = seg_of(start)
+            unit, _ = norm(state_of(layer, start))
+            grad_hidden = r.grad_hid[rows, :]
+            mod_sum(layer, 0, seg, grad_hidden)
+            mod_sum(layer, 1, seg, grad_hidden * unit)
+
+        both(body)
+
+    def sums_mlp(layer):
+        def body(start):
+            rows = span(start, STEP)
+            seg = seg_of(start)
+            unit, _ = norm(r.middle[layer, rows, :])
+            grad_hidden = r.grad_hid[rows, :]
+            mod_sum(layer, 3, seg, grad_hidden)
+            mod_sum(layer, 4, seg, grad_hidden * unit)
+            mod_sum(layer, 2, seg, r.branch[layer, rows, :].astype(F32) * r.token_o[rows, :])
+
+        both(body)
+
+    def sums_gate_mlp(layer, grad):
+        def body(start):
+            rows = span(start, STEP)
+            mod_sum(
+                layer, 5, seg_of(start), r.down[layer, rows, :].astype(F32) * grad[rows, :].astype(F32)
+            )
+
+        both(body)
+
+    def back_middle(layer):
         for part in range(2):
             sum_wait(part)
 
-            def start_branch(start):
+            def step(start):
                 rows = span(start, STEP)
                 seg = seg_of(start)
                 grad_hidden = sum_take(start)
@@ -1160,69 +1203,150 @@
                 grad_branch = (mod(layer, 2, seg) * grad).astype(BF16)
                 r.grad_branch[span(local * n + start, STEP), :] = grad_branch
 
-            each_step(part, start_branch)
+            each_step(part, step)
             tok_send(r.grad_branch, part)
 
-        def sums_mlp(start):
-            rows = span(start, STEP)
-            seg = seg_of(start)
-            unit, _ = norm(r.middle[layer, rows, :])
-            grad_hidden = r.grad_hid[rows, :]
-            mod_sum(layer, 3, seg, grad_hidden)
-            mod_sum(layer, 4, seg, grad_hidden * unit)
-            mod_sum(layer, 2, seg, r.branch[layer, rows, :].astype(F32) * r.token_o[rows, :])
-
-        both(sums_mlp)
-        bias_grad(layer, OUT, r.grad_branch[span(local * n, local), :])
-        if layer < LAYERS - 1:
-            load(OUT, layer).wait()
-            load(QKV, layer).wait()
-        tok_own(r.grad_branch)
-        back_attn_block(layer, 1)
-        tok_other(r.grad_branch)
-        back_attn_block(layer, 0)
-        if layer > 0:
-            load(OUT, layer - 1).start()
-        if layer == 0:
-            grad_spread(DOWN, 1)
-            grad_beside(QKV, 1)
-        for head in range(own_heads):
-            back_attend(layer, head)
+    def back_state(layer, start):
+        rows = span(start, STEP)
+        grad_hidden = sum_take(start)
+        unit, inv = norm(state_of(layer, start))
+        r.grad_hid[rows, :] = grad_hidden
+        r.token_o[rows, :] += norm_back(
+            grad_hidden * (1.0 + mod(layer, 1, seg_of(start))), unit, inv
+        )
+
+    def back_qkv(layer, checked=False):
         for block in range(2):
             rows = block_rows(block)
             r.part[block] = dot(r.grad_qkv[rows, :], r.qkv_v[...], ((1,), (1,)))
+            if checked and block == 0:
+                pl.semaphore_wait(r.credit_sum.at[0], 1)
             sum_block(block)
             if block == 0:
+                if checked:
+                    pl.semaphore_wait(r.credit_sum.at[1], 1)
                 sum_cross()
-        tok_drain(r.grad_branch)
-        if layer > 0:
-            load(QKV, layer - 1).start()
-        if layer == 1:
-            grad_product(OUT, 1)
-            grad_product(QKV, 1)
+
+    hid = r.hid_mlp.at[1]
+    tok_own(hid)
+    up_block(1, 1)
+    pump(1)
+    tok_other(hid)
+    up_block(1, 0)
+    pump(1)
+    grad_product(DOWN, 1)
+    bias_grad(1, DOWN, r.grad_down[span(local * n, local), :])
+    tok_drain(hid)
+    tok_drain(r.grad_down, True)
+    pump_through(DOWN, 1)
+    grad_send(DOWN, 1)
+    weights_ready(DOWN, 1)
+    for block in range(2):
+        back_mlp_block(1, block)
+        sum_block(block)
+        if block == 0:
+            sum_cross()
+    load(UP, 0).start()
+    grad_product(UP, 1)
+    grad_send(UP, 1)
+    bias_grad(1, UP, r.grad_up[...])
+    back_middle(1)
+    for block in range(2):
+        down_block(1, block)
+    load(DOWN, 0).start()
+    sums_mlp(1)
+    bias_grad(1, OUT, r.grad_branch[span(local * n, local), :])
+    tok_own(r.grad_branch)
+    back_attn_block(1, 1)
+    tok_other(r.grad_branch)
+    back_attn_block(1, 0)
+    load(OUT, 0).start()
+    for block in range(2):
+        sum_block(block)
+        if block == 0:
+            sum_cross()
+    grad_product(OUT, 1)
+    grad_send(OUT, 1)
+    for head in range(own_heads):
+        back_attend(1, head)
+        if head == 1:
             grad_beside(DOWN, 1)
-        else:
-            grad_planes(UP, 1)
-            grad_product(UP, 0)
-            grad_planes(OUT, 1)
-            grad_product(OUT, 0)
-            grad_planes(QKV, 1)
-            grad_product(QKV, 0)
-        bias_grad(layer, QKV, r.grad_qkv[...])
+    tok_drain(r.grad_branch)
     for part in range(2):
         sum_wait(part)
-
-        def finish_grad(start):
-            rows = span(start, STEP)
-            seg = seg_of(start)
-            grad_hidden = sum_take(start)
-            unit, inv = norm(state_of(0, start))
-            grad = r.token_o[rows, :] + norm_back(grad_hidden * (1.0 + mod(0, 1, seg)), unit, inv)
-            r.token_o[rows, :] = grad
-            mod_sum(0, 0, seg, grad_hidden)
-            mod_sum(0, 1, seg, grad_hidden * unit)
-
-        each_step(part, finish_grad)
+        finish_state = after_mlp(1)
+
+        def last(start):
+            finish_state(start, seg_of(start))
+
+        each_step(part, last)
+    credit(r.credit_sum.at[0], core)
+    credit(r.credit_sum.at[1], side)
+    back_qkv(1, True)
+    load(QKV, 0).start()
+    grad_product(QKV, 1)
+    grad_send(QKV, 1)
+    sums_gate_mlp(1, r.cot)
+    grad_beside(UP, 1)
+    bias_grad(1, QKV, r.grad_qkv[...])
+    for part in range(2):
+        sum_wait(part)
+
+        def start_down(start):
+            back_state(1, start)
+            grad_down = (mod(0, 5, seg_of(start)) * r.token_o[span(start, STEP), :]).astype(BF16)
+            r.grad_down[span(local * n + start, STEP), :] = grad_down
+
+        each_step(part, start_down)
+        tok_send(r.grad_down, part)
+    sums_attn(1)
+    sums_gate_mlp(0, r.token_o)
+    bias_grad(0, DOWN, r.grad_down[span(local * n, local), :])
+    load(DOWN, 0).wait()
+    load(UP, 0).wait()
+    grad_beside(OUT, 1)
+    grad_join(DOWN, 1)
+    tok_own(r.grad_down)
+    back_mlp_block(0, 1)
+    sum_block(1)
+    tok_other(r.grad_down)
+    back_mlp_block(0, 0)
+    sum_block(0)
+    sum_cross()
+    grad_product(DOWN, 0)
+    bias_grad(0, UP, r.grad_up[...])
+    tok_drain(r.grad_down)
+    back_middle(0)
+    grad_product(UP, 0)
+    grad_planes(DOWN, 1)
+    grad_send(DOWN, 0)
+    grad_join(UP, 1)
+    grad_join(OUT, 1)
+    sums_mlp(0)
+    bias_grad(0, OUT, r.grad_branch[span(local * n, local), :])
+    grad_beside(QKV, 1)
+    load(OUT, 0).wait()
+    load(QKV, 0).wait()
+    tok_own(r.grad_branch)
+    back_attn_block(0, 1)
+    tok_other(r.grad_branch)
+    back_attn_block(0, 0)
+    grad_spread(DOWN, 1)
+    grad_product(OUT, 0)
+    for head in range(own_heads):
+        back_attend(0, head)
+        if head == 1:
+            grad_planes(UP, 1)
+            grad_send(UP, 0)
+    back_qkv(0)
+    grad_join(QKV, 1)
+    grad_product(QKV, 0)
+    tok_drain(r.grad_branch)
+    bias_grad(0, QKV, r.grad_qkv[...])
+    for part in range(2):
+        sum_wait(part)
+        each_step(part, partial(back_state, 0))
+    sums_attn(0)
 
     def quarter_back(k, incoming=False):
         device, idx = narrow_peers[k]
@@ -1239,7 +1363,7 @@
 
     def bias_wide(j, incoming=False):
         return remote(
-            r.bias_grad, r.bias_all.at[(w - j + wide) % wide if incoming else w],
+            r.bias_half, r.bias_all.at[(w - j + wide) % wide if incoming else w],
             (r.bias_wide_s.at[j - 1], r.bias_wide_r.at[j - 1]), wide_peer(j),
         )
 
@@ -1272,32 +1396,37 @@
 
     for k in range(3):
         quarter_back(k).start()
-    grad_beside(DOWN, 0)
-    grad_spread(UP, 1)
-    grad_spread(OUT, 1)
     own_at = span(LANES * mod_start(tiles, narrow, n), mod_cols, LANES)
     total = r.mod_grad[:, own_at]
     for k in range(3):
         quarter_back(k, True).wait_recv()
         total = total + r.quarter_rx[k]
-    r.quarter_sum[...] = total
+    r.quarter_sum[...] = folded(total, mod_cols // 2)
     for j in range(1, wide):
         wide_back(j).start()
+    r.bias_half[...] = folded(r.bias_grad[...], 5 * LANES)
     for j in range(1, wide):
         bias_wide(j).start()
-    r.quarter_all[pl.ds(w, 1)] = total[None]
-    r.bias_all[pl.ds(w, 1)] = r.bias_grad[...][None]
+    r.quarter_all[pl.ds(w, 1)] = r.quarter_sum[...][None]
+    r.bias_all[pl.ds(w, 1)] = r.bias_half[...][None]
+    grad_planes(OUT, 1)
+    grad_send(OUT, 0)
+    grad_beside(DOWN, 0)
+    grad_planes(QKV, 1)
+    grad_send(QKV, 0)
+    grad_spread(UP, 1)
+    grad_spread(OUT, 1)
     grad_spread(QKV, 1)
-    grad_beside(UP, 0)
-    grad_beside(OUT, 0)
     for which in (DOWN, UP, OUT, QKV):
         grad_pass(which, 1)
-    grad_planes(DOWN, 0)
-    grad_spread(DOWN, 0)
-    grad_beside(QKV, 0)
+    grad_join(DOWN, 0)
+    grad_beside(UP, 0)
+    wait_all(wide_back)
     for j in range(1, wide):
-        wide_back(j, True).wait_recv()
-    r.mod_all[...] = r.quarter_all[...].reshape(wide * LAYERS * SEGS, mod_cols).astype(BF16)
+        mod_copy(j).wait_send()
+    for row in range(wide):
+        r.mod_part[row] = unfolded(r.quarter_all[row], mod_cols)
+    r.mod_all[...] = r.mod_part[...].reshape(wide * LAYERS * SEGS, mod_cols).astype(BF16)
     mod_own = pltpu.make_async_copy(r.mod_all, r.mod_o.at[n], r.mod_own_sem)
     mod_own.start()
     for k in range(3):
@@ -1312,24 +1441,29 @@
     for j in range(1, wide):
         lead_back(j).start()
     r.lead_back[pl.ds(w, 1)] = r.lead_tx[pl.ds(w, 1)]
-    for j in range(1, wide):
-        bias_wide(j, True).wait_recv()
-    r.bias_row[...] = jnp.sum(r.bias_all[...], 0)
+    grad_planes(DOWN, 0)
+    grad_spread(DOWN, 0)
+    grad_beside(OUT, 0)
+    wait_all(bias_wide)
+    r.bias_row[...] = unfolded(jnp.sum(r.bias_all[...].astype(F32), 0), width)
     bias_own = pltpu.make_async_copy(r.bias_row, r.bias_o.at[n], r.bias_own_sem)
     bias_own.start()
     for k in range(3):
         bias_narrow(k).start()
-    for j in range(1, wide):
-        lead_back(j, True).wait_recv()
+    grad_join(UP, 0)
+    grad_join(OUT, 0)
+    grad_beside(QKV, 0)
+    wait_all(lead_back)
     lead_own = pltpu.make_async_copy(r.lead_back, r.lead_g.at[n], r.lead_own_sem)
     lead_own.start()
     for k in range(3):
         lead_narrow(k).start()
+    grad_pass(DOWN, 0)
+    grad_join(QKV, 0)
     grad_planes(UP, 0)
     grad_spread(UP, 0)
     grad_planes(OUT, 0)
     grad_spread(OUT, 0)
-    grad_pass(DOWN, 0)
     grad_planes(QKV, 0)
     grad_spread(QKV, 0)
     for which in (UP, OUT, QKV):
@@ -1340,7 +1474,7 @@
             weights_drain(which, layer)
             grad_end(which, layer)
     for j in range(1, wide):
-        for copy in (lead_copy, bias_copy, mod_copy, wide_back, bias_wide, lead_back):
+        for copy in (lead_copy, bias_copy, wide_back, bias_wide, lead_back):
             copy(j).wait_send()
     for k in range(3):
         for copy in (quarter_copy, quarter_back, mod_narrow, bias_narrow, lead_narrow):
@@ -1488,7 +1622,7 @@
         grid=(LAYERS, bands),
         out_shape=list(outputs.values()), in_specs=in_specs, out_specs=out_specs,
         scratch_shapes=list(scratch.values()),
-        compiler_params=pltpu.CompilerParams(vmem_limit_bytes=48 * 2**20),
+        compiler_params=pltpu.CompilerParams(vmem_limit_bytes=62 * 2**20),
     )(*inputs.values())
     done = dict(zip(outputs, results))
     out = [got["mixed_o"][None], got["token_o"][None], done["cond_g"][None]]
@@ -1549,13 +1683,13 @@
         grad_down=vmem((row_len, width), BF16), grad_branch=vmem((row_len, width), BF16),
         grad_up=vmem((row_len, hidden), BF16), grad_qkv=vmem((row_len, 3 * cols), BF16),
         grad_heads=vmem((heads, row_len, LANES), BF16),
-        key_sum=vmem((row_len, LANES), F32), value_sum=vmem((row_len, LANES), F32),
         part=vmem((2, 2 * local, width), F32),
         core_tx=vmem((2, local, width), BF16), core_rx=vmem((2, local, width), BF16),
         side_tx=vmem((local, width), BF16), side_rx=vmem((local, width), BF16),
         ada_v=vmem((LAYERS, depth, mod_cols), BF16),
         lead=vmem((wide, 16, depth), BF16), lead_rx=vmem((wide, 16, depth), BF16),
-        bias_tx=vmem((8, 7 * LANES), F32), bias_rx=vmem((wide, 8, 7 * LANES), F32),
+        bias_rows=vmem((32, 3 * LANES), F32), bias_tx=vmem((32, 3 * LANES), BF16),
+        bias_rx=vmem((wide, 32, 3 * LANES), BF16),
         ada_full=vmem((1, LAYERS, tiles * LANES), F32), qkv_full=vmem((1, LAYERS, 3 * width), F32),
         out_full=vmem((1, LAYERS, width), F32), up_full=vmem((1, LAYERS, narrow * hidden), F32),
         down_full=vmem((1, LAYERS, width), F32), seg_col=vmem((row_len, 1), jnp.int32),
@@ -1564,40 +1698,43 @@
         lead_t=vmem((LAYERS, wide * LAYERS * SEGS, depth), F32),
         lead_tx=vmem((wide, SEGS, depth), F32), lead_back=vmem((wide, SEGS, depth), F32),
         bias_sum=vmem((4 * LAYERS, width), F32),
-        mod_tx=vmem((wide, LAYERS * SEGS, mod_cols), F32), mod_rx=vmem((wide, LAYERS * SEGS, mod_cols), F32),
+        mod_part=vmem((wide, LAYERS * SEGS, mod_cols), F32),
+        mod_rx=vmem((wide, LAYERS * SEGS, mod_cols), F32),
         mod_q=vmem((narrow, LAYERS * SEGS, mod_cols), F32),
         mods=vmem((LAYERS * SEGS, tiles * LANES), F32),
         mod_grad=vmem((LAYERS * SEGS, tiles * LANES), F32),
         quarter_rx=vmem((3, LAYERS * SEGS, mod_cols), F32),
-        quarter_sum=vmem((LAYERS * SEGS, mod_cols), F32),
-        quarter_all=vmem((wide, LAYERS * SEGS, mod_cols), F32),
+        quarter_sum=vmem((16, mod_cols // 2), BF16),
+        quarter_all=vmem((wide, 16, mod_cols // 2), BF16),
         mod_all=vmem((wide * LAYERS * SEGS, mod_cols), BF16),
-        bias_grad=vmem((4 * LAYERS, width), F32), bias_all=vmem((wide, 4 * LAYERS, width), F32),
+        bias_grad=vmem((4 * LAYERS, width), F32), bias_all=vmem((wide, 16, 5 * LANES), BF16),
+        bias_half=vmem((16, 5 * LANES), BF16),
         bias_row=vmem((4 * LAYERS, width), F32),
         qkv_d=vmem((width, 3 * cols), BF16), out_d=vmem((cols, width), BF16),
         up_d=vmem((width, hidden), BF16), down_d=vmem((hidden, width), BF16),
         qkv_xr=vmem((PLANES, depth, 3 * cols), BF16), out_xr=vmem((1, depth, width), BF16),
         up_xr=vmem((PLANES, depth, hidden), BF16), down_xr=vmem((PLANES, hidden_own, width), BF16),
-        qkv_zr=vmem((PLANES - 1, depth, 3 * cols), BF16), out_zr=vmem((PLANES - 1, depth, width), BF16),
-        up_zr=vmem((PLANES - 1, depth, hidden), BF16), down_zr=vmem((PLANES - 1, hidden_own, width), BF16),
+        qkv_zr=vmem((PLANES, depth, 3 * cols), BF16), out_zr=vmem((PLANES, depth, width), BF16),
+        up_zr=vmem((PLANES, depth, hidden), BF16), down_zr=vmem((PLANES, hidden_own, width), BF16),
         qkv_f=vmem((depth, 3 * cols), BF16), out_f=vmem((depth, width), BF16),
         up_f=vmem((depth, hidden), BF16), down_f=vmem((hidden_own, width), BF16),
-        wz_s=dma((8, 5)), wz_r=dma((8, 4)), wx_s=dma((8, 4)), wx_r=dma((8, 4)), w_own=dma((8,)),
-        load_sem=dma((4,)), tok_s=dma((6,)), tok_r=dma((6,)), sum_s=dma((4,)), sum_r=dma((4,)),
+        wz_s=dma((8, 4)), wz_r=dma((8, 4)), wx_s=dma((8, 4)), wx_r=dma((8, 4)), w_own=dma((8,)),
+        load_sem=dma((4,)), tok_s=dma((12,)), tok_r=dma((12,)), sum_s=dma((4,)), sum_r=dma((4,)),
         lead_sem_s=dma((wide - 1,)), lead_sem_r=dma((wide - 1,)),
         bias_sem_s=dma((wide - 1,)), bias_sem_r=dma((wide - 1,)),
         mod_sem_s=dma((wide - 1,)), mod_sem_r=dma((wide - 1,)),
         quarter_s=dma((3,)), quarter_r=dma((3,)), ada_sem=dma, raw_sem=dma((LAYERS, 3 + wide)), lead_own_sem=dma,
         lead_back_s=dma((wide - 1,)), lead_back_r=dma((wide - 1,)),
         lead_narrow_s=dma((3,)), lead_narrow_r=dma((3,)),
-        dx_s=dma((4, 4)), dx_r=dma((4, 4)), dz_s=dma((4, 3)), dz_r=dma((4, 3)),
+        dx_s=dma((4, 4)), dx_r=dma((4, 4)), dz_s=dma((4, 3)), dz_r=dma((4, 4)),
         spread_s=dma((8, 3)), spread_r=dma((8, 3)), spread_l=dma((8,)),
         back_s=dma((3,)), back_r=dma((3,)),
         wide_s=dma((wide - 1,)), wide_r=dma((wide - 1,)),
         bias_wide_s=dma((wide - 1,)), bias_wide_r=dma((wide - 1,)),
         bias_narrow_s=dma((3,)), bias_narrow_r=dma((3,)),
         mod_narrow_s=dma((3,)), mod_narrow_r=dma((3,)), mod_own_sem=dma, bias_own_sem=dma,
-        credit_x=pltpu.SemaphoreType.REGULAR((4,)), credit_z=pltpu.SemaphoreType.REGULAR((4,)),
+        credit_x=pltpu.SemaphoreType.REGULAR((4,)), credit_z=pltpu.SemaphoreType.REGULAR((4, 2)),
+        credit_sum=pltpu.SemaphoreType.REGULAR((2,)),
     )
     cfg = SimpleNamespace(
         names=[*inputs, *outputs, *scratch], wide=wide, narrow=narrow, width=width, depth=depth,

time: 544 us -> 446 us (0.82)
  Pallas kernels: 530 us -> 438 us
  local copies, waits for them, and re-layouts: 9.4 us -> 2.85 us
    pallas_call x1, Pallas kernels: 513 us -> 420 us  [fused_device(): pl.pallas_call(partial(block_kernel, cfg), out_shape=list(outputs.values(...]
    unnamed x22 -> x6, local copies, waits for them, and re-layouts: 8.08 us -> 1.54 us
where the time goes in v4:
time: 446 us; the launch traced here: 442 us
  Pallas kernels  438 us (98%)
    pallas_call x1, Pallas kernels, fused_device(): pl.pallas_call(partial(block_kernel, cfg), out_shape=list(outputs.values(...  420 us
    pallas_call x1, Pallas kernels, finish(): pl.pallas_call(partial(finish_kernel, cfg), grid=(LAYERS, bands), out_sha...  18.5 us

profile of v4, /device:TPU:17, one launch (start us, length us, event | category | flops | bytes accessed | tf_op | source)
XLA Modules:
  0.0 441.9 jit_solution(12627834811070281366)
XLA Ops:
  0.6 1.3 copy.28.refs_2_.refs_9_
  2.0 419.6 %shard_map.246 = (bf16[128,1152]{1,0:T(8,128)(2,1)}, f32[128,1152]{1,0:T(8,128)}, bf16[2,4,144,864]{3,2,1,0:T(8,128)(2,1)}, bf16[2,144,1152]{2,1,0:T(8,128)(2,1)...) custom-call(bf16[128,1152]{1,0:T(8,128)(2,1)} %bitcast.10, ...), custom_call_target="tpu_custom_call" | custom-call | tf_op jit(solution)/shard_map/pallas_call | solution.py:1747
  421.6 0.0 copy-start.1
  421.6 0.0 copy-start
  421.6 18.5 %shard_map.247 = (f32[2,144,6912]{2,1,0:T(8,128)}, f32[2,144,3456]{2,1,0:T(8,128)}, f32[2,144,1152]{2,1,0:T(8,128)}, f32[2,144,4608]{2,1,0:T(8,128)}, f32[2,576,...) custom-call(bf16[2,4,144,864]{3,2,1,0:T(8,128)(2,1)} %get-tuple-elem, ...), custom_call_target="tpu_custom_call" | custom-call | tf_op jit(solution)/shard_map/pallas_call | solution.py:1620
  440.1 0.0 copy-done.1
  440.1 0.7 copy.32
  440.8 0.0 copy-done
  440.9 0.8 copy.33
Async XLA Ops:
  421.6 18.6 %copy-start.1 = (bf16[128,1152]{1,0:T(8,128)(2,1)S(1)}, bf16[128,1152]{1,0:T(8,128)(2,1)}, u32[]{:S(2)}) copy-start(bf16[128,1152]{1,0:T(8,128)(2,1)} %get-tuple-element.34) | copy-start | bytes 884740
  421.6 19.3 %copy-start = (f32[128,1152]{1,0:T(8,128)S(1)}, f32[128,1152]{1,0:T(8,128)}, u32[]{:S(2)}) copy-start(f32[128,1152]{1,0:T(8,128)} %get-tuple-element.35) | copy-start | bytes 1769476

commit v5 on v4

--- a/solution.py
+++ b/solution.py
@@ -388,14 +388,16 @@
     def w_block(which, layer, plane_idx, col):
         return full[which].at[layer, w_rows(which, plane_idx, col)]
 
-    def w_z(which, layer, kind, plane_idx, own=False):
-        slot = layer * 4 + which
-        block = w_block(which, layer, plane_idx, x)
+    def w_z(which, layer, kind, plane_idx, own=False, other=False):
+        slot = 4 * LAYERS if other else layer * 4 + which
+        block = w_block(which, layer, plane_idx, 1 - x if other else x)
         return remote(
             shard(which, layer) if own else block, block,
             (r.wz_s.at[slot, kind], r.wz_r.at[slot, plane_idx]),
             at_plane(z_inner if kind == 1 else z_partner),
         )
+
+    x_first = None
 
     def w_x(which, layer, plane_idx, col, own=False):
         slot = layer * 4 + which
@@ -432,19 +434,42 @@
                 pl.when(onward)(lambda: w_z(which, layer, kind, plane_idx).start())
             w_x(which, layer, plane_idx, x).start()
 
+        def ahead():
+            slot = layer * 4 + which + 2
+            if 2 < slot < 4 * LAYERS:
+                weights_start(slot % 4, slot // 4)
+
         def step(plane_idx, kind):
+            if kind == 0:
+                ahead()
             passed(plane_idx, kind)
-            slot = layer * 4 + which + 2
-            if kind == 2 and 2 < slot < 4 * LAYERS:
-                weights_start(slot % 4, slot // 4)
 
         def only():
+            ahead()
             pl.when(z != n)(lambda: passed(n, 2))
-            slot = layer * 4 + which + 2
-            weights_start(slot % 4, slot // 4)
+
+        def beside_first():
+            w_x(which, layer, z, 1 - x).wait_recv()
+            for kind in (1, 0):
+                w_z(which, layer, kind, z, other=True).start()
+
+        def step_both(plane_idx, kind):
+            for other in (False, True):
+                w_z(which, layer, 0, plane_idx, other=other).wait_recv()
+                if kind:
+                    pl.when(is_inner)(
+                        lambda: w_z(which, layer, kind, plane_idx, other=other).start()
+                    )
+            if kind == 0:
+                ahead()
 
         if which == OUT:
             return [only]
+        if (which, layer) == x_first:
+            return [beside_first] + [
+                partial(step_both, idx, kind)
+                for idx, kind in ((z_partner, 0), (z_inner, 2), (z_outer, 3))
+            ]
         return [
             partial(step, idx, kind) for idx, kind in ((z_partner, 0), (z_inner, 2), (z_outer, 3))
         ]
@@ -469,28 +494,38 @@
             w_x(which, layer, n, 1 - x).wait_recv()
             pl.when(z == n)(lambda: w_own(which, layer).wait())
         else:
-            for idx in range(PLANES):
-                w_x(which, layer, idx, 1 - x).wait_recv()
+            if (which, layer) != x_first:
+                for idx in range(PLANES):
+                    w_x(which, layer, idx, 1 - x).wait_recv()
             w_own(which, layer).wait()
 
     def weights_drain(which, layer):
-        def own():
-            for kind in range(2):
-                w_z(which, layer, kind, z, True).wait_send()
-
+        both = (False, True) if (which, layer) == x_first else (False,)
         if which == OUT:
             w_x(which, layer, n, x).wait_send()
-            pl.when(z == n)(own)
+
+            @pl.when(z == n)
+            def _():
+                for kind in range(2):
+                    w_z(which, layer, kind, z).wait_send()
+
             pl.when(passes_out)(lambda: w_z(which, layer, 2, n).wait_send())
         else:
-            own()
-            for idx in range(PLANES):
-                w_x(which, layer, idx, x).wait_send()
+            for other in both:
+                for kind in range(2):
+                    w_z(which, layer, kind, z, other=other).wait_send()
+
+            if (which, layer) == x_first:
+                w_x(which, layer, z, x).wait_send()
+            else:
+                for idx in range(PLANES):
+                    w_x(which, layer, idx, x).wait_send()
 
             @pl.when(is_inner)
             def _():
-                w_z(which, layer, 2, z_inner).wait_send()
-                w_z(which, layer, 3, z_outer).wait_send()
+                for other in both:
+                    w_z(which, layer, 2, z_inner, other=other).wait_send()
+                    w_z(which, layer, 3, z_outer, other=other).wait_send()
 
     def load(which, layer):
         return pltpu.make_async_copy(full[which].at[layer], loaded[which], r.load_sem.at[which])
@@ -1020,6 +1055,71 @@
         if layer == 1:
             credit(r.credit_x.at[which], beside)
 
+    def e_z(kind, other):
+        idx = (z_partner, z_inner, z_outer)[kind]
+        src = sums[DOWN].at[d_rows(DOWN, idx, 1 - x if other else x)]
+        slots = from_x[DOWN] if other else from_z[DOWN]
+
+        def send(slot, plane_idx):
+            return remote(
+                src, slots.at[slot], (r.e_s.at[int(other), kind], r.e_r.at[int(other), slot]),
+                at_plane(plane_idx),
+            )
+
+        return send
+
+    def e_in(slot, other):
+        ref = (from_x[DOWN] if other else from_z[DOWN]).at[slot]
+        remote(
+            ref, ref, (r.e_s.at[int(other), 0], r.e_r.at[int(other), slot]), at_plane(z_partner)
+        ).wait_recv()
+        return ref[...].astype(F32)
+
+    def e_x():
+        return remote(from_x[DOWN].at[0], r.down_e, (r.ex_s, r.ex_r), beside)
+
+    def first_send():
+        @pl.when(jnp.logical_not(is_inner))
+        def _():
+            for kind in (2, 1):
+                for other in (True, False):
+                    e_z(kind, other)(kind + 1, z_partner).start()
+
+        for other in (True, False):
+            e_z(0, other)(0, z_partner).start()
+
+    def first_join():
+        @pl.when(is_inner)
+        def _():
+            for kind, idx in ((2, z_outer), (1, z_inner)):
+                for other in (True, False):
+                    rows = d_rows(DOWN, idx, 1 - x if other else x)
+                    total = sums[DOWN][rows, :].astype(F32) + e_in(kind + 1, other)
+                    sums[DOWN][rows, :] = total.astype(BF16)
+                    e_z(kind, other)(1, idx).start()
+
+    def first_planes():
+        for other in (True, False):
+            rows = d_rows(DOWN, z, 1 - x if other else x)
+            total = sums[DOWN][rows, :].astype(F32) + e_in(0, other) + e_in(1, other)
+            if other:
+                from_x[DOWN][0] = total.astype(BF16)
+                e_x().start()
+            else:
+                final[DOWN][...] = total.astype(BF16)
+        for kind in range(3):
+            for other in (True, False):
+                e_z(kind, other)(0, z_partner).wait_send()
+        credit(r.credit_z.at[DOWN, 0], at_plane(z_partner))
+        credit(r.credit_z.at[DOWN, 1], at_plane(z_inner))
+
+    def first_beside():
+        e_x().wait_recv()
+        total = final[DOWN][...].astype(F32) + r.down_e[...].astype(F32)
+        final[DOWN][...] = total.astype(BF16)
+        e_x().wait_send()
+        credit(r.credit_x.at[DOWN], beside)
+
     def spread(which, layer, kind, source=None):
         slot = layer * 4 + which
         if which == OUT:
@@ -1239,7 +1339,7 @@
     tok_drain(hid)
     tok_drain(r.grad_down, True)
     pump_through(DOWN, 1)
-    grad_send(DOWN, 1)
+    first_send()
     weights_ready(DOWN, 1)
     for block in range(2):
         back_mlp_block(1, block)
@@ -1269,8 +1369,8 @@
     grad_send(OUT, 1)
     for head in range(own_heads):
         back_attend(1, head)
-        if head == 1:
-            grad_beside(DOWN, 1)
+        if head == 2:
+            first_join()
     tok_drain(r.grad_branch)
     for part in range(2):
         sum_wait(part)
@@ -1305,7 +1405,7 @@
     load(DOWN, 0).wait()
     load(UP, 0).wait()
     grad_beside(OUT, 1)
-    grad_join(DOWN, 1)
+    first_planes()
     tok_own(r.grad_down)
     back_mlp_block(0, 1)
     sum_block(1)
@@ -1318,7 +1418,7 @@
     tok_drain(r.grad_down)
     back_middle(0)
     grad_product(UP, 0)
-    grad_planes(DOWN, 1)
+    first_beside()
     grad_send(DOWN, 0)
     grad_join(UP, 1)
     grad_join(OUT, 1)
@@ -1574,7 +1674,8 @@
     hidden_own = got["up_o"].shape[-1] // wide
     hidden_all = got["up_o"].shape[-1] * narrow
     down_rows = narrow * hidden_own
-    bands = depth // 16
+    bands = depth // 48
+    rows = depth // bands
     shape, vmem = jax.ShapeDtypeStruct, pltpu.VMEM
 
     def whole(values):
@@ -1592,8 +1693,8 @@
         cond=cond, cond_index=cond_index,
     )
     in_specs = [
-        band(narrow, 16, 3 * cols), band(narrow, 16, wide * hidden_own), band(16, width),
-        band(down_rows // bands, width), band(16, got["lead_o"].shape[-1]),
+        band(narrow, rows, 3 * cols), band(narrow, rows, wide * hidden_own), band(rows, width),
+        band(down_rows // bands, width), band(rows, got["lead_o"].shape[-1]),
         *[whole(inputs[name]) for name in ("mod_i", "bias_i", "lead_i2", "cond", "cond_index")],
     ]
     outputs = dict(
@@ -1605,7 +1706,7 @@
         down_bg=shape((LAYERS, depth), F32), cond_g=shape((SEGS, width), F32),
     )
     out_specs = [
-        band(16, tiles * LANES), band(16, 3 * width), band(16, width), band(16, hidden_all),
+        band(rows, tiles * LANES), band(rows, 3 * width), band(rows, width), band(rows, hidden_all),
         band(down_rows // bands, width),
         *[whole(outputs[name]) for name in ("ada_bg", "qkv_bg", "out_bg", "up_bg", "down_bg", "cond_g")],
     ]
@@ -1718,7 +1819,7 @@
         up_zr=vmem((PLANES, depth, hidden), BF16), down_zr=vmem((PLANES, hidden_own, width), BF16),
         qkv_f=vmem((depth, 3 * cols), BF16), out_f=vmem((depth, width), BF16),
         up_f=vmem((depth, hidden), BF16), down_f=vmem((hidden_own, width), BF16),
-        wz_s=dma((8, 4)), wz_r=dma((8, 4)), wx_s=dma((8, 4)), wx_r=dma((8, 4)), w_own=dma((8,)),
+        wz_s=dma((9, 4)), wz_r=dma((9, 4)), wx_s=dma((8, 4)), wx_r=dma((8, 4)), w_own=dma((8,)),
         load_sem=dma((4,)), tok_s=dma((12,)), tok_r=dma((12,)), sum_s=dma((4,)), sum_r=dma((4,)),
         lead_sem_s=dma((wide - 1,)), lead_sem_r=dma((wide - 1,)),
         bias_sem_s=dma((wide - 1,)), bias_sem_r=dma((wide - 1,)),
@@ -1727,6 +1828,8 @@
         lead_back_s=dma((wide - 1,)), lead_back_r=dma((wide - 1,)),
         lead_narrow_s=dma((3,)), lead_narrow_r=dma((3,)),
         dx_s=dma((4, 4)), dx_r=dma((4, 4)), dz_s=dma((4, 3)), dz_r=dma((4, 4)),
+        e_s=dma((2, 3)), e_r=dma((2, 4)), ex_s=dma, ex_r=dma,
+        down_e=vmem((hidden_own, width), BF16),
         spread_s=dma((8, 3)), spread_r=dma((8, 3)), spread_l=dma((8,)),
         back_s=dma((3,)), back_r=dma((3,)),
         wide_s=dma((wide - 1,)), wide_r=dma((wide - 1,)),

time: 446 us -> 429 us (0.962)
  Pallas kernels: 438 us -> 420 us
    pallas_call x1, Pallas kernels: 420 us -> 407 us  [fused_device(): pl.pallas_call(partial(block_kernel, cfg), out_shape=list(outputs.values(...]
    pallas_call x1, Pallas kernels: 18.5 us -> 13 us  [finish(): pl.pallas_call(partial(finish_kernel, cfg), grid=(LAYERS, bands), out_sha...]
where the time goes in v5:
time: 429 us; the launch traced here: 424 us
  Pallas kernels  420 us (98%)
    pallas_call x1, Pallas kernels, fused_device(): pl.pallas_call(partial(block_kernel, cfg), out_shape=list(outputs.values(...  407 us
    pallas_call x1, Pallas kernels, finish(): pl.pallas_call(partial(finish_kernel, cfg), grid=(LAYERS, bands), out_sha...  13 us

profile of v5, /device:TPU:17, one launch (start us, length us, event | category | flops | bytes accessed | tf_op | source)
XLA Modules:
  0.0 424.0 jit_solution(10527655354147681779)
XLA Ops:
  0.6 1.3 copy.28.refs_2_.refs_9_
  2.0 407.2 %shard_map.246 = (bf16[128,1152]{1,0:T(8,128)(2,1)}, f32[128,1152]{1,0:T(8,128)}, bf16[2,4,144,864]{3,2,1,0:T(8,128)(2,1)}, bf16[2,144,1152]{2,1,0:T(8,128)(2,1)...) custom-call(bf16[128,1152]{1,0:T(8,128)(2,1)} %bitcast.10, ...), custom_call_target="tpu_custom_call" | custom-call | tf_op jit(solution)/shard_map/pallas_call | solution.py:1850
  409.1 0.0 copy-start.1
  409.1 0.0 copy-start
  409.2 13.0 %shard_map.247 = (f32[2,144,6912]{2,1,0:T(8,128)}, f32[2,144,3456]{2,1,0:T(8,128)}, f32[2,144,1152]{2,1,0:T(8,128)}, f32[2,144,4608]{2,1,0:T(8,128)}, f32[2,576,...) custom-call(bf16[2,4,144,864]{3,2,1,0:T(8,128)(2,1)} %get-tuple-elem, ...), custom_call_target="tpu_custom_call" | custom-call | tf_op jit(solution)/shard_map/pallas_call | solution.py:1721
  422.2 0.0 copy-done.1
  422.2 0.7 copy.32
  422.9 0.0 copy-done
  422.9 0.8 copy.33
Async XLA Ops:
  409.1 13.0 %copy-start.1 = (bf16[128,1152]{1,0:T(8,128)(2,1)S(1)}, bf16[128,1152]{1,0:T(8,128)(2,1)}, u32[]{:S(2)}) copy-start(bf16[128,1152]{1,0:T(8,128)(2,1)} %get-tuple-element.34) | copy-start | bytes 884740
  409.1 13.7 %copy-start = (f32[128,1152]{1,0:T(8,128)S(1)}, f32[128,1152]{1,0:T(8,128)}, u32[]{:S(2)}) copy-start(f32[128,1152]{1,0:T(8,128)} %get-tuple-element.35) | copy-start | bytes 1769476

commit v6 on v5

--- a/solution.py
+++ b/solution.py
@@ -388,16 +388,14 @@
     def w_block(which, layer, plane_idx, col):
         return full[which].at[layer, w_rows(which, plane_idx, col)]
 
-    def w_z(which, layer, kind, plane_idx, own=False, other=False):
-        slot = 4 * LAYERS if other else layer * 4 + which
-        block = w_block(which, layer, plane_idx, 1 - x if other else x)
+    def w_z(which, layer, kind, plane_idx, own=False):
+        slot = layer * 4 + which
+        block = w_block(which, layer, plane_idx, x)
         return remote(
             shard(which, layer) if own else block, block,
             (r.wz_s.at[slot, kind], r.wz_r.at[slot, plane_idx]),
             at_plane(z_inner if kind == 1 else z_partner),
         )
-
-    x_first = None
 
     def w_x(which, layer, plane_idx, col, own=False):
         slot = layer * 4 + which
@@ -412,12 +410,23 @@
             shard(which, layer), w_block(which, layer, z, x), r.w_own.at[layer * 4 + which]
         )
 
+    def weights_beside(which, layer):
+        w_x(which, layer, z, x, True).start()
+        w_own(which, layer).start()
+
+    def weights_along(which, layer):
+        w_z(which, layer, 1, z, True).start()
+        w_z(which, layer, 0, z, True).start()
+
+    early, early_outer = ((UP, 0), (DOWN, 0)), ((QKV, 1), (UP, 1))
+
     def weights_start(which, layer):
         def go():
-            w_z(which, layer, 1, z, True).start()
-            w_z(which, layer, 0, z, True).start()
-            w_x(which, layer, z, x, True).start()
-            w_own(which, layer).start()
+            weights_along(which, layer)
+            if (which, layer) in early_outer:
+                pl.when(is_inner)(lambda: weights_beside(which, layer))
+            elif (which, layer) not in early:
+                weights_beside(which, layer)
 
         if which == OUT:
             pl.when(z == n)(go)
@@ -448,28 +457,8 @@
             ahead()
             pl.when(z != n)(lambda: passed(n, 2))
 
-        def beside_first():
-            w_x(which, layer, z, 1 - x).wait_recv()
-            for kind in (1, 0):
-                w_z(which, layer, kind, z, other=True).start()
-
-        def step_both(plane_idx, kind):
-            for other in (False, True):
-                w_z(which, layer, 0, plane_idx, other=other).wait_recv()
-                if kind:
-                    pl.when(is_inner)(
-                        lambda: w_z(which, layer, kind, plane_idx, other=other).start()
-                    )
-            if kind == 0:
-                ahead()
-
         if which == OUT:
             return [only]
-        if (which, layer) == x_first:
-            return [beside_first] + [
-                partial(step_both, idx, kind)
-                for idx, kind in ((z_partner, 0), (z_inner, 2), (z_outer, 3))
-            ]
         return [
             partial(step, idx, kind) for idx, kind in ((z_partner, 0), (z_inner, 2), (z_outer, 3))
         ]
@@ -494,13 +483,11 @@
             w_x(which, layer, n, 1 - x).wait_recv()
             pl.when(z == n)(lambda: w_own(which, layer).wait())
         else:
-            if (which, layer) != x_first:
-                for idx in range(PLANES):
-                    w_x(which, layer, idx, 1 - x).wait_recv()
+            for idx in range(PLANES):
+                w_x(which, layer, idx, 1 - x).wait_recv()
             w_own(which, layer).wait()
 
     def weights_drain(which, layer):
-        both = (False, True) if (which, layer) == x_first else (False,)
         if which == OUT:
             w_x(which, layer, n, x).wait_send()
 
@@ -511,21 +498,15 @@
 
             pl.when(passes_out)(lambda: w_z(which, layer, 2, n).wait_send())
         else:
-            for other in both:
-                for kind in range(2):
-                    w_z(which, layer, kind, z, other=other).wait_send()
-
-            if (which, layer) == x_first:
-                w_x(which, layer, z, x).wait_send()
-            else:
-                for idx in range(PLANES):
-                    w_x(which, layer, idx, x).wait_send()
+            for kind in range(2):
+                w_z(which, layer, kind, z).wait_send()
+            for idx in range(PLANES):
+                w_x(which, layer, idx, x).wait_send()
 
             @pl.when(is_inner)
             def _():
-                for other in both:
-                    w_z(which, layer, 2, z_inner, other=other).wait_send()
-                    w_z(which, layer, 3, z_outer, other=other).wait_send()
+                w_z(which, layer, 2, z_inner).wait_send()
+                w_z(which, layer, 3, z_outer).wait_send()
 
     def load(which, layer):
         return pltpu.make_async_copy(full[which].at[layer], loaded[which], r.load_sem.at[which])
@@ -712,12 +693,24 @@
             r.mod_part[row, at, :] = product[16 * row : 16 * row + SEGS]
     for j in range(1, wide):
         mod_copy(j).start()
-    weights_start(OUT, 0)
     r.mod_rx[pl.ds(w, 1)] = r.mod_part[pl.ds(w, 1)]
     for which, layer in ((UP, 0), (QKV, 1), (UP, 1)):
         pack_shard(which, layer)
+    for item in early:
+        weights_beside(*item)
+
+    def after_first():
+        weights_start(OUT, 0)
+        weights_along(UP, 0)
+
+    @pl.when(jnp.logical_not(is_inner))
+    def _():
+        for item in early_outer:
+            weights_beside(*item)
+        after_first()
+
     pump_through(QKV, 0)
-    weights_start(UP, 0)
+    pl.when(is_inner)(after_first)
     r.mod_grad[...] = jnp.zeros_like(r.mod_grad)
     r.lead_t[...] = jnp.zeros_like(r.lead_t)
     for layer in range(LAYERS):
@@ -992,16 +985,14 @@
             for k, idx in ((2, z_outer), (1, z_inner), (0, z_partner), (None, z)):
                 d_x(which, idx).wait_recv()
                 add(idx, d_rows(which, idx, x))
+                if k == 2 and layer == 0:
+                    pl.semaphore_wait(r.credit_z.at[which, 0], 1)
                 if k == 0:
-                    if layer == 0:
-                        pl.semaphore_wait(r.credit_z.at[which, 0], 1)
-
-                    @pl.when(jnp.logical_not(is_inner))
-                    def _():
-                        d_z(which, 2)(3, z_partner).start()
-                        d_z(which, 1)(2, z_partner).start()
-
                     d_z(which, 0)(0, z_partner).start()
+                elif k:
+                    pl.when(jnp.logical_not(is_inner))(
+                        lambda: d_z(which, k)(k + 1, z_partner).start()
+                    )
             for idx in range(PLANES):
                 d_x(which, idx).wait_send()
 
@@ -1442,6 +1433,7 @@
     grad_join(QKV, 1)
     grad_product(QKV, 0)
     tok_drain(r.grad_branch)
+    grad_beside(DOWN, 0)
     bias_grad(0, QKV, r.grad_qkv[...])
     for part in range(2):
         sum_wait(part)
@@ -1511,7 +1503,6 @@
     r.bias_all[pl.ds(w, 1)] = r.bias_half[...][None]
     grad_planes(OUT, 1)
     grad_send(OUT, 0)
-    grad_beside(DOWN, 0)
     grad_planes(QKV, 1)
     grad_send(QKV, 0)
     grad_spread(UP, 1)
@@ -1819,7 +1810,7 @@
         up_zr=vmem((PLANES, depth, hidden), BF16), down_zr=vmem((PLANES, hidden_own, width), BF16),
         qkv_f=vmem((depth, 3 * cols), BF16), out_f=vmem((depth, width), BF16),
         up_f=vmem((depth, hidden), BF16), down_f=vmem((hidden_own, width), BF16),
-        wz_s=dma((9, 4)), wz_r=dma((9, 4)), wx_s=dma((8, 4)), wx_r=dma((8, 4)), w_own=dma((8,)),
+        wz_s=dma((8, 4)), wz_r=dma((8, 4)), wx_s=dma((8, 4)), wx_r=dma((8, 4)), w_own=dma((8,)),
         load_sem=dma((4,)), tok_s=dma((12,)), tok_r=dma((12,)), sum_s=dma((4,)), sum_r=dma((4,)),
         lead_sem_s=dma((wide - 1,)), lead_sem_r=dma((wide - 1,)),
         bias_sem_s=dma((wide - 1,)), bias_sem_r=dma((wide - 1,)),

time: 429 us -> 413 us (0.963)
  Pallas kernels: 420 us -> 406 us
    pallas_call x1, Pallas kernels: 407 us -> 393 us  [fused_device(): pl.pallas_call(partial(block_kernel, cfg), out_shape=list(outputs.values(...]
where the time goes in v6:
time: 413 us; the launch traced here: 410 us
  Pallas kernels  406 us (98%)
    pallas_call x1, Pallas kernels, fused_device(): pl.pallas_call(partial(block_kernel, cfg), out_shape=list(outputs.values(...  393 us
    pallas_call x1, Pallas kernels, finish(): pl.pallas_call(partial(finish_kernel, cfg), grid=(LAYERS, bands), out_sha...  13 us

profile of v6, /device:TPU:17, one launch (start us, length us, event | category | flops | bytes accessed | tf_op | source)
XLA Modules:
  0.0 409.5 jit_solution(13798777868798773174)
XLA Ops:
  0.6 1.3 copy.28.refs_2_.refs_9_
  2.0 392.7 %shard_map.246 = (bf16[128,1152]{1,0:T(8,128)(2,1)}, f32[128,1152]{1,0:T(8,128)}, bf16[2,4,144,864]{3,2,1,0:T(8,128)(2,1)}, bf16[2,144,1152]{2,1,0:T(8,128)(2,1)...) custom-call(bf16[128,1152]{1,0:T(8,128)(2,1)} %bitcast.10, ...), custom_call_target="tpu_custom_call" | custom-call | tf_op jit(solution)/shard_map/pallas_call | solution.py:1841
  394.7 0.0 copy-start.1
  394.7 0.0 copy-start
  394.7 13.0 %shard_map.247 = (f32[2,144,6912]{2,1,0:T(8,128)}, f32[2,144,3456]{2,1,0:T(8,128)}, f32[2,144,1152]{2,1,0:T(8,128)}, f32[2,144,4608]{2,1,0:T(8,128)}, f32[2,576,...) custom-call(bf16[2,4,144,864]{3,2,1,0:T(8,128)(2,1)} %get-tuple-elem, ...), custom_call_target="tpu_custom_call" | custom-call | tf_op jit(solution)/shard_map/pallas_call | solution.py:1712
  407.7 0.0 copy-done.1
  407.7 0.7 copy.32
  408.5 0.0 copy-done
  408.5 0.8 copy.33
Async XLA Ops:
  394.7 13.0 %copy-start.1 = (bf16[128,1152]{1,0:T(8,128)(2,1)S(1)}, bf16[128,1152]{1,0:T(8,128)(2,1)}, u32[]{:S(2)}) copy-start(bf16[128,1152]{1,0:T(8,128)(2,1)} %get-tuple-element.34) | copy-start | bytes 884740
  394.7 13.7 %copy-start = (f32[128,1152]{1,0:T(8,128)S(1)}, f32[128,1152]{1,0:T(8,128)}, u32[]{:S(2)}) copy-start(f32[128,1152]{1,0:T(8,128)} %get-tuple-element.35) | copy-start | bytes 1769476

commit v7 on v6

--- a/solution.py
+++ b/solution.py
@@ -1396,7 +1396,6 @@
     load(DOWN, 0).wait()
     load(UP, 0).wait()
     grad_beside(OUT, 1)
-    first_planes()
     tok_own(r.grad_down)
     back_mlp_block(0, 1)
     sum_block(1)
@@ -1404,6 +1403,7 @@
     back_mlp_block(0, 0)
     sum_block(0)
     sum_cross()
+    first_planes()
     grad_product(DOWN, 0)
     bias_grad(0, UP, r.grad_up[...])
     tok_drain(r.grad_down)
@@ -1587,11 +1587,13 @@
 
 def chosen_of(cond, index):
     values = cond[...].astype(F32)
-    rows = index[...]
-    chosen = jnp.zeros(values.shape, F32)
-    for k in range(SEGS):
-        chosen = jnp.where(rows == k, values[k : k + 1], chosen)
-    return chosen
+    rows = []
+    for s in range(SEGS):
+        row = values[SEGS - 1 : SEGS]
+        for k in range(SEGS - 1):
+            row = jnp.where(index[:, s : s + 1] == k, values[k : k + 1], row)
+        rows.append(row)
+    return jnp.concatenate(rows, 0)
 
 
 def finish_kernel(cfg, *refs):
@@ -1654,9 +1656,11 @@
             at = slice(depth * row, depth * (row + 1))
             grad = lead_grad[row] * slope[:, at]
             for k in range(SEGS):
-                r.cond_g[k : k + 1, at] = jnp.sum(
-                    jnp.where(r.cond_index[...] == k, grad, 0.0), 0, keepdims=True
-                )
+                total = jnp.zeros((1, depth), F32)
+                for s in range(SEGS):
+                    own = r.cond_index[:, s : s + 1] == k
+                    total = total + jnp.where(own, grad[s : s + 1], 0.0)
+                r.cond_g[k : k + 1, at] = total
 
 
 def finish(wide, narrow, got, cond, cond_index, tiles, mod_cols, w):
@@ -1740,7 +1744,7 @@
     mod_cols = LANES * -(-tiles // narrow)
 
     inputs = dict(
-        tok=tokens[0], cond=cond[0], cond_index=cond_index.reshape(SEGS, 1), seg_row=seg_ids,
+        tok=tokens[0], cond=cond[0], cond_index=cond_index, seg_row=seg_ids,
         cot=cotangent[0], ada_b=ada_bias, qkv_b=qkv_bias, out_b=out_bias, up_b=up_bias, down_b=down_bias,
         ada=ada_weight, qkv_w=qkv_weight, out_w=out_weight, up_w=up_weight, down_w=down_weight,
     )

time: 413 us -> 409 us (level)
  no operation moved by 1% of the time
where the time goes in v7:
time: 409 us; the launch traced here: 406 us
  Pallas kernels  404 us (99%)
    pallas_call x1, Pallas kernels, fused_device(): pl.pallas_call(partial(block_kernel, cfg), out_shape=list(outputs.values(...  389 us
    pallas_call x1, Pallas kernels, finish(): pl.pallas_call(partial(finish_kernel, cfg), grid=(LAYERS, bands), out_sha...  14.4 us

profile of v7, /device:TPU:17, one launch (start us, length us, event | category | flops | bytes accessed | tf_op | source)
XLA Modules:
  0.0 406.2 jit_solution(15137525831642933658)
XLA Ops:
  0.6 389.3 %shard_map.246 = (bf16[128,1152]{1,0:T(8,128)(2,1)}, f32[128,1152]{1,0:T(8,128)}, bf16[2,4,144,864]{3,2,1,0:T(8,128)(2,1)}, bf16[2,144,1152]{2,1,0:T(8,128)(2,1)...) custom-call(bf16[128,1152]{1,0:T(8,128)(2,1)} %bitcast.9, ...), custom_call_target="tpu_custom_call" | custom-call | tf_op jit(solution)/shard_map/pallas_call | solution.py:1845
  390.0 0.0 copy-start.1
  390.0 0.0 copy-start
  390.0 14.4 %shard_map.247 = (f32[2,144,6912]{2,1,0:T(8,128)}, f32[2,144,3456]{2,1,0:T(8,128)}, f32[2,144,1152]{2,1,0:T(8,128)}, f32[2,144,4608]{2,1,0:T(8,128)}, f32[2,576,...) custom-call(bf16[2,4,144,864]{3,2,1,0:T(8,128)(2,1)} %get-tuple-elem, ...), custom_call_target="tpu_custom_call" | custom-call | tf_op jit(solution)/shard_map/pallas_call | solution.py:1716
  404.4 0.0 copy-done.1
  404.4 0.7 copy.30
  405.1 0.0 copy-done
  405.1 0.8 copy.31
Async XLA Ops:
  390.0 14.4 %copy-start.1 = (bf16[128,1152]{1,0:T(8,128)(2,1)S(1)}, bf16[128,1152]{1,0:T(8,128)(2,1)}, u32[]{:S(2)}) copy-start(bf16[128,1152]{1,0:T(8,128)(2,1)} %get-tuple-element.34) | copy-start | bytes 884740
  390.0 15.1 %copy-start = (f32[128,1152]{1,0:T(8,128)S(1)}, f32[128,1152]{1,0:T(8,128)}, u32[]{:S(2)}) copy-start(f32[128,1152]{1,0:T(8,128)} %get-tuple-element.35) | copy-start | bytes 1769476

commit v8 on v7

--- a/solution.py
+++ b/solution.py
@@ -1508,9 +1508,9 @@
     grad_spread(UP, 1)
     grad_spread(OUT, 1)
     grad_spread(QKV, 1)
+    grad_join(DOWN, 0)
     for which in (DOWN, UP, OUT, QKV):
         grad_pass(which, 1)
-    grad_join(DOWN, 0)
     grad_beside(UP, 0)
     wait_all(wide_back)
     for j in range(1, wide):

time: 409 us -> 409 us (level)
  no operation moved by 1% of the time
where the time goes in v8:
time: 409 us; the launch traced here: 406 us
  Pallas kernels  404 us (99%)
    pallas_call x1, Pallas kernels, fused_device(): pl.pallas_call(partial(block_kernel, cfg), out_shape=list(outputs.values(...  389 us
    pallas_call x1, Pallas kernels, finish(): pl.pallas_call(partial(finish_kernel, cfg), grid=(LAYERS, bands), out_sha...  14.4 us

profile of v8, /device:TPU:17, one launch (start us, length us, event | category | flops | bytes accessed | tf_op | source)
XLA Modules:
  0.0 406.2 jit_solution(9084399238466681137)
XLA Ops:
  0.6 389.3 %shard_map.246 = (bf16[128,1152]{1,0:T(8,128)(2,1)}, f32[128,1152]{1,0:T(8,128)}, bf16[2,4,144,864]{3,2,1,0:T(8,128)(2,1)}, bf16[2,144,1152]{2,1,0:T(8,128)(2,1)...) custom-call(bf16[128,1152]{1,0:T(8,128)(2,1)} %bitcast.9, ...), custom_call_target="tpu_custom_call" | custom-call | tf_op jit(solution)/shard_map/pallas_call | solution.py:1845
  390.0 0.0 copy-start.1
  390.0 0.0 copy-start
  390.0 14.4 %shard_map.247 = (f32[2,144,6912]{2,1,0:T(8,128)}, f32[2,144,3456]{2,1,0:T(8,128)}, f32[2,144,1152]{2,1,0:T(8,128)}, f32[2,144,4608]{2,1,0:T(8,128)}, f32[2,576,...) custom-call(bf16[2,4,144,864]{3,2,1,0:T(8,128)(2,1)} %get-tuple-elem, ...), custom_call_target="tpu_custom_call" | custom-call | tf_op jit(solution)/shard_map/pallas_call | solution.py:1716
  404.4 0.0 copy-done.1
  404.4 0.7 copy.30
  405.1 0.0 copy-done
  405.1 0.8 copy.31
Async XLA Ops:
  390.0 14.4 %copy-start.1 = (bf16[128,1152]{1,0:T(8,128)(2,1)S(1)}, bf16[128,1152]{1,0:T(8,128)(2,1)}, u32[]{:S(2)}) copy-start(bf16[128,1152]{1,0:T(8,128)(2,1)} %get-tuple-element.34) | copy-start | bytes 884740
  390.0 15.1 %copy-start = (f32[128,1152]{1,0:T(8,128)S(1)}, f32[128,1152]{1,0:T(8,128)}, u32[]{:S(2)}) copy-start(f32[128,1152]{1,0:T(8,128)} %get-tuple-element.35) | copy-start | bytes 1769476
